TPU v7x, 32 devices: a whole 2x2x4 slice. The times are simulated.
32 devices in a mesh: groups: 2 (over y), member: 4 (over z), fsdp: 4 (over x, core).
Axes of the slice: x: 2, y: 2, z: 4, core: 2. Of those that a mesh axis runs over, the one named last changes fastest.
Arguments:
- tokens: bfloat16 [8, 768, 4096], P(('groups', 'member'), 'fsdp'), parts along dimension 0, may hold values from -6 to 6
- grad_out: bfloat16 [8, 768, 4096], P(('groups', 'member'), 'fsdp'), parts along dimension 0, may hold values from -6 to 6
- gate_up: bfloat16 [8, 4096, 256], P(('groups', 'member'), 'fsdp'), parts along dimension 0, may hold values from -6 to 6
- down: bfloat16 [8, 128, 4096], P(('groups', 'member'), 'fsdp'), parts along dimension 0, may hold values from -6 to 6
- mom1_gate_up: float32 [8, 4096, 256], P(('groups', 'member'), 'fsdp'), parts along dimension 0, may hold values from -4 to 4
- mom2_gate_up: float32 [8, 4096, 256], P(('groups', 'member'), 'fsdp'), parts along dimension 0, may hold values from 0.1 to 4
- mom1_down: float32 [8, 128, 4096], P(('groups', 'member'), 'fsdp'), parts along dimension 0, may hold values from -4 to 4
- mom2_down: float32 [8, 128, 4096], P(('groups', 'member'), 'fsdp'), parts along dimension 0, may hold values from 0.1 to 4
- learning: float32 [8], P('groups'), parts along dimension 0, may hold values from 0.02 to 0.2
- winner: int32 [8], P('groups'), parts along dimension 0, may hold values from 0 to 3, as said below
Outputs:
- new_gate_up: bfloat16 [8, 4096, 256], P(('groups', 'member'), 'fsdp'), parts along dimension 0
- new_down: bfloat16 [8, 128, 4096], P(('groups', 'member'), 'fsdp'), parts along dimension 0
- new_mom1_gate_up: float32 [8, 4096, 256], P(('groups', 'member'), 'fsdp'), parts along dimension 0
- new_mom2_gate_up: float32 [8, 4096, 256], P(('groups', 'member'), 'fsdp'), parts along dimension 0
- new_mom1_down: float32 [8, 128, 4096], P(('groups', 'member'), 'fsdp'), parts along dimension 0
- new_mom2_down: float32 [8, 128, 4096], P(('groups', 'member'), 'fsdp'), parts along dimension 0
There are 2 independent parts, one for each index of `groups`. A program takes and returns all parts, laid end to end along the dimension named above; each array names one. Nothing has to cross between parts.
Inputs may be any that keep to these rules, and one draw needn't show every extreme that they name: Every winner names itself; a member that names another member is named by no one; no member is named by more than four others, and some member is named by four others (by half of the members where there are fewer than eight).
All inputs are finite; a program needn't handle non-finite values.
Results may differ from a plain program's by a relative error of at most 0.008.
Values may be sent and summed in bfloat16 or wider, within the bound.
No kernel may reach another device: no remote copies, remote signals or barrier semaphores. Data moves between devices by JAX's collectives and lax.ppermute only.
A program may use at most 64 MiB of HBM per device.

v0:
```python
import jax
import jax.numpy as jnp
from jax import lax
from jax.sharding import PartitionSpec as P

beta_one = 0.9
beta_two = 0.95
epsilon = 1e-08
decay = 0.1


def spread(block, axis, source):
    block = jnp.where(lax.axis_index(axis) == source, block, jnp.zeros_like(block))
    return lax.psum(block, axis)


def adamw(weight, grad, first, second, rate):
    first_new = beta_one * first + (1.0 - beta_one) * grad
    second_new = beta_two * second + (1.0 - beta_two) * grad * grad
    wide = weight.astype(jnp.float32)
    updated = wide - rate * (first_new / (jnp.sqrt(second_new) + epsilon) + decay * wide)
    return (updated.astype(jnp.bfloat16), first_new, second_new)


def on_device(
    tokens,
    grad_out,
    gate_up,
    down,
    mom1_gate_up,
    mom2_gate_up,
    mom1_down,
    mom2_down,
    learning,
    winner,
):
    members = lax.axis_size("member")
    member_index = lax.axis_index("member")
    rows_in = tokens[0]
    upstream = grad_out[0]
    width = rows_in.shape[1]
    units = gate_up.shape[2] // 2
    shard_gu = gate_up[0]
    shard_dn = down[0]
    cut = shard_gu.size // members

    def joined(first_part, second_part):
        return jnp.concatenate(
            [first_part.reshape(members, -1), second_part.reshape(members, -1)], axis=1
        )

    def parted(flat):
        return (flat[:, :cut].reshape(shard_gu.shape), flat[:, cut:].reshape(shard_dn.shape))

    own_source = winner[member_index]

    def take_root(root, carry):
        sent_gu, sent_dn = (spread(shard_gu, "member", root), spread(shard_dn, "member", root))
        wanted = own_source == root
        return (jnp.where(wanted, sent_gu, carry[0]), jnp.where(wanted, sent_dn, carry[1]))

    copied_gu, copied_dn = lax.fori_loop(0, members, take_root, (shard_gu, shard_dn))
    first_gu, first_dn = parted(
        lax.all_to_all(
            jnp.take(
                lax.all_to_all(
                    joined(mom1_gate_up[0], mom1_down[0]).astype(jnp.bfloat16),
                    "member",
                    split_axis=0,
                    concat_axis=0,
                    tiled=True,
                ).astype(jnp.float32),
                winner,
                axis=0,
            ).astype(jnp.bfloat16),
            "member",
            split_axis=0,
            concat_axis=0,
            tiled=True,
        ).astype(jnp.float32)
    )
    second_gu, second_dn = parted(
        lax.all_to_all(
            jnp.take(
                lax.all_to_all(
                    joined(mom2_gate_up[0], mom2_down[0]).astype(jnp.bfloat16),
                    "member",
                    split_axis=0,
                    concat_axis=0,
                    tiled=True,
                ).astype(jnp.float32),
                winner,
                axis=0,
            ).astype(jnp.bfloat16),
            "member",
            split_axis=0,
            concat_axis=0,
            tiled=True,
        ).astype(jnp.float32)
    )
    rate = learning[winner[member_index]]
    columns = rows_in
    preact = jnp.dot(
        columns,
        lax.all_gather(copied_gu, "fsdp", axis=0, tiled=True),
        preferred_element_type=jnp.float32,
    ) * width ** (-0.5)
    gate = preact[:, :units]
    upper = preact[:, units:]
    sigma = jax.nn.sigmoid(gate)
    active = gate * sigma
    hidden = (active * upper).astype(jnp.bfloat16)
    dhidden = lax.dot_general(
        upstream,
        lax.all_gather(copied_dn, "fsdp", axis=0, tiled=True),
        (((1,), (1,)), ((), ())),
        preferred_element_type=jnp.float32,
    ) * units ** (-0.5)
    dgate = dhidden * upper * (sigma * (1.0 + gate * (1.0 - sigma)))
    dupper = dhidden * active
    dpreact = (jnp.concatenate([dgate, dupper], axis=1) * width ** (-0.5)).astype(jnp.bfloat16)
    columns = rows_in
    grad_gu = lax.psum_scatter(
        lax.dot_general(
            columns, dpreact, (((0,), (0,)), ((), ())), preferred_element_type=jnp.float32
        ).astype(jnp.bfloat16),
        "fsdp",
        scatter_dimension=0,
        tiled=True,
    ).astype(jnp.float32)
    columns = hidden
    product = lax.dot_general(
        columns, upstream, (((0,), (0,)), ((), ())), preferred_element_type=jnp.float32
    )
    grad_dn = lax.psum_scatter(
        (product * units ** (-0.5)).astype(jnp.bfloat16), "fsdp", scatter_dimension=0, tiled=True
    ).astype(jnp.float32)
    new_gu, new_first_gu, new_second_gu = adamw(copied_gu, grad_gu, first_gu, second_gu, rate)
    new_dn, new_first_dn, new_second_dn = adamw(copied_dn, grad_dn, first_dn, second_dn, rate)
    return (
        new_gu[None],
        new_dn[None],
        new_first_gu[None],
        new_second_gu[None],
        new_first_dn[None],
        new_second_dn[None],
    )


def solution(mesh):
    return jax.shard_map(
        on_device,
        mesh=mesh,
        in_specs=(
            P(("groups", "member"), "fsdp", None),
            P(("groups", "member"), "fsdp", None),
            P(("groups", "member"), "fsdp", None),
            P(("groups", "member"), "fsdp", None),
            P(("groups", "member"), "fsdp", None),
            P(("groups", "member"), "fsdp", None),
            P(("groups", "member"), "fsdp", None),
            P(("groups", "member"), "fsdp", None),
            P("groups"),
            P("groups"),
        ),
        out_specs=(
            P(("groups", "member"), "fsdp", None),
            P(("groups", "member"), "fsdp", None),
            P(("groups", "member"), "fsdp", None),
            P(("groups", "member"), "fsdp", None),
            P(("groups", "member"), "fsdp", None),
            P(("groups", "member"), "fsdp", None),
        ),
        check_vma=False,
    )
```

profile of v0, /device:TPU:0, one launch (start us, length us, event | category | flops | bytes accessed | tf_op | source)
XLA Modules:
  0.0 405.9 jit_solution(5410318081336801022)
XLA Ops:
  8.0 1.2 convert.23
  10.8 1.7 reduce.1
  12.5 1.7 reshape.137
  14.2 6.4 %all-to-all-start.2 = ((bf16[4,2,49152]{2,1,0:T(2,128)(2,1)}), bf16[4,2,49152]{2,1,0:T(2,128)(2,1)}, u32[]{:S(2)}, u32[]{:S(2)}) async-start(bf16[4,2,49152]{2,1,0:T(2,128)(2,1)} %reshape.137), calls=%async_computation.3 | async-start | bytes 1572864 | tf_op jit(solution)/shard_map/all_to_all | solution.py:85
  20.9 0.8 convert.20
  21.7 1.5 concatenate.33
  23.2 1.2 pad_maximum_fusion
  24.6 3.6 reduce
  28.2 2.8 reshape.141
  31.7 9.2 %all-to-all-done.2 = bf16[4,2,49152]{2,1,0:T(2,128)(2,1)} async-done(((bf16[4,2,49152]{2,1,0:T(2,128)(2,1)}), bf16[4,2,49152]{2,1,0:T(2,128)(2,1)}, u32[]{:S(2)}, u32[]{:S(2)}) %all-to-all-start.2) | async-done | bytes 786464 | tf_op jit(solution)/shard_map/all_to_all | solution.py:85
  40.9 4.2 %all-to-all-start = ((bf16[4,2,49152]{2,1,0:T(2,128)(2,1)}), bf16[4,2,49152]{2,1,0:T(2,128)(2,1)}, u32[]{:S(2)}, u32[]{:S(2)}) async-start(bf16[4,2,49152]{2,1,0:T(2,128)(2,1)} %reshape.141), calls=%async_computation | async-start | bytes 1572864 | tf_op jit(solution)/shard_map/all_to_all | solution.py:66
  45.1 202.3 %while.15 = (s32[]{:T(128)}, bf16[1024,256]{1,0:T(8,128)(2,1)S(1)}, bf16[32,4096]{1,0:T(8,128)(2,1)S(1)}, s32[]{:T(128)}, bf16[1024,256]{1,0:T(8,128)(2,1)S(1)},...) while((s32[]{:T(128)}, bf16[1024,256]{1,0:T(8,128)(2,1)S(1)}, ...), condition=%wide.region_3.4_spmd, body=%wide.region_0.3_spmd.sunk | while | flops 1179655 | bytes 9699551 | solution.py:62
  45.9 0.8 broadcast_select_fusion.8
  47.4 54.1 %all-reduce.5.cloned.1.call-done = (bf16[1024,256]{1,0:T(8,128)(2,1)}, bf16[32,4096]{1,0:T(8,128)(2,1)}) async-done(((bf16[1024,256]{1,0:T(8,128)(2,1)}, bf16[32,4096]{1,0:T(8,128)(2,1)}), (bf16[1024,256]{1,0:T(8,128)(2,1)}, bf16[32,4096]{1,0:T(8,128)(2,1)})) %all-reduce.5.cloned.1.call-update) | async-done | bytes 786448 | tf_op jit(solution)/shard_map/while/body/eval_jaxpr/psum | solution.py:14
  101.6 0.8 copy-done.7
  103.3 0.8 broadcast_select_fusion.8
  104.8 45.1 %all-reduce.5.cloned.1.call-done = (bf16[1024,256]{1,0:T(8,128)(2,1)}, bf16[32,4096]{1,0:T(8,128)(2,1)}) async-done(((bf16[1024,256]{1,0:T(8,128)(2,1)}, bf16[32,4096]{1,0:T(8,128)(2,1)}), (bf16[1024,256]{1,0:T(8,128)(2,1)}, bf16[32,4096]{1,0:T(8,128)(2,1)})) %all-reduce.5.cloned.1.call-update) | async-done | bytes 786448 | tf_op jit(solution)/shard_map/while/body/eval_jaxpr/psum | solution.py:14
  151.8 0.8 broadcast_select_fusion.8
  153.3 44.8 %all-reduce.5.cloned.1.call-done = (bf16[1024,256]{1,0:T(8,128)(2,1)}, bf16[32,4096]{1,0:T(8,128)(2,1)}) async-done(((bf16[1024,256]{1,0:T(8,128)(2,1)}, bf16[32,4096]{1,0:T(8,128)(2,1)}), (bf16[1024,256]{1,0:T(8,128)(2,1)}, bf16[32,4096]{1,0:T(8,128)(2,1)})) %all-reduce.5.cloned.1.call-update) | async-done | bytes 786448 | tf_op jit(solution)/shard_map/while/body/eval_jaxpr/psum | solution.py:14
  199.9 0.8 broadcast_select_fusion.8
  201.4 44.7 %all-reduce.5.cloned.1.call-done = (bf16[1024,256]{1,0:T(8,128)(2,1)}, bf16[32,4096]{1,0:T(8,128)(2,1)}) async-done(((bf16[1024,256]{1,0:T(8,128)(2,1)}, bf16[32,4096]{1,0:T(8,128)(2,1)}), (bf16[1024,256]{1,0:T(8,128)(2,1)}, bf16[32,4096]{1,0:T(8,128)(2,1)})) %all-reduce.5.cloned.1.call-update) | async-done | bytes 786448 | tf_op jit(solution)/shard_map/while/body/eval_jaxpr/psum | solution.py:14
  246.1 1.2 broadcast_select_fusion.10
  248.3 3.8 reshape.138
  252.0 2.4 copy.56
  254.5 3.9 reshape.142
  258.3 2.4 copy.57
  260.8 2.1 gather_fusion.1
  262.9 2.1 gather_fusion
  265.1 3.0 fusion.25
  268.1 2.8 reduce.3
  270.8 1.7 reshape.139
  272.5 3.6 all-to-all-start.3
  278.0 1.0 copy.36
  280.3 2.8 reduce.2
  283.1 1.7 reshape.143
  284.8 11.6 %all-to-all-done.3 = bf16[4,2,49152]{2,1,0:T(2,128)(2,1)S(1)} async-done(((bf16[4,2,49152]{2,1,0:T(2,128)(2,1)}), bf16[4,2,49152]{2,1,0:T(2,128)(2,1)S(1)}, u32[]{:S(2)}, u32[]{:S(2)}) %all-to-all-start.3) | async-done | bytes 786464 | tf_op jit(solution)/shard_map/all_to_all | solution.py:83
  296.4 4.2 %all-to-all-start.1 = ((bf16[4,2,49152]{2,1,0:T(2,128)(2,1)}), bf16[4,2,49152]{2,1,0:T(2,128)(2,1)}, u32[]{:S(2)}, u32[]{:S(2)}) async-start(bf16[4,2,49152]{2,1,0:T(2,128)(2,1)} %reshape.143), calls=%async_computation.1 | async-start | bytes 1572864 | tf_op jit(solution)/shard_map/all_to_all | solution.py:64
  300.9 2.4 reshape.140
  303.3 1.0 copy.54
  304.3 1.1 copy-done.8
  305.5 1.2 slice_multiply_fusion
  306.7 13.5 %all-to-all-done.1 = bf16[4,2,49152]{2,1,0:T(2,128)(2,1)} async-done(((bf16[4,2,49152]{2,1,0:T(2,128)(2,1)}), bf16[4,2,49152]{2,1,0:T(2,128)(2,1)}, u32[]{:S(2)}, u32[]{:S(2)}) %all-to-all-start.1) | async-done | bytes 786464 | tf_op jit(solution)/shard_map/all_to_all | solution.py:64
  320.3 3.7 reshape.144
  324.0 2.4 copy.55
  326.4 1.3 slice_multiply_fusion.1
  327.7 2.3 fusion.11
  330.0 1.5 fusion.1
  331.6 2.0 slice_multiply_fusion.2
  333.6 2.3 multiply_multiply_fusion.2
  335.9 2.1 fusion
  338.0 0.9 slice_multiply_fusion.3
  338.9 2.9 mul.142
  341.8 2.6 copy.44
  344.5 1.2 mul.158
  345.6 1.7 mul.126
  347.3 2.7 copy.40
  350.0 1.2 mul.151
  351.1 4.0 reduce-scatter.5.cloned.1.call-done
  355.2 3.3 fusion.36
  358.5 30.8 %reduce-scatter.3.cloned.1.call-done = bf16[1024,256]{0,1:T(8,128)(2,1)} async-done(((bf16[4096,256]{0,1:T(8,128)(2,1)}), bf16[1024,256]{0,1:T(8,128)(2,1)}) %reduce-scatter.3.cloned.1.call-update) | async-done | bytes 524304 | tf_op jit(solution)/shard_map/reduce_scatter | solution.py:123
  389.2 4.3 %fusion.28 = (f32[1,1024,256]{1,2,0:T(8,128)}, bf16[1,1024,256]{1,2,0:T(8,128)(2,1)}, f32[1,1024,256]{1,2,0:T(8,128)}) fusion(f32[1024,256]{0,1:T(8,128)S(1)} %copy-done.11, bf16[1024,256]{0,1:T(8,128)(2,1)} %reduce-scatter.3.cloned.1.call-done, f32[1024,256]{0,1:T(8,128)} %copy.40, f32[]{:T(128)} %bitcast.3, bf16[1024,256]{0,1:T(8,128)(2,1)S(1)} %copy-done.15), kind=kLoop, calls=%fused_computation.46 | loop fusion | flops 3670016 | bytes 5767172 | tf_op jit(solution)/shard_map/broadcast_in_dim | solution.py:144
  393.5 2.6 copy.47
  396.2 1.0 copy.45
  397.2 1.3 copy.46
  (96 shorter events, 10.4 us)
Async XLA Ops:
  8.0 319.7 %copy-start = (bf16[1,192,4096]{2,1,0:T(8,128)(2,1)S(1)}, bf16[1,192,4096]{2,1,0:T(8,128)(2,1)}, u32[]{:S(2)}) copy-start(bf16[1,192,4096]{2,1,0:T(8,128)(2,1)} %param.14) | copy-start | bytes 4718596
  8.0 1.5 copy-start.19
  14.2 6.5 %copy-start.21 = (f32[1,32,4096]{2,1,0:T(8,128)S(1)}, f32[1,32,4096]{2,1,0:T(8,128)}, u32[]{:S(2)}) copy-start(f32[1,32,4096]{2,1,0:T(8,128)} %param.20) | copy-start | bytes 1572868
  14.2 6.7 %copy-start.20 = (f32[1,1024,256]{2,1,0:T(8,128)S(1)}, f32[1,1024,256]{2,1,0:T(8,128)}, u32[]{:S(2)}) copy-start(f32[1,1024,256]{2,1,0:T(8,128)} %param.18) | copy-start | bytes 3145732
  14.2 26.7 %all-to-all-start.2 = ((bf16[4,2,49152]{2,1,0:T(2,128)(2,1)}), bf16[4,2,49152]{2,1,0:T(2,128)(2,1)}, u32[]{:S(2)}, u32[]{:S(2)}) async-start(bf16[4,2,49152]{2,1,0:T(2,128)(2,1)} %reshape.137), calls=%async_computation.3 | async-start | bytes 1572864 | tf_op jit(solution)/shard_map/all_to_all | solution.py:85
  21.7 2.8 copy-start.6
  21.7 2.8 copy-start.3
  24.6 6.5 %copy-start.22 = (s32[4]{0:T(128)S(1)}, s32[4]{0:T(128)}, u32[]{:S(2)}) copy-start(s32[4]{0:T(128)} %param.23) | copy-start | bytes 52
  40.9 213.6 %all-to-all-start = ((bf16[4,2,49152]{2,1,0:T(2,128)(2,1)}), bf16[4,2,49152]{2,1,0:T(2,128)(2,1)}, u32[]{:S(2)}, u32[]{:S(2)}) async-start(bf16[4,2,49152]{2,1,0:T(2,128)(2,1)} %reshape.141), calls=%async_computation | async-start | bytes 1572864 | tf_op jit(solution)/shard_map/all_to_all | solution.py:66
  45.1 56.4 %all-reduce.5.cloned.1.call-start = ((), (), s32[]{:S(2)}) async-start(), calls=%async_computation.10 | async-start | bytes 1572864 | tf_op jit(solution)/shard_map/while/body/eval_jaxpr/psum | solution.py:14
  101.5 0.9 copy-start.7
  102.5 47.4 %all-reduce.5.cloned.1.call-start = ((), (), s32[]{:S(2)}) async-start(), calls=%async_computation.10 | async-start | bytes 1572864 | tf_op jit(solution)/shard_map/while/body/eval_jaxpr/psum | solution.py:14
  149.9 0.9 copy-start.7
  151.0 47.1 %all-reduce.5.cloned.1.call-start = ((), (), s32[]{:S(2)}) async-start(), calls=%async_computation.10 | async-start | bytes 1572864 | tf_op jit(solution)/shard_map/while/body/eval_jaxpr/psum | solution.py:14
  198.1 0.9 copy-start.7
  199.1 46.9 %all-reduce.5.cloned.1.call-start = ((), (), s32[]{:S(2)}) async-start(), calls=%async_computation.10 | async-start | bytes 1572864 | tf_op jit(solution)/shard_map/while/body/eval_jaxpr/psum | solution.py:14
  246.1 1.2 copy-start.7
  247.4 0.8 copy-start.1
  247.4 7.0 %copy-start.4 = (bf16[32,4096]{1,0:T(8,128)(2,1)}, bf16[32,4096]{1,0:T(8,128)(2,1)S(1)}, u32[]{:S(2)}) copy-start(bf16[32,4096]{1,0:T(8,128)(2,1)S(1)} %get-tuple-element.118) | copy-start | bytes 786436
  247.4 80.2 %all-gather.5.cloned.1.call-start = ((), (), s32[]{:S(2)}) async-start(), calls=%async_computation.7 | async-start | bytes 2621440 | tf_op jit(solution)/shard_map/all_gather | solution.py:105
  262.9 2.1 copy-start.14
  270.8 7.2 %copy-start.2 = (bf16[1024,256]{1,0:T(8,128)(2,1)S(1)}, bf16[1024,256]{1,0:T(8,128)(2,1)}, u32[]{:S(2)}) copy-start(bf16[1024,256]{1,0:T(8,128)(2,1)} %copy-done.1) | copy-start | bytes 1572868
  272.5 7.2 %copy-start.23 = (f32[4]{0:T(128)S(1)}, f32[4]{0:T(128)}, u32[]{:S(2)}) copy-start(f32[4]{0:T(128)} %param.22) | copy-start | bytes 52
  272.5 23.8 %all-to-all-start.3 = ((bf16[4,2,49152]{2,1,0:T(2,128)(2,1)}), bf16[4,2,49152]{2,1,0:T(2,128)(2,1)S(1)}, u32[]{:S(2)}, u32[]{:S(2)}) async-start(bf16[4,2,49152]{2,1,0:T(2,128)(2,1)} %reshape.139), calls=%async_computation.4 | async-start | bytes 1572864 | tf_op jit(solution)/shard_map/all_to_all | solution.py:83
  276.2 57.4 %all-gather.3.cloned.1.call-start = ((), (), s32[]{:S(2)}) async-start(), calls=%async_computation.6 | async-start | bytes 1310720 | tf_op jit(solution)/shard_map/all_gather | solution.py:115
  296.4 4.2 %copy-start.13 = (bf16[4,2,49152]{2,1,0:T(2,128)(2,1)}, bf16[4,2,49152]{2,1,0:T(2,128)(2,1)S(1)}, u32[]{:S(2)}) copy-start(bf16[4,2,49152]{2,1,0:T(2,128)(2,1)S(1)} %all-to-all-done.3) | copy-start | bytes 2359300
  296.4 23.9 %all-to-all-start.1 = ((bf16[4,2,49152]{2,1,0:T(2,128)(2,1)}), bf16[4,2,49152]{2,1,0:T(2,128)(2,1)}, u32[]{:S(2)}, u32[]{:S(2)}) async-start(bf16[4,2,49152]{2,1,0:T(2,128)(2,1)} %reshape.143), calls=%async_computation.1 | async-start | bytes 1572864 | tf_op jit(solution)/shard_map/all_to_all | solution.py:64
  300.6 54.6 %reduce-scatter.5.cloned.1.call-start = ((), (), s32[]{:S(2)}) async-start(), calls=%async_computation.9 | async-start | bytes 1310720 | tf_op jit(solution)/shard_map/reduce_scatter | solution.py:135
  304.3 1.2 copy-start.8
  327.7 2.3 copy-start.9
  331.5 57.7 %reduce-scatter.3.cloned.1.call-start = ((), (), s32[]{:S(2)}) async-start(), calls=%async_computation.8 | async-start | bytes 2621440 | tf_op jit(solution)/shard_map/reduce_scatter | solution.py:123
  341.8 2.7 copy-start.17
  341.8 3.8 copy-start.10
  347.3 2.7 copy-start.18
  347.3 7.8 %copy-start.5 = (bf16[32,4096]{1,0:T(8,128)(2,1)S(1)}, bf16[32,4096]{1,0:T(8,128)(2,1)}, u32[]{:S(2)}) copy-start(bf16[32,4096]{1,0:T(8,128)(2,1)} %copy-done.4) | copy-start | bytes 786436
  351.1 38.1 %copy-start.11 = (f32[1024,256]{0,1:T(8,128)S(1)}, f32[1024,256]{0,1:T(8,128)}, u32[]{:S(2)}) copy-start(f32[1024,256]{0,1:T(8,128)} %copy.44) | copy-start | bytes 3145732
  351.1 38.1 %copy-start.15 = (bf16[1024,256]{0,1:T(8,128)(2,1)S(1)}, bf16[1024,256]{0,1:T(8,128)(2,1)}, u32[]{:S(2)}) copy-start(bf16[1024,256]{0,1:T(8,128)(2,1)} %copy.36) | copy-start | bytes 1572868
  393.5 2.7 copy-start.16
  393.5 3.7 copy-start.12
Sparse Core Ops, SparseCore 0:
  48.9 52.5 all-reduce.4
  106.4 43.5 all-reduce.4
  154.8 43.2 all-reduce.4
  202.7 43.3 all-reduce.4
Sparse Core Ops, SparseCore 1:
  250.0 21.4 all-gather.4
  278.8 17.5 all-gather.2
  331.6 23.5 reduce-scatter.4
  357.9 31.3 reduce-scatter.2
where the time goes:
time: 407 us; the launch traced here: 406 us
  waiting for transfers between devices  258 us (63%)
  local copies, waits for them, and re-layouts  60.8 us (15%)
  other arithmetic  38.8 us (10%)
  starting transfers between devices  19.2 us (5%)
  between operations  17.6 us (4%)
  matrix products  8.17 us (2%)
    psum x4, waiting for transfers between devices, spread(): return lax.psum(block, axis)  189 us
    unnamed x61, local copies, waits for them, and re-layouts  32 us
    reduce_scatter x1, waiting for transfers between devices, on_device(): lax.psum_scatter(lax.dot_general(columns, dpreact, (((0,), (0,)), ((), ()...  30.8 us
    all_to_all x1, waiting for transfers between devices, on_device(): lax.all_to_all(jnp.take(lax.all_to_all(joined(mom1_gate_up[0], mom1_down[...  13.5 us
    all_to_all x1, waiting for transfers between devices, on_device(): lax.all_to_all(jnp.take(lax.all_to_all(joined(mom2_gate_up[0], mom2_down[...  11.6 us
    all_to_all x1, waiting for transfers between devices, on_device(): lax.all_to_all(joined(mom2_gate_up[0], mom2_down[0]).astype(jnp.bfloat16)...  9.19 us
  transfers between devices with their start and end apart: 12, of which 9 were waited for; matrix products, arithmetic and copies ran while one was open for 22% of the time, Pallas kernels for 0%

commit v1 on v0

--- a/solution.py
+++ b/solution.py
@@ -22,7 +22,7 @@
     return (updated.astype(jnp.bfloat16), first_new, second_new)
 
 
-def on_device(
+def on_device_any(
     tokens,
     grad_out,
     gate_up,
@@ -147,9 +147,211 @@
     )
 
 
+def one_source_ring(chunk_count, stagger, own_chunk, distance, members):
+    ring = [(i, (i + 1) % members) for i in range(members)]
+    got = []
+    for step in range(chunk_count + stagger * (members - 2)):
+        if step < stagger:
+            send = own_chunk(step)
+        elif step < chunk_count:
+            send = jnp.where(distance == 0, own_chunk(step), got[step - stagger])
+        else:
+            send = got[step - stagger]
+        got.append(lax.ppermute(send, "member", ring))
+    return got
+
+
+def blocks_of(rows, cols):
+    return rows.reshape(rows.shape[0], -1, cols).transpose(1, 0, 2).reshape(-1, cols)
+
+
+def rows_of(blocks, count):
+    return blocks.reshape(-1, count, blocks.shape[1]).transpose(1, 0, 2).reshape(count, -1)
+
+
+def on_device_four(
+    tokens,
+    grad_out,
+    gate_up,
+    down,
+    mom1_gate_up,
+    mom2_gate_up,
+    mom1_down,
+    mom2_down,
+    learning,
+    winner,
+):
+    f32 = jnp.float32
+    bf16 = jnp.bfloat16
+    members = lax.axis_size("member")
+    member_index = lax.axis_index("member")
+    fsdp_index = lax.axis_index("fsdp")
+    chip = fsdp_index // 2
+    core = fsdp_index % 2
+    over_x = [(0, 2), (2, 0), (1, 3), (3, 1)]
+    over_core = [(0, 1), (1, 0), (2, 3), (3, 2)]
+    rows_in = tokens[0]
+    upstream = grad_out[0]
+    shard_gu = gate_up[0]
+    shard_dn = down[0]
+    count, width = rows_in.shape
+    half = width // 2
+    units = gate_up.shape[2] // 2
+    rows_gu, cols = shard_gu.shape
+    rows_dn = shard_dn.shape[0]
+    total = rows_gu + shard_dn.size // cols
+
+    mine = winner[member_index]
+    keep = mine == member_index
+    others = jnp.where(winner != jnp.arange(members, dtype=winner.dtype), winner, -1)
+    source = jnp.maximum(jnp.max(others), 0)
+    distance = lax.rem(member_index - source + members, members)
+    rate = learning[mine]
+
+    def my_half(x):
+        return lax.dynamic_slice_in_dim(x, chip * half, half, axis=1)
+
+    def their_half(x):
+        return lax.dynamic_slice_in_dim(x, (1 - chip) * half, half, axis=1)
+
+    dn_mine = my_half(shard_dn)
+    dn_near = lax.ppermute(their_half(shard_dn), "fsdp", over_x)
+    tok_mine = my_half(rows_in)
+    tok_near = lax.ppermute(their_half(rows_in), "fsdp", over_x)
+    up_mine = my_half(upstream)
+    up_near = lax.ppermute(their_half(upstream), "fsdp", over_x)
+
+    dn_pair = jnp.where(
+        chip == 0, jnp.concatenate([dn_mine, dn_near]), jnp.concatenate([dn_near, dn_mine])
+    )
+    dn_blocks = blocks_of(dn_pair, cols)
+    w_chunks = 4
+    m_chunks = 8
+    w_rows = total // w_chunks
+    m_rows = total // m_chunks
+    stagger = 2
+
+    def cut(first, second, start, stop):
+        parts = []
+        if start < rows_gu:
+            parts.append(first[start : min(stop, rows_gu)])
+        if stop > rows_gu:
+            parts.append(second[max(start - rows_gu, 0) : stop - rows_gu])
+        return parts[0] if len(parts) == 1 else jnp.concatenate(parts)
+
+    m1_blocks = blocks_of(mom1_down[0], cols)
+    m2_blocks = blocks_of(mom2_down[0], cols)
+
+    def own_chunk(c):
+        if c < w_chunks:
+            return cut(shard_gu, dn_blocks, c * w_rows, (c + 1) * w_rows)
+        c -= w_chunks
+        at = (c * m_rows, (c + 1) * m_rows)
+        return jnp.concatenate(
+            [cut(mom1_gate_up[0], m1_blocks, *at), cut(mom2_gate_up[0], m2_blocks, *at)]
+        ).astype(bf16)
+
+    chunks = w_chunks + m_chunks
+    got = one_source_ring(chunks, stagger, own_chunk, distance, members)
+
+    def arrived(c):
+        value = got[c]
+        for hop in range(1, members - 1):
+            value = jnp.where(distance == hop + 1, got[c + stagger * hop], value)
+        return value
+
+    weights = [jnp.where(keep, own_chunk(c), arrived(c)) for c in range(w_chunks)]
+    cut_chunk = rows_gu // w_rows
+    at = rows_gu - cut_chunk * w_rows
+    copied_gu = jnp.concatenate(weights[:cut_chunk] + [weights[cut_chunk][:at]])
+    copied_dn_blocks = jnp.concatenate([weights[cut_chunk][at:]] + weights[cut_chunk + 1 :])
+    copied_dn_pair = rows_of(copied_dn_blocks, 2 * rows_dn)
+
+    mate_gu = lax.ppermute(copied_gu, "fsdp", over_core)
+    gu_half = jnp.where(
+        core == 0,
+        jnp.concatenate([copied_gu, mate_gu]),
+        jnp.concatenate([mate_gu, copied_gu]),
+    )
+    mate_dn = lax.ppermute(copied_dn_pair, "fsdp", over_core)
+    both = jnp.stack([copied_dn_pair, mate_dn]).reshape(2, 2, rows_dn, half)
+    both = jnp.where(core == 0, both, both[::-1])
+    dn_half = both.transpose(1, 0, 2, 3).reshape(units, half)
+    dn_there = lax.dynamic_slice_in_dim(copied_dn_pair, (1 - chip) * rows_dn, rows_dn, axis=0)
+    dn_here = lax.dynamic_slice_in_dim(copied_dn_pair, chip * rows_dn, rows_dn, axis=0)
+    dn_back = lax.ppermute(dn_there, "fsdp", over_x)
+
+    def joined(here, back):
+        return jnp.where(
+            chip == 0,
+            jnp.concatenate([here, back], axis=1),
+            jnp.concatenate([back, here], axis=1),
+        )
+
+    copied_dn = joined(dn_here, dn_back)
+
+    tok = jnp.concatenate([tok_mine, tok_near])
+    up = jnp.concatenate([up_mine, up_near])
+    part = jnp.concatenate(
+        [
+            jnp.dot(tok, gu_half, preferred_element_type=f32),
+            lax.dot_general(up, dn_half, (((1,), (1,)), ((), ())), preferred_element_type=f32),
+        ],
+        axis=1,
+    )
+    near = lax.ppermute(part, "fsdp", over_x)
+    whole = part + jnp.concatenate([near[count:], near[:count]])
+    gate = whole[:, :units] * width ** (-0.5)
+    upper = whole[:, units : 2 * units] * width ** (-0.5)
+    dhidden = whole[:, 2 * units :] * units ** (-0.5)
+    sigma = jax.nn.sigmoid(gate)
+    active = gate * sigma
+    hidden = (active * upper).astype(bf16)
+    dgate = dhidden * upper * (sigma * (1.0 + gate * (1.0 - sigma)))
+    dupper = dhidden * active
+    dpreact = (jnp.concatenate([dgate, dupper], axis=1) * width ** (-0.5)).astype(bf16)
+
+    half_gu = lax.dot_general(
+        tok, dpreact, (((0,), (0,)), ((), ())), preferred_element_type=f32
+    )
+    for_mate = lax.dynamic_slice_in_dim(half_gu, (1 - core) * rows_gu, rows_gu, axis=0)
+    for_me = lax.dynamic_slice_in_dim(half_gu, core * rows_gu, rows_gu, axis=0)
+    grad_gu = for_me + lax.ppermute(for_mate.astype(bf16), "fsdp", over_core).astype(f32)
+    half_dn = lax.dot_general(
+        hidden, up, (((0,), (0,)), ((), ())), preferred_element_type=f32
+    ) * units ** (-0.5)
+    half_dn = half_dn.reshape(2, 2, rows_dn, half)
+    dn_for_mate = lax.dynamic_index_in_dim(half_dn, 1 - core, axis=1, keepdims=False)
+    dn_for_me = lax.dynamic_index_in_dim(half_dn, core, axis=1, keepdims=False)
+    pair_dn = dn_for_me + lax.ppermute(dn_for_mate.astype(bf16), "fsdp", over_core).astype(f32)
+    grad_there = lax.dynamic_index_in_dim(pair_dn, 1 - chip, axis=0, keepdims=False)
+    grad_here = lax.dynamic_index_in_dim(pair_dn, chip, axis=0, keepdims=False)
+    grad_back = lax.ppermute(grad_there.astype(bf16), "fsdp", over_x).astype(f32)
+    grad_dn = joined(grad_here, grad_back)
+
+    came = [arrived(c) for c in range(w_chunks, chunks)]
+    first = jnp.concatenate([p[:m_rows] for p in came])
+    second = jnp.concatenate([p[m_rows:] for p in came])
+    first_gu = jnp.where(keep, mom1_gate_up[0], first[:rows_gu].astype(f32))
+    second_gu = jnp.where(keep, mom2_gate_up[0], second[:rows_gu].astype(f32))
+    first_dn = jnp.where(keep, mom1_down[0], rows_of(first[rows_gu:], rows_dn).astype(f32))
+    second_dn = jnp.where(keep, mom2_down[0], rows_of(second[rows_gu:], rows_dn).astype(f32))
+    new_gu, new_first_gu, new_second_gu = adamw(copied_gu, grad_gu, first_gu, second_gu, rate)
+    new_dn, new_first_dn, new_second_dn = adamw(copied_dn, grad_dn, first_dn, second_dn, rate)
+    return (
+        new_gu[None],
+        new_dn[None],
+        new_first_gu[None],
+        new_second_gu[None],
+        new_first_dn[None],
+        new_second_dn[None],
+    )
+
+
 def solution(mesh):
+    small = mesh.shape["member"] == 4 and mesh.shape["fsdp"] == 4
     return jax.shard_map(
-        on_device,
+        on_device_four if small else on_device_any,
         mesh=mesh,
         in_specs=(
             P(("groups", "member"), "fsdp", None),

time: 407 us -> 140 us (0.34)
  waiting for transfers between devices: 258 us -> 66.7 us
  local copies, waits for them, and re-layouts: 60.8 us -> 28.3 us
  other arithmetic: 38.8 us -> 17.5 us
  between operations: 17.6 us -> 5.03 us
  starting transfers between devices: 19.2 us -> 14.5 us
    psum x4 -> x0, waiting for transfers between devices: 189 us -> none  [spread(): return lax.psum(block, axis)]
    ppermute x0 -> x26, waiting for transfers between devices: none -> 66.7 us  [the longest x16 53.9 us: one_source_ring(): got.append(lax.ppermute(send, 'member', ring))]
    reduce_scatter x2 -> x0, waiting for transfers between devices: 34.8 us -> none  [the longest x1 30.8 us: on_device(): lax.psum_scatter(lax.dot_general(columns, dpreact, (((0,), (0,)), ((), ()...]
    all_to_all x4 -> x0, waiting for transfers between devices: 34.3 us -> none  [the longest x1 13.5 us: on_device(): lax.all_to_all(jnp.take(lax.all_to_all(joined(mom1_gate_up[0], mom1_down[...]
    unnamed x61 -> x154, local copies, waits for them, and re-layouts: 32 us -> 2.88 us
    all_to_all x4 -> x0, starting transfers between devices: 18.5 us -> none  [the longest x1 6.45 us: on_device(): lax.all_to_all(joined(mom2_gate_up[0], mom2_down[0]).astype(jnp.bfloat16)...]
    ppermute x0 -> x26, starting transfers between devices: none -> 14.5 us  [the longest x16 5.5 us: one_source_ring(): got.append(lax.ppermute(send, 'member', ring))]
    mul x6 -> x0, local copies, waits for them, and re-layouts: 12.2 us -> none  [the longest x3 6.74 us: adamw(): second_new = beta_two * second + (1.0 - beta_two) * grad * grad]
  transfers between devices with their start and end apart: 12 -> 26, of which waited for: 9 -> 16; matrix products, arithmetic and copies ran while one was open for 22% -> 34% of each run, Pallas kernels for 0% -> 0%
where the time goes in v1:
time: 140 us; the launch traced here: 139 us
  waiting for transfers between devices  66.7 us (48%)
  local copies, waits for them, and re-layouts  28.3 us (20%)
  other arithmetic  17.5 us (12%)
  starting transfers between devices  14.5 us (10%)
  matrix products  7.16 us (5%)
  between operations  5.03 us (4%)
    ppermute x16, waiting for transfers between devices, one_source_ring(): got.append(lax.ppermute(send, 'member', ring))  53.9 us
    ppermute x1, waiting for transfers between devices, on_device_four(): near = lax.ppermute(part, 'fsdp', over_x)  8.42 us
    ppermute x16, starting transfers between devices, one_source_ring(): got.append(lax.ppermute(send, 'member', ring))  5.5 us
    ppermute x1, waiting for transfers between devices, on_device_four(): lax.ppermute(grad_there.astype(bf16), 'fsdp', over_x).astype(f32)  4.34 us
    slice x4, local copies, waits for them, and re-layouts, cut(): parts.append(first[start:min(stop, rows_gu)])  4.27 us
    dynamic_slice x3, local copies, waits for them, and re-layouts, my_half(): return lax.dynamic_slice_in_dim(x, chip * half, half, axis=1)  4.11 us
    convert_element_type x1, other arithmetic, adamw(): return (updated.astype(jnp.bfloat16), first_new, second_new)  3.21 us
    convert_element_type x2, local copies, waits for them, and re-layouts, on_device_four(): rows_of(first[rows_gu:], rows_dn).astype(f32)  3.03 us
  transfers between devices with their start and end apart: 26, of which 16 were waited for; matrix products, arithmetic and copies ran while one was open for 34% of the time, Pallas kernels for 0%

profile of v1, /device:TPU:0, one launch (start us, length us, event | category | flops | bytes accessed | tf_op | source)
XLA Modules:
  0.0 139.1 jit_solution(12187512290580290503)
XLA Ops:
  0.7 1.7 %constant_dynamic-slice_fusion.2 = (bf16[1,32,2048]{2,1,0:T(8,128)(2,1)}, bf16[32,2048]{1,0:T(8,128)(2,1)}) fusion(bf16[1,32,4096]{2,1,0:T(8,128)(2,1)} %param.13, s32[]{:T(128)S(6)} %select_n.313, s32[]{:T(128)S(6)} %select_n.314), kind=kLoop, calls=%fused_computation.139 | loop fusion | bytes 524296 | tf_op jit(solution)/shard_map/dynamic_slice | solution.py:212
  2.4 2.9 %collective-permute-start = (bf16[32,2048]{1,0:T(8,128)(2,1)}, bf16[32,2048]{1,0:T(8,128)(2,1)}, u32[]{:S(2)}, u32[]{:S(2)}) collective-permute-start(bf16[32,2048]{1,0:T(8,128)(2,1)} %get-tuple-element.51), channel_id=1, source_target_pairs={{0,2},{2,0},{1,3},{3,1},{4,6},{6,4},{5,7},{7,5},{8,10},{10,8},{9,1... | collective-permute-start | bytes 393224 | tf_op jit(solution)/shard_map/ppermute | solution.py:218
  5.3 1.8 %slice_bitcast_fusion = (bf16[384,256]{1,0:T(8,128)(2,1)}, bf16[384,256]{1,0:T(8,128)(2,1)}) fusion(bf16[1,1024,256]{2,1,0:T(8,128)(2,1)} %param.12), kind=kLoop, calls=%fused_computation.102 | loop fusion | bytes 786432 | tf_op jit(solution)/shard_map/slice | solution.py:237
  7.1 1.6 %collective-permute-start.4 = (bf16[384,256]{1,0:T(8,128)(2,1)}, bf16[384,256]{1,0:T(8,128)(2,1)S(1)}, u32[]{:S(2)}, u32[]{:S(2)}) collective-permute-start(bf16[384,256]{1,0:T(8,128)(2,1)} %get-tuple-element.32), channel_id=1, source_target_pairs={{0,4},{4,8},{8,12},{12,0},{1,5},{5,9},{9,13},{13,1},{2,6},{6,10},{... | collective-permute-start | bytes 589832 | tf_op jit(solution)/shard_map/ppermute | solution.py:160
  8.7 1.6 %collective-permute-start.1 = (bf16[384,256]{1,0:T(8,128)(2,1)}, bf16[384,256]{1,0:T(8,128)(2,1)S(1)}, u32[]{:S(2)}, u32[]{:S(2)}) collective-permute-start(bf16[384,256]{1,0:T(8,128)(2,1)} %get-tuple-element.33), channel_id=1, source_target_pairs={{0,4},{4,8},{8,12},{12,0},{1,5},{5,9},{9,13},{13,1},{2,6},{6,10},{... | collective-permute-start | bytes 589832 | tf_op jit(solution)/shard_map/ppermute | solution.py:160
  10.3 0.9 slice_bitcast_fusion.2
  11.2 1.2 convert.75
  12.5 0.7 fusion.53
  13.4 0.7 fusion.54
  14.2 0.9 slice_bitcast_fusion.5
  15.2 0.6 slice_bitcast_fusion.13
  15.8 0.6 fusion.40
  17.0 0.6 slice.332
  17.6 0.6 slice.334
  18.3 1.0 copy.33
  19.8 0.7 copy-done.25
  20.5 1.5 %collective-permute-start.2 = (bf16[384,256]{1,0:T(8,128)(2,1)S(1)}, bf16[384,256]{1,0:T(8,128)(2,1)S(1)}, u32[]{:S(2)}, u32[]{:S(2)}) collective-permute-start(bf16[384,256]{1,0:T(8,128)(2,1)S(1)} %broadcast_select_fusion), channel_id=1, source_target_pairs={{0,4},{4,8},{8,12},{12,0},{1,5},{5,9},{9,13},{13,1},{2,6},{6,10},{... | collective-permute-start | bytes 589832 | tf_op jit(solution)/shard_map/ppermute | solution.py:160
  22.4 7.8 %collective-permute-done.2 = bf16[384,256]{1,0:T(8,128)(2,1)S(1)} collective-permute-done((bf16[384,256]{1,0:T(8,128)(2,1)S(1)}, bf16[384,256]{1,0:T(8,128)(2,1)S(1)}, u32[]{:S(2)}, u32[]{:S(2)}) %collective-permute-start.2) | collective-permute-done | bytes 196640 | tf_op jit(solution)/shard_map/ppermute | solution.py:160
  30.4 3.9 %collective-permute-done.5 = bf16[384,256]{1,0:T(8,128)(2,1)S(1)} collective-permute-done((bf16[384,256]{1,0:T(8,128)(2,1)S(1)}, bf16[384,256]{1,0:T(8,128)(2,1)S(1)}, u32[]{:S(2)}, u32[]{:S(2)}) %collective-permute-start.5) | collective-permute-done | bytes 196640 | tf_op jit(solution)/shard_map/ppermute | solution.py:160
  34.3 4.8 %collective-permute-done.3 = bf16[384,256]{1,0:T(8,128)(2,1)S(1)} collective-permute-done((bf16[384,256]{1,0:T(8,128)(2,1)S(1)}, bf16[384,256]{1,0:T(8,128)(2,1)S(1)}, u32[]{:S(2)}, u32[]{:S(2)}) %collective-permute-start.3) | collective-permute-done | bytes 196640 | tf_op jit(solution)/shard_map/ppermute | solution.py:160
  39.3 4.4 %collective-permute-done.6 = bf16[384,256]{1,0:T(8,128)(2,1)S(1)} collective-permute-done((bf16[384,256]{1,0:T(8,128)(2,1)S(1)}, bf16[384,256]{1,0:T(8,128)(2,1)S(1)}, u32[]{:S(2)}, u32[]{:S(2)}) %collective-permute-start.6) | collective-permute-done | bytes 196640 | tf_op jit(solution)/shard_map/ppermute | solution.py:160
  43.8 3.9 %collective-permute-done.7 = bf16[384,256]{1,0:T(8,128)(2,1)S(1)} collective-permute-done((bf16[384,256]{1,0:T(8,128)(2,1)S(1)}, bf16[384,256]{1,0:T(8,128)(2,1)S(1)}, u32[]{:S(2)}, u32[]{:S(2)}) %collective-permute-start.7) | collective-permute-done | bytes 196640 | tf_op jit(solution)/shard_map/ppermute | solution.py:160
  47.7 4.8 %collective-permute-done.9 = bf16[384,256]{1,0:T(8,128)(2,1)S(1)} collective-permute-done((bf16[384,256]{1,0:T(8,128)(2,1)S(1)}, bf16[384,256]{1,0:T(8,128)(2,1)S(1)}, u32[]{:S(2)}, u32[]{:S(2)}) %collective-permute-start.9) | collective-permute-done | bytes 196640 | tf_op jit(solution)/shard_map/ppermute | solution.py:160
  52.7 4.4 %collective-permute-done.8 = bf16[384,256]{1,0:T(8,128)(2,1)S(1)} collective-permute-done((bf16[384,256]{1,0:T(8,128)(2,1)S(1)}, bf16[384,256]{1,0:T(8,128)(2,1)S(1)}, u32[]{:S(2)}, u32[]{:S(2)}) %collective-permute-start.8) | collective-permute-done | bytes 196640 | tf_op jit(solution)/shard_map/ppermute | solution.py:160
  57.3 4.2 %collective-permute-done.10 = bf16[384,256]{1,0:T(8,128)(2,1)S(1)} collective-permute-done((bf16[384,256]{1,0:T(8,128)(2,1)S(1)}, bf16[384,256]{1,0:T(8,128)(2,1)S(1)}, u32[]{:S(2)}, u32[]{:S(2)}) %collective-permute-start.10) | collective-permute-done | bytes 196640 | tf_op jit(solution)/shard_map/ppermute | solution.py:160
  61.6 4.9 %collective-permute-done.11 = bf16[384,256]{1,0:T(8,128)(2,1)S(1)} collective-permute-done((bf16[384,256]{1,0:T(8,128)(2,1)S(1)}, bf16[384,256]{1,0:T(8,128)(2,1)S(1)}, u32[]{:S(2)}, u32[]{:S(2)}) %collective-permute-start.11) | collective-permute-done | bytes 196640 | tf_op jit(solution)/shard_map/ppermute | solution.py:160
  66.6 1.0 dynamic-slice_bitcast_fusion.3
  67.7 0.9 collective-permute-start.15
  68.6 2.7 %collective-permute-done.12 = bf16[384,256]{1,0:T(8,128)(2,1)} collective-permute-done((bf16[384,256]{1,0:T(8,128)(2,1)S(1)}, bf16[384,256]{1,0:T(8,128)(2,1)}, u32[]{:S(2)}, u32[]{:S(2)}) %collective-permute-start.12) | collective-permute-done | bytes 196640 | tf_op jit(solution)/shard_map/ppermute | solution.py:160
  71.2 4.1 %collective-permute-done.13 = bf16[384,256]{1,0:T(8,128)(2,1)} collective-permute-done((bf16[384,256]{1,0:T(8,128)(2,1)S(1)}, bf16[384,256]{1,0:T(8,128)(2,1)}, u32[]{:S(2)}, u32[]{:S(2)}) %collective-permute-start.13) | collective-permute-done | bytes 196640 | tf_op jit(solution)/shard_map/ppermute | solution.py:160
  75.4 1.3 dynamic-slice_bitcast_fusion.1
  76.7 1.1 collective-permute-start.17
  81.1 0.7 dynamic_slice.64
  81.8 1.5 %collective-permute-done.22 = bf16[384,256]{1,0:T(8,128)(2,1)} collective-permute-done((bf16[384,256]{1,0:T(8,128)(2,1)}, bf16[384,256]{1,0:T(8,128)(2,1)}, u32[]{:S(2)}, u32[]{:S(2)}) %collective-permute-start.22) | collective-permute-done | bytes 196640 | tf_op jit(solution)/shard_map/ppermute | solution.py:160
  83.2 2.3 %select_select_fusion.1 = (bf16[384,256]{1,0:T(8,128)(2,1)S(1)}, bf16[384,256]{1,0:T(8,128)(2,1)}, bf16[384,256]{1,0:T(8,128)(2,1)}, bf16[384,256]{1,0:T(8,128)(2,1)}, bf16[384,256]{1,0:T(8,128)(2,1)S(1)}) fusion(bf16[384,256]{1,0:T(8,128)(2,1)} %collective-permute-done.22, bf16[384,256]{1,0:T(8,128)(2,1)} %collective-permute-done.13, ...), kind=kLoop, calls=%fused_computation.89 | loop fusion | flops 1474560 | bytes 2555907 | tf_op jit(solution)/shard_map/jit(_where)/select_n | solution.py:260
  85.6 0.7 slice.327
  86.3 0.7 fusion.56
  87.0 2.5 %collective-permute-done.23 = bf16[384,256]{1,0:T(8,128)(2,1)S(1)} collective-permute-done((bf16[384,256]{1,0:T(8,128)(2,1)}, bf16[384,256]{1,0:T(8,128)(2,1)S(1)}, u32[]{:S(2)}, u32[]{:S(2)}) %collective-permute-start.23) | collective-permute-done | bytes 196640 | tf_op jit(solution)/shard_map/ppermute | solution.py:160
  89.5 2.1 %select_select_fusion.10 = (bf16[384,256]{1,0:T(8,128)(2,1)S(1)}, bf16[384,256]{1,0:T(8,128)(2,1)S(1)}, bf16[384,256]{1,0:T(8,128)(2,1)S(1)}, bf16[384,256]{1,0:...) fusion(bf16[384,256]{1,0:T(8,128)(2,1)} %copy-done.11, ...), kind=kLoop, calls=%fused_computation.103 | loop fusion | flops 1671168 | bytes 4128771 | tf_op jit(solution)/shard_map/jit(_where)/select_n | solution.py:263
  91.6 0.9 copy.43
  92.5 1.8 %stack.8 = bf16[1,2,32,2048]{3,2,1,0:T(8,128)(2,1)} reshape(bf16[64,8,256]{2,1,0:T(8,128)(2,1)} %bitcast.147) | data formatting | bytes 524288 | tf_op jit(solution)/shard_map/stack | solution.py:277
  94.4 0.8 dynamic-slice_bitcast_fusion.4
  95.2 1.0 collective-permute-start.21
  96.2 1.0 pad_maximum_fusion.7
  97.6 0.7 fusion.55
  98.3 0.7 fusion.57
  99.9 1.7 %fusion.22 = f32[384,128]{0,1:T(8,128)S(1)} fusion(bf16[128,2048]{1,0:T(8,128)(2,1)S(1)} %bitcast.154, bf16[192,2048]{1,0:T(8,128)(2,1)} %collective-permute-done.17, bf16[192,2048]{1,0:T(8,128)(2,1)S(1)} %copy-done.36), kind=kOutput, calls=%fused_computation.33 | convolution fusion | flops 204472320 | bytes 2293760 | tf_op jit(solution)/shard_map/dot_general | solution.py:298
  101.7 1.9 %fusion.4 = f32[384,256]{0,1:T(8,128)S(1)} fusion(bf16[1024,256]{1,0:T(8,128)(2,1)S(1)} %collective-permute-done.16, bf16[256,256]{1,0:T(8,128)(2,1)S(1)} %copy-done.16, bf16[384,256]{1,0:T(8,128)(2,1)S(1)} %get-tuple-element.31, bf16[384,256]{1,0:T(8,128)(2,1)S(1)} %get-tuple-element.30, pred[]{:T(512)S(6)} %eq.19, ...), kind=kOutput, calls=%fused_computation.11 | convolution fusion | flops 414711808 | bytes 3014657 | tf_op jit(solution)/shard_map/dot_general | solution.py:297
  103.6 0.9 pad_maximum_fusion.6
  104.5 1.1 collective-permute-start.19
  105.6 1.1 copy.30
  106.7 1.1 reshape.292
  107.9 1.0 pad_maximum_fusion.11
  108.9 1.1 copy.28
  110.0 1.9 %reshape.290 = f32[1,32,4096]{2,1,0:T(8,128)} reshape(f32[32,16,256]{2,1,0:T(8,128)} %copy.28) | data formatting | bytes 1048576 | tf_op jit(solution)/shard_map/convert_element_type | solution.py:337
  111.9 8.4 %collective-permute-done.19 = f32[384,384]{0,1:T(8,128)} collective-permute-done((f32[384,384]{0,1:T(8,128)}, f32[384,384]{0,1:T(8,128)}, u32[]{:S(2)}, u32[]{:S(2)}) %collective-permute-start.19) | collective-permute-done | bytes 589856 | tf_op jit(solution)/shard_map/ppermute | solution.py:302
  120.3 1.3 fusion.52
  121.6 1.3 maximum_add_fusion
  123.0 1.6 %convolution_multiply_fusion = f32[128,2048]{1,0:T(8,128)S(1)} fusion(bf16[192,2048]{1,0:T(8,128)(2,1)} %collective-permute-done.17, bf16[192,2048]{1,0:T(8,128)(2,1)S(1)} %copy-done.37, f32[384,384]{0,1:T(8,128)S(1)} %maximum_add_fusion), kind=kOutput, calls=%fused_computation | convolution fusion | flops 205127680 | bytes 3014656 | tf_op jit(solution)/shard_map/dot_general | solution.py:320
  124.8 1.9 %fusion.23 = f32[2048,256]{1,0:T(8,128)S(1)} fusion(bf16[192,2048]{1,0:T(8,128)(2,1)} %collective-permute-done.15, bf16[192,2048]{1,0:T(8,128)(2,1)S(1)} %get-tuple-element.14, f32[384,128]{0,1:T(8,128)S(1)} %get-tuple-element.17, f32[384,128]{0,1:T(8,128)S(1)} %get-tuple-element.16), kind=kOutput, calls=%fused_computation.34 | convolution fusion | flops 406093824 | bytes 4063232 | tf_op jit(solution)/shard_map/dot_general | solution.py:314
  127.4 1.1 collective-permute-start.25
  128.6 4.3 %collective-permute-done.25 = bf16[32,2048]{1,0:T(8,128)(2,1)S(1)} collective-permute-done((bf16[32,2048]{1,0:T(8,128)(2,1)S(1)}, bf16[32,2048]{1,0:T(8,128)(2,1)S(1)}, u32[]{:S(2)}, u32[]{:S(2)}) %collective-permute-start.25) | collective-permute-done | bytes 131104 | tf_op jit(solution)/shard_map/ppermute | solution.py:329
  133.1 3.2 %fusion.26 = (bf16[1,32,4096]{2,1,0:T(8,128)(2,1)}, f32[1,32,4096]{2,1,0:T(8,128)}, f32[1,32,4096]{2,1,0:T(8,128)}) fusion(bf16[1,32,2048]{2,1,0:T(8,128)(2,1)} %bitcast.42, bf16[1,32,2048]{2,1,0:T(8,128)(2,1)S(1)} %copy-done.48, f32[]{:T(128)} %bitcast.14, pred[]{:T(512)S(6)} %eq.17, f32[1,32,2048]{2,1,0:T(8,128)S(1)} %constant_dynamic-slice_fusion, ...), kind=kLoop, calls=%fused_computation.47 | loop fusion | flops 3801088 | bytes 4194310 | tf_op jit(solution)/shard_map/convert_element_type | solution.py:22
  136.3 2.8 %fusion.29 = (bf16[1,1024,256]{2,1,0:T(8,128)(2,1)}, f32[1024,256]{1,0:T(8,128)}, f32[1024,256]{1,0:T(8,128)}) fusion(f32[]{:T(128)} %bitcast.14, bf16[256,256]{1,0:T(8,128)(2,1)S(1)} %copy-done.17, bf16[384,256]{1,0:T(8,128)(2,1)S(1)} %copy-done.9, bf16[384,256]{1,0:T(8,128)(2,1)S(1)} %copy-done.7, bf16[1024,256]{1,0:T(8,128)(2,1)S(1)} %collective-permute-done.20, ...), kind=kLoop, calls=%fused_computation.58 | loop fusion | flops 6815744 | bytes 7864329 | tf_op jit(solution)/shard_map/broadcast_in_dim | solution.py:342
  (216 shorter events, 5.3 us)
Async XLA Ops:
  0.6 12.6 %copy-start.2 = (f32[1,32,4096]{2,1,0:T(8,128)S(1)}, f32[1,32,4096]{2,1,0:T(8,128)}, u32[]{:S(2)}) copy-start(f32[1,32,4096]{2,1,0:T(8,128)} %param.17) | copy-start | bytes 1572868
  2.4 15.9 %collective-permute-start = (bf16[32,2048]{1,0:T(8,128)(2,1)}, bf16[32,2048]{1,0:T(8,128)(2,1)}, u32[]{:S(2)}, u32[]{:S(2)}) collective-permute-start(bf16[32,2048]{1,0:T(8,128)(2,1)} %get-tuple-element.51), channel_id=1, source_target_pairs={{0,2},{2,0},{1,3},{3,1},{4,6},{6,4},{5,7},{7,5},{8,10},{10,8},{9,1... | collective-permute-start | bytes 393224 | tf_op jit(solution)/shard_map/ppermute | solution.py:218
  7.1 14.9 %collective-permute-start.4 = (bf16[384,256]{1,0:T(8,128)(2,1)}, bf16[384,256]{1,0:T(8,128)(2,1)S(1)}, u32[]{:S(2)}, u32[]{:S(2)}) collective-permute-start(bf16[384,256]{1,0:T(8,128)(2,1)} %get-tuple-element.32), channel_id=1, source_target_pairs={{0,4},{4,8},{8,12},{12,0},{1,5},{5,9},{9,13},{13,1},{2,6},{6,10},{... | collective-permute-start | bytes 589832 | tf_op jit(solution)/shard_map/ppermute | solution.py:160
  8.7 11.1 %collective-permute-start.1 = (bf16[384,256]{1,0:T(8,128)(2,1)}, bf16[384,256]{1,0:T(8,128)(2,1)S(1)}, u32[]{:S(2)}, u32[]{:S(2)}) collective-permute-start(bf16[384,256]{1,0:T(8,128)(2,1)} %get-tuple-element.33), channel_id=1, source_target_pairs={{0,4},{4,8},{8,12},{12,0},{1,5},{5,9},{9,13},{13,1},{2,6},{6,10},{... | collective-permute-start | bytes 589832 | tf_op jit(solution)/shard_map/ppermute | solution.py:160
  11.2 8.6 %copy-start.18 = (bf16[256,256]{1,0:T(8,128)(2,1)}, bf16[256,256]{1,0:T(8,128)(2,1)S(1)}, u32[]{:S(2)}) copy-start(bf16[256,256]{1,0:T(8,128)(2,1)S(1)} %slice_bitcast_fusion.2) | copy-start | bytes 393220
  18.3 15.9 %copy-start.61 = (bf16[192,256]{1,0:T(8,128)(2,1)S(1)}, bf16[192,256]{1,0:T(8,128)(2,1)}, u32[]{:S(2)}) copy-start(bf16[192,256]{1,0:T(8,128)(2,1)} %get-tuple-element.28) | copy-start | bytes 294916
  18.3 15.9 %copy-start.62 = (bf16[192,256]{1,0:T(8,128)(2,1)S(1)}, bf16[192,256]{1,0:T(8,128)(2,1)}, u32[]{:S(2)}) copy-start(bf16[192,256]{1,0:T(8,128)(2,1)} %get-tuple-element.71) | copy-start | bytes 294916
  18.3 11.9 %copy-start.63 = (bf16[192,256]{1,0:T(8,128)(2,1)S(1)}, bf16[192,256]{1,0:T(8,128)(2,1)}, u32[]{:S(2)}) copy-start(bf16[192,256]{1,0:T(8,128)(2,1)} %get-tuple-element.29) | copy-start | bytes 294916
  18.3 11.9 %copy-start.64 = (bf16[192,256]{1,0:T(8,128)(2,1)S(1)}, bf16[192,256]{1,0:T(8,128)(2,1)}, u32[]{:S(2)}) copy-start(bf16[192,256]{1,0:T(8,128)(2,1)} %get-tuple-element.70) | copy-start | bytes 294916
  19.4 19.8 %copy-start.59 = (bf16[192,256]{1,0:T(8,128)(2,1)S(1)}, bf16[192,256]{1,0:T(8,128)(2,1)}, u32[]{:S(2)}) copy-start(bf16[192,256]{1,0:T(8,128)(2,1)} %get-tuple-element.27) | copy-start | bytes 294916
  19.4 19.8 %copy-start.60 = (bf16[192,256]{1,0:T(8,128)(2,1)S(1)}, bf16[192,256]{1,0:T(8,128)(2,1)}, u32[]{:S(2)}) copy-start(bf16[192,256]{1,0:T(8,128)(2,1)} %get-tuple-element.72) | copy-start | bytes 294916
  19.4 24.2 %copy-start.57 = (bf16[192,256]{1,0:T(8,128)(2,1)S(1)}, bf16[192,256]{1,0:T(8,128)(2,1)}, u32[]{:S(2)}) copy-start(bf16[192,256]{1,0:T(8,128)(2,1)} %get-tuple-element.26) | copy-start | bytes 294916
  19.4 24.2 %copy-start.58 = (bf16[192,256]{1,0:T(8,128)(2,1)S(1)}, bf16[192,256]{1,0:T(8,128)(2,1)}, u32[]{:S(2)}) copy-start(bf16[192,256]{1,0:T(8,128)(2,1)} %get-tuple-element.73) | copy-start | bytes 294916
  19.6 28.1 %copy-start.55 = (bf16[192,256]{1,0:T(8,128)(2,1)S(1)}, bf16[192,256]{1,0:T(8,128)(2,1)}, u32[]{:S(2)}) copy-start(bf16[192,256]{1,0:T(8,128)(2,1)} %get-tuple-element.25) | copy-start | bytes 294916
  19.6 28.1 %copy-start.56 = (bf16[192,256]{1,0:T(8,128)(2,1)S(1)}, bf16[192,256]{1,0:T(8,128)(2,1)}, u32[]{:S(2)}) copy-start(bf16[192,256]{1,0:T(8,128)(2,1)} %get-tuple-element.74) | copy-start | bytes 294916
  19.6 33.0 %copy-start.65 = (bf16[4,32,256]{2,1,0:T(8,128)(2,1)S(1)}, bf16[4,32,256]{2,1,0:T(8,128)(2,1)}, u32[]{:S(2)}) copy-start(bf16[4,32,256]{2,1,0:T(8,128)(2,1)} %slice.332) | copy-start | bytes 196612
  19.7 32.9 %copy-start.66 = (bf16[4,32,256]{2,1,0:T(8,128)(2,1)S(1)}, bf16[4,32,256]{2,1,0:T(8,128)(2,1)}, u32[]{:S(2)}) copy-start(bf16[4,32,256]{2,1,0:T(8,128)(2,1)} %slice.334) | copy-start | bytes 196612
  19.7 32.9 %copy-start.68 = (bf16[64,256]{1,0:T(8,128)(2,1)S(1)}, bf16[64,256]{1,0:T(8,128)(2,1)}, u32[]{:S(2)}) copy-start(bf16[64,256]{1,0:T(8,128)(2,1)} %get-tuple-element.75) | copy-start | bytes 98308
  19.7 32.9 %copy-start.69 = (bf16[64,256]{1,0:T(8,128)(2,1)S(1)}, bf16[64,256]{1,0:T(8,128)(2,1)}, u32[]{:S(2)}) copy-start(bf16[64,256]{1,0:T(8,128)(2,1)} %get-tuple-element.76) | copy-start | bytes 98308
  20.5 36.6 %copy-start.52 = (bf16[6,32,256]{2,1,0:T(8,128)(2,1)S(1)}, bf16[6,32,256]{2,1,0:T(8,128)(2,1)}, u32[]{:S(2)}) copy-start(bf16[6,32,256]{2,1,0:T(8,128)(2,1)} %get-tuple-element.47) | copy-start | bytes 294916
  20.5 36.6 %copy-start.53 = (bf16[6,32,256]{2,1,0:T(8,128)(2,1)S(1)}, bf16[6,32,256]{2,1,0:T(8,128)(2,1)}, u32[]{:S(2)}) copy-start(bf16[6,32,256]{2,1,0:T(8,128)(2,1)} %get-tuple-element.49) | copy-start | bytes 294916
  20.5 9.7 %collective-permute-start.2 = (bf16[384,256]{1,0:T(8,128)(2,1)S(1)}, bf16[384,256]{1,0:T(8,128)(2,1)S(1)}, u32[]{:S(2)}, u32[]{:S(2)}) collective-permute-start(bf16[384,256]{1,0:T(8,128)(2,1)S(1)} %broadcast_select_fusion), channel_id=1, source_target_pairs={{0,4},{4,8},{8,12},{12,0},{1,5},{5,9},{9,13},{13,1},{2,6},{6,10},{... | collective-permute-start | bytes 589832 | tf_op jit(solution)/shard_map/ppermute | solution.py:160
  22.1 39.3 %copy-start.51 = (bf16[6,32,256]{2,1,0:T(8,128)(2,1)S(1)}, bf16[6,32,256]{2,1,0:T(8,128)(2,1)}, u32[]{:S(2)}) copy-start(bf16[6,32,256]{2,1,0:T(8,128)(2,1)} %get-tuple-element.46) | copy-start | bytes 294916
  22.1 12.1 %collective-permute-start.5 = (bf16[384,256]{1,0:T(8,128)(2,1)S(1)}, bf16[384,256]{1,0:T(8,128)(2,1)S(1)}, u32[]{:S(2)}, u32[]{:S(2)}) collective-permute-start(bf16[384,256]{1,0:T(8,128)(2,1)S(1)} %bitcast_select_fusion.3), channel_id=1, source_target_pairs={{0,4},{4,8},{8,12},{12,0},{1,5},{5,9},{9,13},{13,1},{2,6},{6,10},{... | collective-permute-start | bytes 589832 | tf_op jit(solution)/shard_map/ppermute | solution.py:160
  30.2 55.4 %copy-start.10 = (bf16[384,256]{1,0:T(8,128)(2,1)}, bf16[384,256]{1,0:T(8,128)(2,1)S(1)}, u32[]{:S(2)}) copy-start(bf16[384,256]{1,0:T(8,128)(2,1)S(1)} %collective-permute-done.2) | copy-start | bytes 589828
  30.3 36.4 %copy-start.13 = (bf16[1,192,4096]{2,1,0:T(8,128)(2,1)S(1)}, bf16[1,192,4096]{2,1,0:T(8,128)(2,1)}, u32[]{:S(2)}) copy-start(bf16[1,192,4096]{2,1,0:T(8,128)(2,1)} %param.10) | copy-start | bytes 4718596
  30.3 8.8 %collective-permute-start.3 = (bf16[384,256]{1,0:T(8,128)(2,1)S(1)}, bf16[384,256]{1,0:T(8,128)(2,1)S(1)}, u32[]{:S(2)}, u32[]{:S(2)}) collective-permute-start(bf16[384,256]{1,0:T(8,128)(2,1)S(1)} %maximum_select_fusion.5), channel_id=1, source_target_pairs={{0,4},{4,8},{8,12},{12,0},{1,5},{5,9},{9,13},{13,1},{2,6},{6,10},{... | collective-permute-start | bytes 589832 | tf_op jit(solution)/shard_map/ppermute | solution.py:160
  34.2 32.3 %copy-start.27 = (bf16[384,256]{1,0:T(8,128)(2,1)}, bf16[384,256]{1,0:T(8,128)(2,1)S(1)}, u32[]{:S(2)}) copy-start(bf16[384,256]{1,0:T(8,128)(2,1)S(1)} %collective-permute-done.5) | copy-start | bytes 589828
  34.3 9.4 %collective-permute-start.6 = (bf16[384,256]{1,0:T(8,128)(2,1)S(1)}, bf16[384,256]{1,0:T(8,128)(2,1)S(1)}, u32[]{:S(2)}, u32[]{:S(2)}) collective-permute-start(bf16[384,256]{1,0:T(8,128)(2,1)S(1)} %maximum_select_fusion.6), channel_id=1, source_target_pairs={{0,4},{4,8},{8,12},{12,0},{1,5},{5,9},{9,13},{13,1},{2,6},{6,10},{... | collective-permute-start | bytes 589832 | tf_op jit(solution)/shard_map/ppermute | solution.py:160
  39.1 46.5 %copy-start.11 = (bf16[384,256]{1,0:T(8,128)(2,1)}, bf16[384,256]{1,0:T(8,128)(2,1)S(1)}, u32[]{:S(2)}) copy-start(bf16[384,256]{1,0:T(8,128)(2,1)S(1)} %collective-permute-done.3) | copy-start | bytes 589828
  39.2 8.4 %collective-permute-start.7 = (bf16[384,256]{1,0:T(8,128)(2,1)S(1)}, bf16[384,256]{1,0:T(8,128)(2,1)S(1)}, u32[]{:S(2)}, u32[]{:S(2)}) collective-permute-start(bf16[384,256]{1,0:T(8,128)(2,1)S(1)} %maximum_select_fusion.7), channel_id=1, source_target_pairs={{0,4},{4,8},{8,12},{12,0},{1,5},{5,9},{9,13},{13,1},{2,6},{6,10},{... | collective-permute-start | bytes 589832 | tf_op jit(solution)/shard_map/ppermute | solution.py:160
  43.6 22.9 %copy-start.29 = (bf16[384,256]{1,0:T(8,128)(2,1)}, bf16[384,256]{1,0:T(8,128)(2,1)S(1)}, u32[]{:S(2)}) copy-start(bf16[384,256]{1,0:T(8,128)(2,1)S(1)} %collective-permute-done.6) | copy-start | bytes 589828
  43.7 8.9 %collective-permute-start.9 = (bf16[384,256]{1,0:T(8,128)(2,1)S(1)}, bf16[384,256]{1,0:T(8,128)(2,1)S(1)}, u32[]{:S(2)}, u32[]{:S(2)}) collective-permute-start(bf16[384,256]{1,0:T(8,128)(2,1)S(1)} %maximum_select_fusion.10), channel_id=1, source_target_pairs={{0,4},{4,8},{8,12},{12,0},{1,5},{5,9},{9,13},{13,1},{2,6},{6,10},{... | collective-permute-start | bytes 589832 | tf_op jit(solution)/shard_map/ppermute | solution.py:160
  47.7 9.4 %collective-permute-start.8 = (bf16[384,256]{1,0:T(8,128)(2,1)S(1)}, bf16[384,256]{1,0:T(8,128)(2,1)S(1)}, u32[]{:S(2)}, u32[]{:S(2)}) collective-permute-start(bf16[384,256]{1,0:T(8,128)(2,1)S(1)} %maximum_select_fusion.8), channel_id=1, source_target_pairs={{0,4},{4,8},{8,12},{12,0},{1,5},{5,9},{9,13},{13,1},{2,6},{6,10},{... | collective-permute-start | bytes 589832 | tf_op jit(solution)/shard_map/ppermute | solution.py:160
  52.6 13.9 %copy-start.31 = (bf16[384,256]{1,0:T(8,128)(2,1)}, bf16[384,256]{1,0:T(8,128)(2,1)S(1)}, u32[]{:S(2)}) copy-start(bf16[384,256]{1,0:T(8,128)(2,1)S(1)} %collective-permute-done.9) | copy-start | bytes 589828
  52.7 8.8 %collective-permute-start.10 = (bf16[384,256]{1,0:T(8,128)(2,1)S(1)}, bf16[384,256]{1,0:T(8,128)(2,1)S(1)}, u32[]{:S(2)}, u32[]{:S(2)}) collective-permute-start(bf16[384,256]{1,0:T(8,128)(2,1)S(1)} %maximum_select_fusion.9), channel_id=1, source_target_pairs={{0,4},{4,8},{8,12},{12,0},{1,5},{5,9},{9,13},{13,1},{2,6},{6,10},{... | collective-permute-start | bytes 589832 | tf_op jit(solution)/shard_map/ppermute | solution.py:160
  57.1 9.4 %copy-start.43 = (bf16[384,256]{1,0:T(8,128)(2,1)}, bf16[384,256]{1,0:T(8,128)(2,1)S(1)}, u32[]{:S(2)}) copy-start(bf16[384,256]{1,0:T(8,128)(2,1)S(1)} %collective-permute-done.8) | copy-start | bytes 589828
  57.1 18.2 %copy-start.14 = (bf16[1,192,4096]{2,1,0:T(8,128)(2,1)S(1)}, bf16[1,192,4096]{2,1,0:T(8,128)(2,1)}, u32[]{:S(2)}) copy-start(bf16[1,192,4096]{2,1,0:T(8,128)(2,1)} %param.11) | copy-start | bytes 4718596
  57.2 9.3 %collective-permute-start.11 = (bf16[384,256]{1,0:T(8,128)(2,1)S(1)}, bf16[384,256]{1,0:T(8,128)(2,1)S(1)}, u32[]{:S(2)}, u32[]{:S(2)}) collective-permute-start(bf16[384,256]{1,0:T(8,128)(2,1)S(1)} %maximum_select_fusion.11), channel_id=1, source_target_pairs={{0,4},{4,8},{8,12},{12,0},{1,5},{5,9},{9,13},{13,1},{2,6},{6,10},{... | collective-permute-start | bytes 589832 | tf_op jit(solution)/shard_map/ppermute | solution.py:160
  61.5 9.7 %collective-permute-start.12 = (bf16[384,256]{1,0:T(8,128)(2,1)S(1)}, bf16[384,256]{1,0:T(8,128)(2,1)}, u32[]{:S(2)}, u32[]{:S(2)}) collective-permute-start(bf16[384,256]{1,0:T(8,128)(2,1)S(1)} %maximum_select_fusion.12), channel_id=1, source_target_pairs={{0,4},{4,8},{8,12},{12,0},{1,5},{5,9},{9,13},{13,1},{2,6},{6,10},{... | collective-permute-start | bytes 589832 | tf_op jit(solution)/shard_map/ppermute | solution.py:160
  66.6 10.2 %copy-start.67 = (bf16[384,256]{1,0:T(8,128)(2,1)}, bf16[384,256]{1,0:T(8,128)(2,1)S(1)}, u32[]{:S(2)}) copy-start(bf16[384,256]{1,0:T(8,128)(2,1)S(1)} %collective-permute-done.11) | copy-start | bytes 589828
  66.6 8.8 %collective-permute-start.13 = (bf16[384,256]{1,0:T(8,128)(2,1)S(1)}, bf16[384,256]{1,0:T(8,128)(2,1)}, u32[]{:S(2)}, u32[]{:S(2)}) collective-permute-start(bf16[384,256]{1,0:T(8,128)(2,1)S(1)} %collective-permute-done.11), channel_id=1, source_target_pairs={{0,4},{4,8},{8,12},{12,0},{1,5},{5,9},{9,13},{13,1},{2,6},{6,10},{... | collective-permute-start | bytes 589832 | tf_op jit(solution)/shard_map/ppermute | solution.py:160
  67.7 13.3 %copy-start.71 = (f32[4]{0:T(128)S(1)}, f32[4]{0:T(128)}, u32[]{:S(2)}) copy-start(f32[4]{0:T(128)} %param.18) | copy-start | bytes 52
  67.7 33.9 %collective-permute-start.15 = (bf16[192,2048]{1,0:T(8,128)(2,1)}, bf16[192,2048]{1,0:T(8,128)(2,1)}, u32[]{:S(2)}, u32[]{:S(2)}) collective-permute-start(bf16[192,2048]{1,0:T(8,128)(2,1)} %get-tuple-element.15), channel_id=1, source_target_pairs={{0,2},{2,0},{1,3},{3,1},{4,6},{6,4},{5,7},{7,5},{8,10},{10,8},{9,1... | collective-permute-start | bytes 2359304 | tf_op jit(solution)/shard_map/ppermute | solution.py:220
  71.2 10.5 %collective-permute-start.14 = (bf16[384,256]{1,0:T(8,128)(2,1)}, bf16[384,256]{1,0:T(8,128)(2,1)}, u32[]{:S(2)}, u32[]{:S(2)}) collective-permute-start(bf16[384,256]{1,0:T(8,128)(2,1)} %collective-permute-done.12), channel_id=1, source_target_pairs={{0,4},{4,8},{8,12},{12,0},{1,5},{5,9},{9,13},{13,1},{2,6},{6,10},{... | collective-permute-start | bytes 589832 | tf_op jit(solution)/shard_map/ppermute | solution.py:160
  75.4 7.9 %collective-permute-start.22 = (bf16[384,256]{1,0:T(8,128)(2,1)}, bf16[384,256]{1,0:T(8,128)(2,1)}, u32[]{:S(2)}, u32[]{:S(2)}) collective-permute-start(bf16[384,256]{1,0:T(8,128)(2,1)} %collective-permute-done.13), channel_id=1, source_target_pairs={{0,4},{4,8},{8,12},{12,0},{1,5},{5,9},{9,13},{13,1},{2,6},{6,10},{... | collective-permute-start | bytes 589832 | tf_op jit(solution)/shard_map/ppermute | solution.py:160
  76.7 22.9 %collective-permute-start.17 = (bf16[192,2048]{1,0:T(8,128)(2,1)}, bf16[192,2048]{1,0:T(8,128)(2,1)}, u32[]{:S(2)}, u32[]{:S(2)}) collective-permute-start(bf16[192,2048]{1,0:T(8,128)(2,1)} %get-tuple-element.13), channel_id=1, source_target_pairs={{0,2},{2,0},{1,3},{3,1},{4,6},{6,4},{5,7},{7,5},{8,10},{10,8},{9,1... | collective-permute-start | bytes 2359304 | tf_op jit(solution)/shard_map/ppermute | solution.py:222
  81.0 8.4 %copy-start.12 = (bf16[1,1024,256]{2,1,0:T(8,128)(2,1)S(1)}, bf16[1,1024,256]{2,1,0:T(8,128)(2,1)}, u32[]{:S(2)}) copy-start(bf16[1,1024,256]{2,1,0:T(8,128)(2,1)} %param.12) | copy-start | bytes 1572868
  81.0 8.4 %copy-start.24 = (bf16[384,256]{1,0:T(8,128)(2,1)S(1)}, bf16[384,256]{1,0:T(8,128)(2,1)}, u32[]{:S(2)}) copy-start(bf16[384,256]{1,0:T(8,128)(2,1)} %copy-done.23) | copy-start | bytes 589828
  81.0 8.4 %copy-start.26 = (bf16[384,256]{1,0:T(8,128)(2,1)S(1)}, bf16[384,256]{1,0:T(8,128)(2,1)}, u32[]{:S(2)}) copy-start(bf16[384,256]{1,0:T(8,128)(2,1)} %copy-done.25) | copy-start | bytes 589828
  81.0 8.4 %copy-start.28 = (bf16[384,256]{1,0:T(8,128)(2,1)S(1)}, bf16[384,256]{1,0:T(8,128)(2,1)}, u32[]{:S(2)}) copy-start(bf16[384,256]{1,0:T(8,128)(2,1)} %copy-done.27) | copy-start | bytes 589828
  81.1 8.4 %copy-start.30 = (bf16[384,256]{1,0:T(8,128)(2,1)S(1)}, bf16[384,256]{1,0:T(8,128)(2,1)}, u32[]{:S(2)}) copy-start(bf16[384,256]{1,0:T(8,128)(2,1)} %copy-done.29) | copy-start | bytes 589828
  81.1 8.4 %copy-start.32 = (bf16[384,256]{1,0:T(8,128)(2,1)S(1)}, bf16[384,256]{1,0:T(8,128)(2,1)}, u32[]{:S(2)}) copy-start(bf16[384,256]{1,0:T(8,128)(2,1)} %copy-done.31) | copy-start | bytes 589828
  81.8 7.7 %collective-permute-start.23 = (bf16[384,256]{1,0:T(8,128)(2,1)}, bf16[384,256]{1,0:T(8,128)(2,1)S(1)}, u32[]{:S(2)}, u32[]{:S(2)}) collective-permute-start(bf16[384,256]{1,0:T(8,128)(2,1)} %collective-permute-done.14), channel_id=1, source_target_pairs={{0,4},{4,8},{8,12},{12,0},{1,5},{5,9},{9,13},{13,1},{2,6},{6,10},{... | collective-permute-start | bytes 589832 | tf_op jit(solution)/shard_map/ppermute | solution.py:160
  91.6 10.0 %copy-start.6 = (bf16[384,256]{1,0:T(8,128)(2,1)}, bf16[384,256]{1,0:T(8,128)(2,1)S(1)}, u32[]{:S(2)}) copy-start(bf16[384,256]{1,0:T(8,128)(2,1)S(1)} %get-tuple-element.30) | copy-start | bytes 589828
  91.6 10.0 %copy-start.8 = (bf16[384,256]{1,0:T(8,128)(2,1)}, bf16[384,256]{1,0:T(8,128)(2,1)S(1)}, u32[]{:S(2)}) copy-start(bf16[384,256]{1,0:T(8,128)(2,1)S(1)} %get-tuple-element.31) | copy-start | bytes 589828
  94.3 5.0 %collective-permute-start.18 = (bf16[64,2048]{1,0:T(8,128)(2,1)S(1)}, bf16[64,2048]{1,0:T(8,128)(2,1)S(1)}, u32[]{:S(2)}, u32[]{:S(2)}) collective-permute-start(bf16[64,2048]{1,0:T(8,128)(2,1)S(1)} %bitcast.143), channel_id=1, source_target_pairs={{0,1},{1,0},{2,3},{3,2},{4,5},{5,4},{6,7},{7,6},{8,9},{9,8},{10,11... | collective-permute-start | bytes 786440 | tf_op jit(solution)/shard_map/ppermute | solution.py:276
  95.2 37.8 %collective-permute-start.21 = (bf16[32,2048]{1,0:T(8,128)(2,1)}, bf16[32,2048]{1,0:T(8,128)(2,1)}, u32[]{:S(2)}, u32[]{:S(2)}) collective-permute-start(bf16[32,2048]{1,0:T(8,128)(2,1)} %get-tuple-element.45), channel_id=1, source_target_pairs={{0,2},{2,0},{1,3},{3,1},{4,6},{6,4},{5,7},{7,5},{8,10},{10,8},{9,1... | collective-permute-start | bytes 393224 | tf_op jit(solution)/shard_map/ppermute | solution.py:282
  97.1 4.5 %collective-permute-start.16 = (bf16[1024,256]{1,0:T(8,128)(2,1)S(1)}, bf16[1024,256]{1,0:T(8,128)(2,1)S(1)}, u32[]{:S(2)}, u32[]{:S(2)}) collective-permute-start(bf16[1024,256]{1,0:T(8,128)(2,1)S(1)} %pad_maximum_fusion.7), channel_id=1, source_target_pairs={{0,1},{1,0},{2,3},{3,2},{4,5},{5,4},{6,7},{7,6},{8,9},{9,8},{10,11... | collective-permute-start | bytes 1572872 | tf_op jit(solution)/shard_map/ppermute | solution.py:270
  104.5 15.9 %collective-permute-start.19 = (f32[384,384]{0,1:T(8,128)}, f32[384,384]{0,1:T(8,128)}, u32[]{:S(2)}, u32[]{:S(2)}) collective-permute-start(f32[384,384]{0,1:T(8,128)} %pad_maximum_fusion.6), channel_id=1, source_target_pairs={{0,2},{2,0},{1,3},{3,1},{4,6},{6,4},{5,7},{7,5},{8,10},{10,8},{9,1... | collective-permute-start | bytes 1769480 | tf_op jit(solution)/shard_map/ppermute | solution.py:302
  111.9 11.1 %copy-start.37 = (bf16[192,2048]{1,0:T(8,128)(2,1)S(1)}, bf16[192,2048]{1,0:T(8,128)(2,1)}, u32[]{:S(2)}) copy-start(bf16[192,2048]{1,0:T(8,128)(2,1)} %get-tuple-element.12) | copy-start | bytes 2359300
  124.7 2.7 %collective-permute-start.24 = (bf16[2,32,2048]{2,1,0:T(8,128)(2,1)S(1)}, bf16[2,32,2048]{2,1,0:T(8,128)(2,1)S(1)}, u32[]{:S(2)}, u32[]{:S(2)}) collective-permute-start(bf16[2,32,2048]{2,1,0:T(8,128)(2,1)S(1)} %fusion.31), channel_id=1, source_target_pairs={{0,1},{1,0},{2,3},{3,2},{4,5},{5,4},{6,7},{7,6},{8,9},{9,8},{10,11... | collective-permute-start | bytes 786440 | tf_op jit(solution)/shard_map/ppermute | solution.py:326
  126.8 9.5 %collective-permute-start.20 = (bf16[1024,256]{1,0:T(8,128)(2,1)S(1)}, bf16[1024,256]{1,0:T(8,128)(2,1)S(1)}, u32[]{:S(2)}, u32[]{:S(2)}) collective-permute-start(bf16[1024,256]{1,0:T(8,128)(2,1)S(1)} %dynamic-slice_convert_fusion), channel_id=1, source_target_pairs={{0,1},{1,0},{2,3},{3,2},{4,5},{5,4},{6,7},{7,6},{8,9},{9,8},{10,11... | collective-permute-start | bytes 1572872 | tf_op jit(solution)/shard_map/ppermute | solution.py:319
  127.4 5.5 %collective-permute-start.25 = (bf16[32,2048]{1,0:T(8,128)(2,1)S(1)}, bf16[32,2048]{1,0:T(8,128)(2,1)S(1)}, u32[]{:S(2)}, u32[]{:S(2)}) collective-permute-start(bf16[32,2048]{1,0:T(8,128)(2,1)S(1)} %fusion.37), channel_id=1, source_target_pairs={{0,2},{2,0},{1,3},{3,1},{4,6},{6,4},{5,7},{7,5},{8,10},{10,8},{9,1... | collective-permute-start | bytes 393224 | tf_op jit(solution)/shard_map/ppermute | solution.py:329
  (34 other events, 123.4 us)

commit v2 on v0

--- a/solution.py
+++ b/solution.py
@@ -1,6 +1,10 @@
+import functools
+
 import jax
 import jax.numpy as jnp
 from jax import lax
+from jax.experimental import pallas as pl
+from jax.experimental.pallas import tpu as pltpu
 from jax.sharding import PartitionSpec as P
 
 beta_one = 0.9
@@ -22,7 +26,7 @@
     return (updated.astype(jnp.bfloat16), first_new, second_new)
 
 
-def on_device(
+def on_device_any(
     tokens,
     grad_out,
     gate_up,
@@ -147,9 +151,591 @@
     )
 
 
+ANY = pl.BlockSpec(memory_space=pl.ANY)
+SMEM = pl.BlockSpec(memory_space=pltpu.SMEM)
+VMEM = pl.BlockSpec(memory_space=pltpu.VMEM)
+BIG = pltpu.CompilerParams(vmem_limit_bytes=48 * 1024 * 1024)
+STAGGER = 2
+W_CHUNKS = 4
+M_CHUNKS = 8
+CHUNKS = W_CHUNKS + M_CHUNKS
+
+
+def cost(flops, moved):
+    return pl.CostEstimate(flops=flops, bytes_accessed=moved, transcendentals=0)
+
+
+def after(value, *others):
+    return lax.optimization_barrier((value,) + others)[0]
+
+
+def pick(where, pieces, got):
+    def kernel(where_ref, got_ref, *refs):
+        own, out, sems = refs[: len(pieces)], refs[len(pieces)], refs[len(pieces) + 1]
+
+        @pl.when(where_ref[0] == 0)
+        def _():
+            copies = [
+                pltpu.make_async_copy(ref.at[index], out.at[pl.ds(*rows)], sems.at[n])
+                for n, (ref, (_, index, rows)) in enumerate(zip(own, pieces))
+            ]
+            for copy in copies:
+                copy.start()
+            for copy in copies:
+                copy.wait()
+
+    return pl.pallas_call(
+        kernel,
+        out_shape=jax.ShapeDtypeStruct(got.shape, got.dtype),
+        in_specs=[SMEM, ANY] + [ANY] * len(pieces),
+        out_specs=ANY,
+        scratch_shapes=[pltpu.SemaphoreType.DMA((len(pieces),))],
+        input_output_aliases={1: 0},
+        cost_estimate=cost(0, got.size * 2),
+        name="pick",
+    )(where, got, *[array for array, _, _ in pieces])
+
+
+def assemble(mode, own, pieces, out_shape):
+    hops = len(pieces[0][0])
+    flat = [array for arrays, _, _, _ in pieces for array in arrays]
+
+    def kernel(mode_ref, own_ref, *refs):
+        out, sems = refs[len(flat)], refs[len(flat) + 1]
+
+        @pl.when(mode_ref[0] == 0)
+        def _():
+            copy = pltpu.make_async_copy(own_ref, out, sems.at[0])
+            copy.start()
+            copy.wait()
+
+        for hop in range(hops):
+
+            @pl.when(mode_ref[0] == hop + 1)
+            def _():
+                copies = [
+                    pltpu.make_async_copy(
+                        refs[n * hops + hop].at[pl.ds(start, rows)],
+                        out.at[pl.ds(to, rows)],
+                        sems.at[n],
+                    )
+                    for n, (_, start, rows, to) in enumerate(pieces)
+                ]
+                for copy in copies:
+                    copy.start()
+                for copy in copies:
+                    copy.wait()
+
+    return pl.pallas_call(
+        kernel,
+        out_shape=jax.ShapeDtypeStruct(out_shape, own.dtype),
+        in_specs=[SMEM, ANY] + [ANY] * len(flat),
+        out_specs=ANY,
+        scratch_shapes=[pltpu.SemaphoreType.DMA((len(pieces),))],
+        cost_estimate=cost(0, own.size * 4),
+        name="assemble",
+    )(mode, own, *flat)
+
+
+def pack_moments(m1_gu, m2_gu, m1_dn, m2_dn):
+    _, rows_gu, cols = m1_gu.shape
+    _, rows_dn, width = m1_dn.shape
+    part = rows_gu // M_CHUNKS
+    blocks = width // cols // M_CHUNKS
+    each = part + blocks * rows_dn
+    steps = 4
+    per = M_CHUNKS // steps
+
+    def kernel(m1g, m2g, m1d, m2d, out):
+        for n in range(per):
+            for base, gu, dn in ((0, m1g, m1d), (each, m2g, m2d)):
+                out[n, base : base + part] = gu[0, n * part : (n + 1) * part].astype(out.dtype)
+                for b in range(blocks):
+                    at = (n * blocks + b) * cols
+                    to = base + part + b * rows_dn
+                    out[n, to : to + rows_dn] = dn[0, :, at : at + cols].astype(out.dtype)
+
+    gu_spec = pl.BlockSpec((1, per * part, cols), lambda i: (0, i, 0))
+    dn_spec = pl.BlockSpec((1, rows_dn, width // steps), lambda i: (0, 0, i))
+    return pl.pallas_call(
+        kernel,
+        grid=(steps,),
+        out_shape=jax.ShapeDtypeStruct((M_CHUNKS, 2 * each, cols), jnp.bfloat16),
+        in_specs=[gu_spec, gu_spec, dn_spec, dn_spec],
+        out_specs=pl.BlockSpec((per, 2 * each, cols), lambda i: (i, 0, 0)),
+        cost_estimate=cost(0, 12 * (m1_gu.size + m1_dn.size)),
+        name="pack_moments",
+    )(m1_gu, m2_gu, m1_dn, m2_dn)
+
+
+def swap_blocks(place, down, near, cols):
+    _, rows, width = down.shape
+    half = width // 2
+    blocks = half // cols
+
+    def kernel(place_ref, down_ref, near_ref, out, buf, sem):
+        chip = place_ref[0]
+        copy = pltpu.make_async_copy(
+            down_ref.at[0, :, pl.ds(pl.multiple_of(chip * half, half), half)], buf, sem
+        )
+        copy.start()
+        for b in range(blocks):
+            out[b, 1 - chip] = near_ref[:, b * cols : (b + 1) * cols]
+        copy.wait()
+        for b in range(blocks):
+            out[b, chip] = buf[:, b * cols : (b + 1) * cols]
+
+    return pl.pallas_call(
+        kernel,
+        out_shape=jax.ShapeDtypeStruct((blocks, 2, rows, cols), down.dtype),
+        in_specs=[SMEM, ANY, VMEM],
+        out_specs=VMEM,
+        scratch_shapes=[pltpu.VMEM((rows, half), down.dtype), pltpu.SemaphoreType.DMA],
+        cost_estimate=cost(0, down.size * 4),
+        name="swap_blocks",
+    )(place, down, near)
+
+
+def forward(place, tokens, tok_near, grad_out, up_near, gu, gu_mate, dn, dn_mate):
+    _, count, width = tokens.shape
+    half = width // 2
+    rows, cols = gu.shape
+    blocks, _, rows_dn, _ = dn.shape
+    units = 4 * rows_dn
+
+    def kernel(place_ref, tok_r, tokn_r, up_r, upn_r, gu_r, gum_r, dn_r, dnm_r, out, sent, tok, up, gub, dnb, sems):
+        chip, core = place_ref[0], place_ref[1]
+        mine = pl.ds(pl.multiple_of(chip * half, half), half)
+        first = pl.ds(pl.multiple_of(core * rows, rows), rows)
+        second = pl.ds(pl.multiple_of((1 - core) * rows, rows), rows)
+        pairs = [
+            (gu_r, gub.at[first]),
+            (gum_r, gub.at[second]),
+            (tok_r.at[0, :, mine], tok.at[pl.ds(0, count)]),
+            (tokn_r, tok.at[pl.ds(count, count)]),
+            (dn_r, dnb.at[:, :, core]),
+            (dnm_r, dnb.at[:, :, 1 - core]),
+            (up_r.at[0, :, mine], up.at[pl.ds(0, count)]),
+            (upn_r, up.at[pl.ds(count, count)]),
+        ]
+        copies = [pltpu.make_async_copy(a, b, sems.at[n]) for n, (a, b) in enumerate(pairs)]
+        for copy in copies:
+            copy.start()
+        for copy in copies[:4]:
+            copy.wait()
+        pre = jnp.dot(tok[...], gub[...], preferred_element_type=jnp.float32)
+        out[:, :cols] = pre
+        sent[:, :cols] = pre.astype(sent.dtype)
+        for copy in copies[4:]:
+            copy.wait()
+        dh = jnp.zeros((2 * count, units), jnp.float32)
+        for b in range(blocks):
+            dh += lax.dot_general(
+                up[:, b * cols : (b + 1) * cols],
+                dnb[b].reshape(units, cols),
+                (((1,), (1,)), ((), ())),
+                preferred_element_type=jnp.float32,
+            )
+        out[:, cols:] = dh
+        sent[:, cols:] = dh.astype(sent.dtype)
+
+    shape = (2 * count, cols + units)
+    return pl.pallas_call(
+        kernel,
+        out_shape=(
+            jax.ShapeDtypeStruct(shape, jnp.float32),
+            jax.ShapeDtypeStruct(shape, jnp.bfloat16),
+        ),
+        in_specs=[SMEM] + [ANY] * 8,
+        out_specs=(VMEM, VMEM),
+        scratch_shapes=[
+            pltpu.VMEM((2 * count, half), jnp.bfloat16),
+            pltpu.VMEM((2 * count, half), jnp.bfloat16),
+            pltpu.VMEM((half, cols), jnp.bfloat16),
+            pltpu.VMEM((blocks, 2, 2, rows_dn, cols), jnp.bfloat16),
+            pltpu.SemaphoreType.DMA((8,)),
+        ],
+        compiler_params=BIG,
+        cost_estimate=cost(4 * count * half * shape[1], 5 * 1024 * 1024),
+        name="forward",
+    )(place, tokens, tok_near, grad_out, up_near, gu, gu_mate, dn, dn_mate)
+
+
+def backward(place, part, near, tokens, tok_near, grad_out, up_near, rows, rows_dn):
+    _, count, width = tokens.shape
+    half = width // 2
+    units = 4 * rows_dn
+    cols = 2 * units
+    blocks = half // cols
+
+    def kernel(place_ref, part_r, near_r, tok_r, tokn_r, up_r, upn_r, g_own, g_mate, d_own, d_mate, tok, tokm, up, res, sems):
+        chip, core = place_ref[0], place_ref[1]
+        mine = pl.ds(pl.multiple_of(chip * half, half), half)
+        first = pl.multiple_of(core * rows, rows)
+        second = pl.multiple_of((1 - core) * rows, rows)
+        here = pl.multiple_of(chip * half, half)
+        pairs = [
+            (up_r.at[0, :, mine], up.at[pl.ds(0, count)]),
+            (upn_r, up.at[pl.ds(count, count)]),
+            (tok_r.at[0, :, pl.ds(here + second, rows)], tokm.at[pl.ds(0, count)]),
+            (tokn_r.at[:, pl.ds(second, rows)], tokm.at[pl.ds(count, count)]),
+            (tok_r.at[0, :, pl.ds(here + first, rows)], tok.at[pl.ds(0, count)]),
+            (tokn_r.at[:, pl.ds(first, rows)], tok.at[pl.ds(count, count)]),
+        ]
+        copies = [pltpu.make_async_copy(a, b, sems.at[n]) for n, (a, b) in enumerate(pairs)]
+        for copy in copies:
+            copy.start()
+        other = jnp.concatenate([near_r[count:], near_r[:count]]).astype(jnp.float32)
+        whole = part_r[...] + other
+        gate = whole[:, :units] * width ** (-0.5)
+        upper = whole[:, units:cols] * width ** (-0.5)
+        dhidden = whole[:, cols:] * units ** (-0.5)
+        sigma = jax.nn.sigmoid(gate)
+        active = gate * sigma
+        hidden = (active * upper).astype(jnp.bfloat16)
+        dgate = dhidden * upper * (sigma * (1.0 + gate * (1.0 - sigma)))
+        dupper = dhidden * active
+        dpre = (jnp.concatenate([dgate, dupper], axis=1) * width ** (-0.5)).astype(jnp.bfloat16)
+        over_tokens = (((0,), (0,)), ((), ()))
+        copies[0].wait()
+        copies[1].wait()
+        for b in range(blocks):
+            res[b] = lax.dot_general(
+                hidden, up[:, b * cols : (b + 1) * cols], over_tokens, preferred_element_type=jnp.float32
+            ) * units ** (-0.5)
+        for b in range(blocks):
+            for x in range(2):
+                base = x * 2 * rows_dn
+                d_own[b, x] = res[b, pl.ds(pl.multiple_of(base + core * rows_dn, rows_dn), rows_dn)]
+                d_mate[b, x] = res[
+                    b, pl.ds(pl.multiple_of(base + (1 - core) * rows_dn, rows_dn), rows_dn)
+                ].astype(d_mate.dtype)
+        copies[2].wait()
+        copies[3].wait()
+        g_mate[...] = lax.dot_general(
+            tokm[...], dpre, over_tokens, preferred_element_type=jnp.float32
+        ).astype(g_mate.dtype)
+        copies[4].wait()
+        copies[5].wait()
+        g_own[...] = lax.dot_general(tok[...], dpre, over_tokens, preferred_element_type=jnp.float32)
+
+    f32, bf16 = jnp.float32, jnp.bfloat16
+    dn_shape = (blocks, 2, rows_dn, cols)
+    return pl.pallas_call(
+        kernel,
+        out_shape=(
+            jax.ShapeDtypeStruct((rows, cols), f32),
+            jax.ShapeDtypeStruct((rows, cols), bf16),
+            jax.ShapeDtypeStruct(dn_shape, f32),
+            jax.ShapeDtypeStruct(dn_shape, bf16),
+        ),
+        in_specs=[SMEM, VMEM, VMEM] + [ANY] * 4,
+        out_specs=(VMEM,) * 4,
+        scratch_shapes=[
+            pltpu.VMEM((2 * count, rows), bf16),
+            pltpu.VMEM((2 * count, rows), bf16),
+            pltpu.VMEM((2 * count, half), bf16),
+            pltpu.VMEM((blocks, units, cols), f32),
+            pltpu.SemaphoreType.DMA((6,)),
+        ],
+        compiler_params=BIG,
+        cost_estimate=cost(4 * count * half * (cols + units), 6 * 1024 * 1024),
+        name="backward",
+    )(place, part, near, tokens, tok_near, grad_out, up_near)
+
+
+def update(place, rate, moments, came, gu, dn, dn_back, grads):
+    m1_gu, m2_gu, m1_dn, m2_dn = moments
+    _, rows_gu, cols = m1_gu.shape
+    _, rows_dn, width = m1_dn.shape
+    blocks = width // cols
+    half_blocks = blocks // 2
+    part = rows_gu // M_CHUNKS
+    per = blocks // M_CHUNKS
+    each = part + per * rows_dn
+    hops = len(came[0])
+    flat = [array for arrays in came for array in arrays]
+    f32, bf16 = jnp.float32, jnp.bfloat16
+
+    def kernel(place_ref, rate_ref, *refs):
+        m1g, m2g, m1d, m2d = refs[:4]
+        arrived = refs[4 : 4 + len(flat)]
+        gu_r, dn_r, back_r, go_r, gm_r, do_r, dm_r, gb_r = refs[4 + len(flat) : 12 + len(flat)]
+        ngu, ndn, n1g, n2g, n1d, n2d = refs[12 + len(flat) : 18 + len(flat)]
+        (bgu, bdn, bgo, bgm, bdo, bdm, bgb, gdn, own_g, own_d, moved, ogu, odn, o1g, o2g, o1d, o2d, sems, msems, osems) = refs[18 + len(flat) :]
+        chip, mode = place_ref[0], place_ref[2]
+        factor = rate_ref[0]
+        pairs = [
+            (gu_r, bgu),
+            (dn_r.at[:, chip], bdn.at[chip]),
+            (back_r, bdn.at[1 - chip]),
+            (go_r, bgo),
+            (gm_r, bgm),
+            (do_r.at[:, chip], bdo),
+            (dm_r.at[:, chip], bdm),
+            (gb_r, bgb),
+        ]
+        copies = [pltpu.make_async_copy(a, b, sems.at[n]) for n, (a, b) in enumerate(pairs)]
+        for copy in copies:
+            copy.start()
+
+        def own_copies(j):
+            g, d = pl.ds(j * part, part), pl.ds(j * per * cols, per * cols)
+            return [
+                pltpu.make_async_copy(m1g.at[0, g], own_g.at[0, g], msems.at[j, 0]),
+                pltpu.make_async_copy(m2g.at[0, g], own_g.at[1, g], msems.at[j, 1]),
+                pltpu.make_async_copy(m1d.at[0, :, d], own_d.at[0, :, d], msems.at[j, 2]),
+                pltpu.make_async_copy(m2d.at[0, :, d], own_d.at[1, :, d], msems.at[j, 3]),
+            ]
+
+        def moved_copy(j, hop):
+            return pltpu.make_async_copy(arrived[j * hops + hop], moved.at[j], msems.at[j, 0])
+
+        @pl.when(mode == 0)
+        def _():
+            for j in range(M_CHUNKS):
+                for copy in own_copies(j):
+                    copy.start()
+
+        for hop in range(hops):
+
+            @pl.when(mode == hop + 1)
+            def _():
+                for j in range(M_CHUNKS):
+                    moved_copy(j, hop).start()
+
+        for copy in copies:
+            copy.wait()
+        gdn[chip] = bdo[...] + bdm[...].astype(f32)
+        gdn[1 - chip] = bgb[...].astype(f32)
+
+        def step(weight, grad, first, second):
+            first_new = beta_one * first + (1.0 - beta_one) * grad
+            second_new = beta_two * second + (1.0 - beta_two) * grad * grad
+            wide = weight.astype(f32)
+            updated = wide - factor * (first_new / (jnp.sqrt(second_new) + epsilon) + decay * wide)
+            return updated.astype(bf16), first_new, second_new
+
+        outs = []
+        for j in range(M_CHUNKS):
+
+            @pl.when(mode == 0)
+            def _():
+                for copy in own_copies(j):
+                    copy.wait()
+
+            @pl.when(mode != 0)
+            def _():
+                moved_copy(j, 0).wait()
+
+            def moment(n, own, base, size):
+                there = moved[j, n * each + base : n * each + base + size].astype(f32)
+                return jnp.where(mode == 0, own, there)
+
+            g = slice(j * part, (j + 1) * part)
+            first = moment(0, own_g[0, g], 0, part)
+            second = moment(1, own_g[1, g], 0, part)
+            grad = bgo[g] + bgm[g].astype(f32)
+            ogu[g], o1g[g], o2g[g] = step(bgu[g], grad, first, second)
+            for i in range(per):
+                b = j * per + i
+                at = slice(b * cols, (b + 1) * cols)
+                base = part + i * rows_dn
+                first = moment(0, own_d[0, :, at], base, rows_dn)
+                second = moment(1, own_d[1, :, at], base, rows_dn)
+                h, n = divmod(b, half_blocks)
+                odn[:, at], o1d[:, at], o2d[:, at] = step(bdn[h, n], gdn[h, n], first, second)
+            gs, ds = pl.ds(j * part, part), pl.ds(j * per * cols, per * cols)
+            for n, (a, b) in enumerate(
+                (
+                    (ogu.at[gs], ngu.at[0, gs]),
+                    (o1g.at[gs], n1g.at[0, gs]),
+                    (o2g.at[gs], n2g.at[0, gs]),
+                    (odn.at[:, ds], ndn.at[0, :, ds]),
+                    (o1d.at[:, ds], n1d.at[0, :, ds]),
+                    (o2d.at[:, ds], n2d.at[0, :, ds]),
+                )
+            ):
+                copy = pltpu.make_async_copy(a, b, osems.at[j, n])
+                copy.start()
+                outs.append(copy)
+        for copy in outs:
+            copy.wait()
+
+    gu_shape, dn_shape = (rows_gu, cols), (rows_dn, width)
+    side = (half_blocks, rows_dn, cols)
+    shapes = [gu_shape, dn_shape, gu_shape, gu_shape, dn_shape, dn_shape]
+    types = [bf16, bf16, f32, f32, f32, f32]
+    return pl.pallas_call(
+        kernel,
+        out_shape=tuple(jax.ShapeDtypeStruct((1,) + s, t) for s, t in zip(shapes, types)),
+        in_specs=[SMEM, SMEM] + [ANY] * (12 + len(flat)),
+        out_specs=(ANY,) * 6,
+        scratch_shapes=[
+            pltpu.VMEM(gu_shape, bf16),
+            pltpu.VMEM((2,) + side, bf16),
+            pltpu.VMEM(gu_shape, f32),
+            pltpu.VMEM(gu_shape, bf16),
+            pltpu.VMEM(side, f32),
+            pltpu.VMEM(side, bf16),
+            pltpu.VMEM(side, bf16),
+            pltpu.VMEM((2,) + side, f32),
+            pltpu.VMEM((2,) + gu_shape, f32),
+            pltpu.VMEM((2,) + dn_shape, f32),
+            pltpu.VMEM((M_CHUNKS, 2 * each, cols), bf16),
+        ]
+        + [pltpu.VMEM(s, t) for s, t in zip(shapes, types)]
+        + [
+            pltpu.SemaphoreType.DMA((8,)),
+            pltpu.SemaphoreType.DMA((M_CHUNKS, 4)),
+            pltpu.SemaphoreType.DMA((M_CHUNKS, 6)),
+        ],
+        compiler_params=BIG,
+        cost_estimate=cost(0, 10 * 1024 * 1024),
+        name="update",
+    )(place, rate, m1_gu, m2_gu, m1_dn, m2_dn, *flat, gu, dn, dn_back, *grads)
+
+
+def on_device_four(
+    tokens,
+    grad_out,
+    gate_up,
+    down,
+    mom1_gate_up,
+    mom2_gate_up,
+    mom1_down,
+    mom2_down,
+    learning,
+    winner,
+):
+    bf16 = jnp.bfloat16
+    members = lax.axis_size("member")
+    member_index = lax.axis_index("member")
+    fsdp_index = lax.axis_index("fsdp")
+    chip = fsdp_index // 2
+    core = fsdp_index % 2
+    over_x = [(0, 2), (2, 0), (1, 3), (3, 1)]
+    over_core = [(0, 1), (1, 0), (2, 3), (3, 2)]
+    ring = [(i, (i + 1) % members) for i in range(members)]
+    half = tokens.shape[2] // 2
+    _, rows_gu, cols = gate_up.shape
+    rows_dn = down.shape[1]
+    rows_all = rows_gu + down.size // cols
+    w_rows = rows_all // W_CHUNKS
+
+    mine = winner[member_index]
+    others = jnp.where(winner != jnp.arange(members, dtype=winner.dtype), winner, -1)
+    source = jnp.maximum(jnp.max(others), 0)
+    distance = lax.rem(member_index - source + members, members)
+    mode = jnp.where(mine == member_index, 0, distance)
+    rate = learning[mine].reshape(1)
+    where = distance.astype(jnp.int32).reshape(1)
+    place = jnp.stack([chip, core, mode]).astype(jnp.int32)
+    mode = place[2:]
+
+    def theirs(x):
+        return lax.dynamic_slice_in_dim(x[0], (1 - chip) * half, half, axis=1)
+
+    sent = [gate_up[0, :w_rows], gate_up[0, w_rows : 2 * w_rows]]
+    got = [lax.ppermute(sent[0], "member", ring), lax.ppermute(sent[1], "member", ring)]
+    down_t, tokens_t, grad_out_t = (
+        after(down, *sent),
+        after(tokens, *sent),
+        after(grad_out, *sent),
+    )
+    dn_near = lax.ppermute(theirs(down_t), "fsdp", over_x)
+    tok_near = lax.ppermute(theirs(tokens_t), "fsdp", over_x)
+    up_near = lax.ppermute(theirs(grad_out_t), "fsdp", over_x)
+    dn_blocks = swap_blocks(place, down, dn_near, cols)
+    dn_rows = dn_blocks.reshape(-1, cols)
+    packed = pack_moments(after(mom1_gate_up, *sent), mom2_gate_up, mom1_down, mom2_down)
+
+    def pieces_of(c):
+        if c >= W_CHUNKS:
+            return [(packed, c - W_CHUNKS, (0, packed.shape[1]))]
+        low, high = c * w_rows, (c + 1) * w_rows
+        found = []
+        if low < rows_gu:
+            rows = min(high, rows_gu) - low
+            found.append((gate_up, (0, pl.ds(low, rows)), (0, rows)))
+        if high > rows_gu:
+            begin = max(low, rows_gu)
+            found.append((dn_rows, (pl.ds(begin - rows_gu, high - begin),), (begin - low, high - begin)))
+        return found
+
+    held = []
+    hops = members - 1
+    last = STAGGER * (hops - 1)
+
+    def versions(c):
+        return [held[c + STAGGER * hop] for hop in range(hops)]
+
+    gap = {}
+    cut = rows_gu // w_rows
+    for step in range(STAGGER, CHUNKS + last + STAGGER):
+        back = got[step - STAGGER]
+        if step < CHUNKS:
+            back = pick(where, pieces_of(step), back)
+        held.append(back)
+        if step < CHUNKS + last:
+            got.append(lax.ppermute(back, "member", ring))
+        ready = len(held) - 1 - last
+        if ready == cut:
+            gu_pieces = [(versions(c), 0, w_rows, c * w_rows) for c in range(cut)]
+            left = rows_gu - cut * w_rows
+            gu_pieces.append((versions(cut), 0, left, cut * w_rows))
+            gu = assemble(mode, gate_up[0], gu_pieces, gate_up.shape[1:])
+            gu_mate = lax.ppermute(gu, "fsdp", over_core)
+        if ready == W_CHUNKS - 1:
+            dn_pieces = [(versions(cut), left, w_rows - left, 0)]
+            for c in range(cut + 1, W_CHUNKS):
+                dn_pieces.append((versions(c), 0, w_rows, c * w_rows - rows_gu))
+            dn_r = assemble(mode, dn_rows, dn_pieces, dn_rows.shape)
+            dn_mate = lax.ppermute(dn_r, "fsdp", over_core)
+            dn = dn_r.reshape(dn_blocks.shape)
+            dn_there = lax.dynamic_index_in_dim(dn, 1 - chip, axis=1, keepdims=False)
+            dn_back = lax.ppermute(dn_there, "fsdp", over_x)
+        if ready == W_CHUNKS:
+            part, part_sent = forward(
+                place,
+                tokens,
+                tok_near,
+                grad_out,
+                up_near,
+                after(gu, back),
+                gu_mate,
+                dn,
+                dn_mate.reshape(dn_blocks.shape),
+            )
+            near = lax.ppermute(part_sent, "fsdp", over_x)
+        if step == CHUNKS + STAGGER:
+            g_own, g_mate, d_own, d_mate = backward(
+                place, part, after(near, back), tokens, tok_near, grad_out, up_near, rows_gu, rows_dn
+            )
+            g_got = lax.ppermute(g_mate, "fsdp", over_core)
+            d_got = lax.ppermute(d_mate, "fsdp", over_core)
+            d_there = (
+                lax.dynamic_index_in_dim(d_own, 1 - chip, axis=1, keepdims=False)
+                + lax.dynamic_index_in_dim(d_got, 1 - chip, axis=1, keepdims=False)
+            ).astype(bf16)
+            d_back = lax.ppermute(d_there, "fsdp", over_x)
+
+    return update(
+        place,
+        rate,
+        (mom1_gate_up, mom2_gate_up, mom1_down, mom2_down),
+        [versions(c) for c in range(W_CHUNKS, CHUNKS)],
+        gu,
+        dn,
+        dn_back,
+        (g_own, g_got, d_own, d_got, d_back),
+    )
+
+
 def solution(mesh):
+    small = mesh.shape["member"] == 4 and mesh.shape["fsdp"] == 4
     return jax.shard_map(
-        on_device,
+        on_device_four if small else on_device_any,
         mesh=mesh,
         in_specs=(
             P(("groups", "member"), "fsdp", None),

time: 407 us -> 193 us (0.47)
  waiting for transfers between devices: 258 us -> 89.1 us
  Pallas kernels: 0 us -> 47 us
  local copies, waits for them, and re-layouts: 60.8 us -> 20.9 us
  other arithmetic: 38.8 us -> 3.68 us
  between operations: 17.6 us -> 3.97 us
  matrix products: 8.17 us -> 0 us
  starting transfers between devices: 19.2 us -> 24.5 us
    psum x4 -> x0, waiting for transfers between devices: 189 us -> none  [spread(): return lax.psum(block, axis)]
    ppermute x0 -> x26, waiting for transfers between devices: none -> 89.1 us  [the longest x14 89.1 us: on_device_four(): got.append(lax.ppermute(back, 'member', ring))]
    pallas_call x0 -> x17, Pallas kernels: none -> 47 us  [the longest x2 26.1 us: assemble(): pl.pallas_call(kernel, out_shape=jax.ShapeDtypeStruct(out_shape, own.dtyp...]
    reduce_scatter x2 -> x0, waiting for transfers between devices: 34.8 us -> none  [the longest x1 30.8 us: on_device(): lax.psum_scatter(lax.dot_general(columns, dpreact, (((0,), (0,)), ((), ()...]
    all_to_all x4 -> x0, waiting for transfers between devices: 34.3 us -> none  [the longest x1 13.5 us: on_device(): lax.all_to_all(jnp.take(lax.all_to_all(joined(mom1_gate_up[0], mom1_down[...]
    ppermute x0 -> x26, starting transfers between devices: none -> 24.5 us  [the longest x14 12.9 us: on_device_four(): got.append(lax.ppermute(back, 'member', ring))]
    unnamed x61 -> x66, local copies, waits for them, and re-layouts: 32 us -> 12 us
    all_to_all x4 -> x0, starting transfers between devices: 18.5 us -> none  [the longest x1 6.45 us: on_device(): lax.all_to_all(joined(mom2_gate_up[0], mom2_down[0]).astype(jnp.bfloat16)...]
  transfers between devices with their start and end apart: 12 -> 26, of which waited for: 9 -> 13; matrix products, arithmetic and copies ran while one was open for 22% -> 6% of each run, Pallas kernels for 0% -> 22%
where the time goes in v2:
time: 193 us; the launch traced here: 189 us
  waiting for transfers between devices  89.1 us (46%)
  Pallas kernels  47 us (24%)
  starting transfers between devices  24.5 us (13%)
  local copies, waits for them, and re-layouts  20.9 us (11%)
  between operations  3.97 us (2%)
  other arithmetic  3.68 us (2%)
    ppermute x14, waiting for transfers between devices, on_device_four(): got.append(lax.ppermute(back, 'member', ring))  89.1 us
    pallas_call x2, Pallas kernels, assemble(): pl.pallas_call(kernel, out_shape=jax.ShapeDtypeStruct(out_shape, own.dtyp...  26.1 us
    ppermute x14, starting transfers between devices, on_device_four(): got.append(lax.ppermute(back, 'member', ring))  12.9 us
    unnamed x66, local copies, waits for them, and re-layouts  12 us
    pallas_call x1, Pallas kernels, update(): pl.pallas_call(kernel, out_shape=tuple((jax.ShapeDtypeStruct((1,) + s, t)...  6.02 us
    pallas_call x1, Pallas kernels, forward(): pl.pallas_call(kernel, out_shape=(jax.ShapeDtypeStruct(shape, jnp.float32...  4.6 us
  transfers between devices with their start and end apart: 26, of which 13 were waited for; matrix products, arithmetic and copies ran while one was open for 6% of the time, Pallas kernels for 22%

profile of v2, /device:TPU:0, one launch (start us, length us, event | category | flops | bytes accessed | tf_op | source)
XLA Modules:
  0.0 189.1 jit_solution(5620515604014045700)
XLA Ops:
  0.6 1.8 slice_bitcast_fusion
  2.5 3.0 %collective-permute-start.6 = (bf16[384,256]{1,0:T(8,128)(2,1)}, bf16[384,256]{1,0:T(8,128)(2,1)}, u32[]{:S(2)}, u32[]{:S(2)}) collective-permute-start(bf16[384,256]{1,0:T(8,128)(2,1)} %get-tuple-element.30), channel_id=1, source_target_pairs={{0,4},{4,8},{8,12},{12,0},{1,5},{5,9},{9,13},{13,1},{2,6},{6,10},{... | collective-permute-start | bytes 589832 | tf_op jit(solution)/shard_map/ppermute | solution.py:640
  5.5 1.6 collective-permute-start
  7.1 0.9 dynamic-slice_bitcast_fusion.3
  8.0 1.6 collective-permute-start.1
  9.6 1.3 fusion.1
  11.5 1.2 dynamic_slice.32
  13.3 0.7 pad_add_fusion.place_ref
  13.9 0.7 copy-done.31
  14.6 2.5 %swap_blocks.1 = bf16[8,2,32,256]{3,2,1,0:T(8,128)(2,1)} custom-call(s32[3]{0:T(128)} %pad_add_fusion.place_ref, bf16[1,32,4096]{2,1,0:T(8,128)(2,1)} %down_ref.1, bf16[32,2048]{1,0:T(8,128)(2,1)} %copy-done.31), custom_call_target="tpu_custom_call" | custom-call | bytes 524288 | tf_op jit(solution)/shard_map/swap_blocks/pallas_call | solution.py:288
  17.2 0.7 copy-done.29
  17.9 1.6 collective-permute-start.2
  19.5 0.9 dynamic-slice_bitcast_fusion
  20.4 0.6 collective-permute-start.19
  21.0 3.8 %pack_moments.1.refs_0_ = bf16[8,384,256]{2,1,0:T(8,128)(2,1)} custom-call(f32[1,1024,256]{2,1,0:T(8,128)} %refs_0_.3, f32[1,1024,256]{2,1,0:T(8,128)} %refs_1_.1, f32[1,32,4096]{2,1,0:T(8,128)} %refs_2_.1, f32[1,32,4096]{2,1,0:T(8,128)} %refs_3_.1), custom_call_target="tpu_custom_call" | custom-call | bytes 4718592 | tf_op jit(solution)/shard_map/pack_moments/pallas_call | solution.py:260
  24.9 0.4 collective-permute-start.7
  25.3 6.2 %collective-permute-done.2.got_ref = bf16[384,256]{1,0:T(8,128)(2,1)S(1)} collective-permute-done((bf16[384,256]{1,0:T(8,128)(2,1)}, bf16[384,256]{1,0:T(8,128)(2,1)S(1)}, u32[]{:S(2)}, u32[]{:S(2)}) %collective-permute-start.2) | collective-permute-done | bytes 196640 | tf_op jit(solution)/shard_map/ppermute | solution.py:681
  31.5 0.7 copy-done.27
  32.2 2.4 %collective-permute-start.3 = (bf16[384,256]{1,0:T(8,128)(2,1)}, bf16[384,256]{1,0:T(8,128)(2,1)S(1)}, u32[]{:S(2)}, u32[]{:S(2)}) collective-permute-start(bf16[384,256]{1,0:T(8,128)(2,1)} %pick.11.refs_1_.refs_6_.refs_0_), channel_id=1, source_target_pairs={{0,4},{4,8},{8,12},{12,0},{1,5},{5,9},{9,13},{13,1},{2,6},{6,10},{... | collective-permute-start | bytes 589832 | tf_op jit(solution)/shard_map/ppermute | solution.py:681
  34.6 0.9 dynamic-slice_bitcast_fusion.1
  35.6 1.4 collective-permute-start.18
  36.9 6.9 %collective-permute-done.7.got_ref = bf16[384,256]{1,0:T(8,128)(2,1)S(1)} collective-permute-done((bf16[384,256]{1,0:T(8,128)(2,1)}, bf16[384,256]{1,0:T(8,128)(2,1)S(1)}, u32[]{:S(2)}, u32[]{:S(2)}) %collective-permute-start.7) | collective-permute-done | bytes 196640 | tf_op jit(solution)/shard_map/ppermute | solution.py:681
  43.8 0.7 copy-done.28
  44.5 0.3 collective-permute-start.8
  44.8 6.9 %collective-permute-done.3.got_ref = bf16[384,256]{1,0:T(8,128)(2,1)S(1)} collective-permute-done((bf16[384,256]{1,0:T(8,128)(2,1)}, bf16[384,256]{1,0:T(8,128)(2,1)S(1)}, u32[]{:S(2)}, u32[]{:S(2)}) %collective-permute-start.3) | collective-permute-done | bytes 196640 | tf_op jit(solution)/shard_map/ppermute | solution.py:681
  51.6 0.7 copy-done.1
  52.6 9.1 %collective-permute-done.8.got_ref = bf16[384,256]{1,0:T(8,128)(2,1)S(1)} collective-permute-done((bf16[384,256]{1,0:T(8,128)(2,1)}, bf16[384,256]{1,0:T(8,128)(2,1)S(1)}, u32[]{:S(2)}, u32[]{:S(2)}) %collective-permute-start.8) | collective-permute-done | bytes 196640 | tf_op jit(solution)/shard_map/ppermute | solution.py:681
  61.6 0.7 copy-done.7
  62.3 7.1 %collective-permute-done.4.got_ref = bf16[384,256]{1,0:T(8,128)(2,1)S(1)} collective-permute-done((bf16[384,256]{1,0:T(8,128)(2,1)}, bf16[384,256]{1,0:T(8,128)(2,1)S(1)}, u32[]{:S(2)}, u32[]{:S(2)}) %collective-permute-start.4) | collective-permute-done | bytes 196640 | tf_op jit(solution)/shard_map/ppermute | solution.py:681
  69.5 0.7 copy-done.3
  70.2 17.0 %assemble.2.gu_r.refs_28_ = bf16[1024,256]{1,0:T(8,128)(2,1)} custom-call(s32[1]{0:T(128)} %bitcast.3.mode_ref, bf16[1024,256]{1,0:T(8,128)(2,1)} %bitcast.29, bf16[384,256]{1,0:T(8,128)(2,1)} %pick.10.refs_0_, bf16[384,256]{1,0:T(8,128)(2,1)} %pick.11.refs_1_.refs_6_.refs_0_, bf16[384,256]{1,0:T(8,128)(2,1)} %pick.12.refs_2_.refs_7_.refs_1_.refs_4_, ...), custom_call_target="tpu_custom_call" | custom-call | bytes 1048576 | tf_op jit(solution)/shard_map/assemble/pallas_call | solution.py:229
  87.3 16.5 %collective-permute-done.9.got_ref = bf16[384,256]{1,0:T(8,128)(2,1)S(1)} collective-permute-done((bf16[384,256]{1,0:T(8,128)(2,1)S(1)}, bf16[384,256]{1,0:T(8,128)(2,1)S(1)}, u32[]{:S(2)}, u32[]{:S(2)}) %collective-permute-start.9) | collective-permute-done | bytes 196640 | tf_op jit(solution)/shard_map/ppermute | solution.py:681
  103.8 0.7 copy-done.10
  104.5 9.1 %assemble.3 = bf16[512,256]{1,0:T(8,128)(2,1)} custom-call(s32[1]{0:T(128)} %bitcast.3.mode_ref, bf16[512,256]{1,0:T(8,128)(2,1)} %bitcast.28, bf16[384,256]{1,0:T(8,128)(2,1)} %pick.11.refs_1_.refs_6_.refs_0_, bf16[384,256]{1,0:T(8,128)(2,1)} %pick.12.refs_2_.refs_7_.refs_1_.refs_4_, bf16[384,256]{1,0:T(8,128)(2,1)} %pick.13.refs_8_.refs_2_.refs_5_.refs_10_, ...), custom_call_target="tpu_custom_call" | custom-call | bytes 524288 | tf_op jit(solution)/shard_map/assemble/pallas_call | solution.py:229
  113.8 14.3 %collective-permute-done.5.got_ref = bf16[384,256]{1,0:T(8,128)(2,1)S(1)} collective-permute-done((bf16[384,256]{1,0:T(8,128)(2,1)S(1)}, bf16[384,256]{1,0:T(8,128)(2,1)S(1)}, u32[]{:S(2)}, u32[]{:S(2)}) %collective-permute-start.5) | collective-permute-done | bytes 196640 | tf_op jit(solution)/shard_map/ppermute | solution.py:681
  128.0 0.7 copy-done.14
  128.9 4.6 %forward.1 = (f32[384,384]{1,0:T(8,128)S(1)}, bf16[384,384]{1,0:T(8,128)(2,1)}) custom-call(s32[3]{0:T(128)S(1)} %copy-done.25, bf16[1,192,4096]{2,1,0:T(8,128)(2,1)S(1)} %copy-done, bf16[192,2048]{1,0:T(8,128)(2,1)} %collective-permute-done.18.tokn_r, bf16[1,192,4096]{2,1,0:T(8,128)(2,1)} %up_r.3, bf16[192,2048]{1,0:T(8,128)(2,1)S(1)} %collective-permute-done.19.upn_r, ...), custom_call_target="tpu_custom_call" | custom-call | flops 603979776 | bytes 5242880 | tf_op jit(solution)/shard_map/forward/pallas_call | solution.py:343
  133.5 0.8 copy-done.23
  134.3 0.7 collective-permute-start.22
  135.0 0.4 collective-permute-start.10
  135.3 7.3 %collective-permute-done.11.refs_12_.refs_17_.refs_22_ = bf16[384,256]{1,0:T(8,128)(2,1)} collective-permute-done((bf16[384,256]{1,0:T(8,128)(2,1)}, bf16[384,256]{1,0:T(8,128)(2,1)}, u32[]{:S(2)}, u32[]{:S(2)}) %collective-permute-start.11) | collective-permute-done | bytes 196640 | tf_op jit(solution)/shard_map/ppermute | solution.py:681
  142.6 2.3 %collective-permute-start.13 = (bf16[384,256]{1,0:T(8,128)(2,1)}, bf16[384,256]{1,0:T(8,128)(2,1)S(1)}, u32[]{:S(2)}, u32[]{:S(2)}) collective-permute-start(bf16[384,256]{1,0:T(8,128)(2,1)} %collective-permute-done.11.refs_12_.refs_17_.refs_22_), channel_id=1, source_target_pairs={{0,4},{4,8},{8,12},{12,0},{1,5},{5,9},{9,13},{13,1},{2,6},{6,10},{... | collective-permute-start | bytes 589832 | tf_op jit(solution)/shard_map/ppermute | solution.py:681
  144.9 4.7 %collective-permute-done.10.got_ref = bf16[384,256]{1,0:T(8,128)(2,1)S(1)} collective-permute-done((bf16[384,256]{1,0:T(8,128)(2,1)S(1)}, bf16[384,256]{1,0:T(8,128)(2,1)S(1)}, u32[]{:S(2)}, u32[]{:S(2)}) %collective-permute-start.10) | collective-permute-done | bytes 196640 | tf_op jit(solution)/shard_map/ppermute | solution.py:681
  149.6 0.7 copy-done.12
  150.3 0.7 collective-permute-start.12
  151.0 1.4 collective-permute-done.13.refs_18_.refs_23_
  152.4 0.7 copy-done.21
  153.1 3.8 %backward.1 = (f32[1024,256]{1,0:T(8,128)S(1)}, bf16[1024,256]{1,0:T(8,128)(2,1)}, f32[8,2,32,256]{3,2,1,0:T(8,128)S(1)}, bf16[8,2,32,256]{3,2,1,0:T(8,128)(2,1)S(1)}) custom-call(s32[3]{0:T(128)S(1)} %copy-done.25, f32[384,384]{1,0:T(8,128)S(1)} %copy-done.24, bf16[384,384]{1,0:T(8,128)(2,1)S(1)} %collective-permute-done.22.near_r, ...), custom_call_target="tpu_custom_call" | custom-call | flops 603979776 | bytes 6291456 | tf_op jit(solution)/shard_map/backward/pallas_call | solution.py:424
  156.9 0.8 copy-done.18
  157.7 1.0 copy-done.20
  158.7 0.7 copy.26
  159.5 3.9 %collective-permute-done.12.refs_15_.refs_20_.refs_25_ = bf16[384,256]{1,0:T(8,128)(2,1)} collective-permute-done((bf16[384,256]{1,0:T(8,128)(2,1)}, bf16[384,256]{1,0:T(8,128)(2,1)}, u32[]{:S(2)}, u32[]{:S(2)}) %collective-permute-start.12) | collective-permute-done | bytes 196640 | tf_op jit(solution)/shard_map/ppermute | solution.py:681
  163.4 0.7 dynamic-slice_bitcast_fusion.2
  164.1 1.3 collective-permute-start.17
  165.4 4.4 %collective-permute-start.15 = (bf16[384,256]{1,0:T(8,128)(2,1)}, bf16[384,256]{1,0:T(8,128)(2,1)}, u32[]{:S(2)}, u32[]{:S(2)}) collective-permute-start(bf16[384,256]{1,0:T(8,128)(2,1)} %copy-done.21), channel_id=1, source_target_pairs={{0,4},{4,8},{8,12},{12,0},{1,5},{5,9},{9,13},{13,1},{2,6},{6,10},{... | collective-permute-start | bytes 589832 | tf_op jit(solution)/shard_map/ppermute | solution.py:681
  169.8 3.4 %collective-permute-done.14.refs_21_.refs_26_ = bf16[384,256]{1,0:T(8,128)(2,1)} collective-permute-done((bf16[384,256]{1,0:T(8,128)(2,1)}, bf16[384,256]{1,0:T(8,128)(2,1)}, u32[]{:S(2)}, u32[]{:S(2)}) %collective-permute-start.14) | collective-permute-done | bytes 196640 | tf_op jit(solution)/shard_map/ppermute | solution.py:681
  173.3 1.7 fusion
  175.0 1.3 collective-permute-start.25
  178.0 0.7 dynamic_slice.33.rate_ref
  178.7 1.0 copy.28.refs_34_
  179.7 1.4 collective-permute-done.16.refs_27_
  181.1 1.0 copy-done.19
  182.2 0.9 copy-done.22
  183.1 6.0 %update.1 = (bf16[1,1024,256]{2,1,0:T(8,128)(2,1)}, bf16[1,32,4096]{2,1,0:T(8,128)(2,1)}, f32[1,1024,256]{2,1,0:T(8,128)}, f32[1,1024,256]{2,1,0:T(8,128)}, f32[...) custom-call(s32[3]{0:T(128)S(1)} %copy-done.25, f32[1]{0:T(128)} %dynamic_slice.33.rate_ref, f32[1,1024,256]{2,1,0:T(8,128)} %refs_0_.3, ...), custom_call_target="tpu_custom_call" | custom-call | bytes 10485760 | tf_op jit(solution)/shard_map/update/pallas_call | solution.py:569
  (83 shorter events, 0.8 us)
Async XLA Ops:
  0.6 18.9 %copy-start.26 = (bf16[1,192,4096]{2,1,0:T(8,128)(2,1)S(1)}, bf16[1,192,4096]{2,1,0:T(8,128)(2,1)}, u32[]{:S(2)}) copy-start(bf16[1,192,4096]{2,1,0:T(8,128)(2,1)} %up_r.3) | copy-start | bytes 4718596
  2.5 22.4 %collective-permute-start.6 = (bf16[384,256]{1,0:T(8,128)(2,1)}, bf16[384,256]{1,0:T(8,128)(2,1)}, u32[]{:S(2)}, u32[]{:S(2)}) collective-permute-start(bf16[384,256]{1,0:T(8,128)(2,1)} %get-tuple-element.30), channel_id=1, source_target_pairs={{0,4},{4,8},{8,12},{12,0},{1,5},{5,9},{9,13},{13,1},{2,6},{6,10},{... | collective-permute-start | bytes 589832 | tf_op jit(solution)/shard_map/ppermute | solution.py:640
  5.5 11.6 %collective-permute-start = (bf16[384,256]{1,0:T(8,128)(2,1)S(1)}, bf16[384,256]{1,0:T(8,128)(2,1)S(1)}, u32[]{:S(2)}, u32[]{:S(2)}) collective-permute-start(bf16[384,256]{1,0:T(8,128)(2,1)S(1)} %get-tuple-element.31), channel_id=1, source_target_pairs={{0,4},{4,8},{8,12},{12,0},{1,5},{5,9},{9,13},{13,1},{2,6},{6,10},{... | collective-permute-start | bytes 589832 | tf_op jit(solution)/shard_map/ppermute | solution.py:640
  8.0 5.9 %collective-permute-start.1 = (bf16[32,2048]{1,0:T(8,128)(2,1)S(1)}, bf16[32,2048]{1,0:T(8,128)(2,1)S(1)}, u32[]{:S(2)}, u32[]{:S(2)}) collective-permute-start(bf16[32,2048]{1,0:T(8,128)(2,1)S(1)} %dynamic-slice_bitcast_fusion.3), channel_id=1, source_target_pairs={{0,2},{2,0},{1,3},{3,1},{4,6},{6,4},{5,7},{7,5},{8,10},{10,8},{9,1... | collective-permute-start | bytes 393224 | tf_op jit(solution)/shard_map/ppermute | solution.py:646
  13.9 0.7 copy-start.31
  17.2 0.7 copy-start.29
  17.9 13.6 %collective-permute-start.2 = (bf16[384,256]{1,0:T(8,128)(2,1)}, bf16[384,256]{1,0:T(8,128)(2,1)S(1)}, u32[]{:S(2)}, u32[]{:S(2)}) collective-permute-start(bf16[384,256]{1,0:T(8,128)(2,1)} %pick.10.refs_0_), channel_id=1, source_target_pairs={{0,4},{4,8},{8,12},{12,0},{1,5},{5,9},{9,13},{13,1},{2,6},{6,10},{... | collective-permute-start | bytes 589832 | tf_op jit(solution)/shard_map/ppermute | solution.py:681
  20.4 108.4 %collective-permute-start.19 = (bf16[192,2048]{1,0:T(8,128)(2,1)}, bf16[192,2048]{1,0:T(8,128)(2,1)S(1)}, u32[]{:S(2)}, u32[]{:S(2)}) collective-permute-start(bf16[192,2048]{1,0:T(8,128)(2,1)} %dynamic-slice_bitcast_fusion), channel_id=1, source_target_pairs={{0,2},{2,0},{1,3},{3,1},{4,6},{6,4},{5,7},{7,5},{8,10},{10,8},{9,1... | collective-permute-start | bytes 2359304 | tf_op jit(solution)/shard_map/ppermute | solution.py:648
  24.9 9.8 %copy-start = (bf16[1,192,4096]{2,1,0:T(8,128)(2,1)S(1)}, bf16[1,192,4096]{2,1,0:T(8,128)(2,1)}, u32[]{:S(2)}) copy-start(bf16[1,192,4096]{2,1,0:T(8,128)(2,1)} %tok_r.3) | copy-start | bytes 4718596
  24.9 18.9 %collective-permute-start.7 = (bf16[384,256]{1,0:T(8,128)(2,1)}, bf16[384,256]{1,0:T(8,128)(2,1)S(1)}, u32[]{:S(2)}, u32[]{:S(2)}) collective-permute-start(bf16[384,256]{1,0:T(8,128)(2,1)} %pick.15.refs_3_), channel_id=1, source_target_pairs={{0,4},{4,8},{8,12},{12,0},{1,5},{5,9},{9,13},{13,1},{2,6},{6,10},{... | collective-permute-start | bytes 589832 | tf_op jit(solution)/shard_map/ppermute | solution.py:681
  31.5 0.7 copy-start.27
  32.2 19.4 %collective-permute-start.3 = (bf16[384,256]{1,0:T(8,128)(2,1)}, bf16[384,256]{1,0:T(8,128)(2,1)S(1)}, u32[]{:S(2)}, u32[]{:S(2)}) collective-permute-start(bf16[384,256]{1,0:T(8,128)(2,1)} %pick.11.refs_1_.refs_6_.refs_0_), channel_id=1, source_target_pairs={{0,4},{4,8},{8,12},{12,0},{1,5},{5,9},{9,13},{13,1},{2,6},{6,10},{... | collective-permute-start | bytes 589832 | tf_op jit(solution)/shard_map/ppermute | solution.py:681
  35.6 93.2 %collective-permute-start.18 = (bf16[192,2048]{1,0:T(8,128)(2,1)}, bf16[192,2048]{1,0:T(8,128)(2,1)}, u32[]{:S(2)}, u32[]{:S(2)}) collective-permute-start(bf16[192,2048]{1,0:T(8,128)(2,1)} %dynamic-slice_bitcast_fusion.1), channel_id=1, source_target_pairs={{0,2},{2,0},{1,3},{3,1},{4,6},{6,4},{5,7},{7,5},{8,10},{10,8},{9,1... | collective-permute-start | bytes 2359304 | tf_op jit(solution)/shard_map/ppermute | solution.py:647
  43.8 0.7 copy-start.28
  44.5 17.2 %collective-permute-start.8 = (bf16[384,256]{1,0:T(8,128)(2,1)}, bf16[384,256]{1,0:T(8,128)(2,1)S(1)}, u32[]{:S(2)}, u32[]{:S(2)}) collective-permute-start(bf16[384,256]{1,0:T(8,128)(2,1)} %pick.16.refs_4_.refs_3_), channel_id=1, source_target_pairs={{0,4},{4,8},{8,12},{12,0},{1,5},{5,9},{9,13},{13,1},{2,6},{6,10},{... | collective-permute-start | bytes 589832 | tf_op jit(solution)/shard_map/ppermute | solution.py:681
  51.6 0.7 copy-start.1
  52.3 17.1 %collective-permute-start.4 = (bf16[384,256]{1,0:T(8,128)(2,1)}, bf16[384,256]{1,0:T(8,128)(2,1)S(1)}, u32[]{:S(2)}, u32[]{:S(2)}) collective-permute-start(bf16[384,256]{1,0:T(8,128)(2,1)} %pick.12.refs_2_.refs_7_.refs_1_.refs_4_), channel_id=1, source_target_pairs={{0,4},{4,8},{8,12},{12,0},{1,5},{5,9},{9,13},{13,1},{2,6},{6,10},{... | collective-permute-start | bytes 589832 | tf_op jit(solution)/shard_map/ppermute | solution.py:681
  61.6 0.7 copy-start.7
  69.5 0.7 copy-start.3
  70.1 17.1 %copy-start.8 = (bf16[384,256]{1,0:T(8,128)(2,1)S(1)}, bf16[384,256]{1,0:T(8,128)(2,1)}, u32[]{:S(2)}) copy-start(bf16[384,256]{1,0:T(8,128)(2,1)} %pick.17.refs_5_.refs_4_.refs_7_) | copy-start | bytes 589828
  87.2 26.5 %copy-start.4 = (bf16[384,256]{1,0:T(8,128)(2,1)S(1)}, bf16[384,256]{1,0:T(8,128)(2,1)}, u32[]{:S(2)}) copy-start(bf16[384,256]{1,0:T(8,128)(2,1)} %pick.13.refs_8_.refs_2_.refs_5_.refs_10_) | copy-start | bytes 589828
  87.2 41.7 %collective-permute-start.20 = (bf16[1024,256]{1,0:T(8,128)(2,1)}, bf16[1024,256]{1,0:T(8,128)(2,1)}, u32[]{:S(2)}, u32[]{:S(2)}) collective-permute-start(bf16[1024,256]{1,0:T(8,128)(2,1)} %assemble.2.gu_r.refs_28_), channel_id=1, source_target_pairs={{0,1},{1,0},{2,3},{3,2},{4,5},{5,4},{6,7},{7,6},{8,9},{9,8},{10,11... | collective-permute-start | bytes 1572872 | tf_op jit(solution)/shard_map/ppermute | solution.py:688
  87.3 16.5 %collective-permute-start.9 = (bf16[384,256]{1,0:T(8,128)(2,1)S(1)}, bf16[384,256]{1,0:T(8,128)(2,1)S(1)}, u32[]{:S(2)}, u32[]{:S(2)}) collective-permute-start(bf16[384,256]{1,0:T(8,128)(2,1)S(1)} %copy-done.8), channel_id=1, source_target_pairs={{0,4},{4,8},{8,12},{12,0},{1,5},{5,9},{9,13},{13,1},{2,6},{6,10},{... | collective-permute-start | bytes 589832 | tf_op jit(solution)/shard_map/ppermute | solution.py:681
  103.8 0.7 copy-start.10
  104.5 24.4 %copy-start.5 = (bf16[1024,256]{1,0:T(8,128)(2,1)S(1)}, bf16[1024,256]{1,0:T(8,128)(2,1)}, u32[]{:S(2)}) copy-start(bf16[1024,256]{1,0:T(8,128)(2,1)} %assemble.2.gu_r.refs_28_) | copy-start | bytes 1572868
  104.5 24.4 %copy-start.25 = (s32[3]{0:T(128)S(1)}, s32[3]{0:T(128)}, u32[]{:S(2)}) copy-start(s32[3]{0:T(128)} %pad_add_fusion.place_ref) | copy-start | bytes 40
  113.6 15.3 %copy-start.6 = (bf16[512,256]{1,0:T(8,128)(2,1)S(1)}, bf16[512,256]{1,0:T(8,128)(2,1)}, u32[]{:S(2)}) copy-start(bf16[512,256]{1,0:T(8,128)(2,1)} %assemble.3) | copy-start | bytes 786436
  113.6 15.2 %collective-permute-start.21 = (bf16[512,256]{1,0:T(8,128)(2,1)}, bf16[512,256]{1,0:T(8,128)(2,1)}, u32[]{:S(2)}, u32[]{:S(2)}) collective-permute-start(bf16[512,256]{1,0:T(8,128)(2,1)} %assemble.3), channel_id=1, source_target_pairs={{0,1},{1,0},{2,3},{3,2},{4,5},{5,4},{6,7},{7,6},{8,9},{9,8},{10,11... | collective-permute-start | bytes 786440 | tf_op jit(solution)/shard_map/ppermute | solution.py:694
  113.7 14.3 %collective-permute-start.5 = (bf16[384,256]{1,0:T(8,128)(2,1)S(1)}, bf16[384,256]{1,0:T(8,128)(2,1)S(1)}, u32[]{:S(2)}, u32[]{:S(2)}) collective-permute-start(bf16[384,256]{1,0:T(8,128)(2,1)S(1)} %copy-done.4), channel_id=1, source_target_pairs={{0,4},{4,8},{8,12},{12,0},{1,5},{5,9},{9,13},{13,1},{2,6},{6,10},{... | collective-permute-start | bytes 589832 | tf_op jit(solution)/shard_map/ppermute | solution.py:681
  128.0 0.7 copy-start.14
  128.7 13.9 %collective-permute-start.11 = (bf16[384,256]{1,0:T(8,128)(2,1)}, bf16[384,256]{1,0:T(8,128)(2,1)}, u32[]{:S(2)}, u32[]{:S(2)}) collective-permute-start(bf16[384,256]{1,0:T(8,128)(2,1)} %pick.14.refs_6_.refs_11_.refs_16_), channel_id=1, source_target_pairs={{0,4},{4,8},{8,12},{12,0},{1,5},{5,9},{9,13},{13,1},{2,6},{6,10},{... | collective-permute-start | bytes 589832 | tf_op jit(solution)/shard_map/ppermute | solution.py:681
  128.9 6.1 %copy-start.11 = (bf16[384,256]{1,0:T(8,128)(2,1)S(1)}, bf16[384,256]{1,0:T(8,128)(2,1)}, u32[]{:S(2)}) copy-start(bf16[384,256]{1,0:T(8,128)(2,1)} %pick.18.refs_5_.refs_8_.refs_13_) | copy-start | bytes 589828
  133.5 0.8 copy-start.23
  134.3 18.8 %copy-start.24 = (f32[384,384]{1,0:T(8,128)S(1)}, f32[384,384]{1,0:T(8,128)}, u32[]{:S(2)}) copy-start(f32[384,384]{1,0:T(8,128)} %copy-done.23) | copy-start | bytes 1769476
  134.3 18.1 %collective-permute-start.22 = (bf16[384,384]{1,0:T(8,128)(2,1)}, bf16[384,384]{1,0:T(8,128)(2,1)S(1)}, u32[]{:S(2)}, u32[]{:S(2)}) collective-permute-start(bf16[384,384]{1,0:T(8,128)(2,1)} %get-tuple-element.24), channel_id=1, source_target_pairs={{0,2},{2,0},{1,3},{3,1},{4,6},{6,4},{5,7},{7,5},{8,10},{10,8},{9,1... | collective-permute-start | bytes 884744 | tf_op jit(solution)/shard_map/ppermute | solution.py:710
  135.0 14.6 %collective-permute-start.10 = (bf16[384,256]{1,0:T(8,128)(2,1)S(1)}, bf16[384,256]{1,0:T(8,128)(2,1)S(1)}, u32[]{:S(2)}, u32[]{:S(2)}) collective-permute-start(bf16[384,256]{1,0:T(8,128)(2,1)S(1)} %copy-done.11), channel_id=1, source_target_pairs={{0,4},{4,8},{8,12},{12,0},{1,5},{5,9},{9,13},{13,1},{2,6},{6,10},{... | collective-permute-start | bytes 589832 | tf_op jit(solution)/shard_map/ppermute | solution.py:681
  142.6 9.8 %collective-permute-start.13 = (bf16[384,256]{1,0:T(8,128)(2,1)}, bf16[384,256]{1,0:T(8,128)(2,1)S(1)}, u32[]{:S(2)}, u32[]{:S(2)}) collective-permute-start(bf16[384,256]{1,0:T(8,128)(2,1)} %collective-permute-done.11.refs_12_.refs_17_.refs_22_), channel_id=1, source_target_pairs={{0,4},{4,8},{8,12},{12,0},{1,5},{5,9},{9,13},{13,1},{2,6},{6,10},{... | collective-permute-start | bytes 589832 | tf_op jit(solution)/shard_map/ppermute | solution.py:681
  149.6 0.7 copy-start.12
  150.3 13.1 %collective-permute-start.12 = (bf16[384,256]{1,0:T(8,128)(2,1)}, bf16[384,256]{1,0:T(8,128)(2,1)}, u32[]{:S(2)}, u32[]{:S(2)}) collective-permute-start(bf16[384,256]{1,0:T(8,128)(2,1)} %pick.19.refs_9_.refs_14_.refs_19_), channel_id=1, source_target_pairs={{0,4},{4,8},{8,12},{12,0},{1,5},{5,9},{9,13},{13,1},{2,6},{6,10},{... | collective-permute-start | bytes 589832 | tf_op jit(solution)/shard_map/ppermute | solution.py:681
  152.4 0.7 copy-start.21
  153.1 24.9 %copy-start.32 = (f32[4]{0:T(128)S(1)}, f32[4]{0:T(128)}, u32[]{:S(2)}) copy-start(f32[4]{0:T(128)} %param.18) | copy-start | bytes 52
  156.9 0.8 copy-start.18
  157.7 1.0 copy-start.20
  158.7 22.3 %copy-start.2 = (bf16[384,256]{1,0:T(8,128)(2,1)S(1)}, bf16[384,256]{1,0:T(8,128)(2,1)}, u32[]{:S(2)}) copy-start(bf16[384,256]{1,0:T(8,128)(2,1)} %pick.12.refs_2_.refs_7_.refs_1_.refs_4_) | copy-start | bytes 589828
  158.7 22.3 %copy-start.9 = (bf16[384,256]{1,0:T(8,128)(2,1)S(1)}, bf16[384,256]{1,0:T(8,128)(2,1)}, u32[]{:S(2)}) copy-start(bf16[384,256]{1,0:T(8,128)(2,1)} %pick.17.refs_5_.refs_4_.refs_7_) | copy-start | bytes 589828
  158.7 22.4 %copy-start.13 = (bf16[384,256]{1,0:T(8,128)(2,1)S(1)}, bf16[384,256]{1,0:T(8,128)(2,1)}, u32[]{:S(2)}) copy-start(bf16[384,256]{1,0:T(8,128)(2,1)} %pick.19.refs_9_.refs_14_.refs_19_) | copy-start | bytes 589828
  158.7 22.4 %copy-start.15 = (bf16[384,256]{1,0:T(8,128)(2,1)S(1)}, bf16[384,256]{1,0:T(8,128)(2,1)}, u32[]{:S(2)}) copy-start(bf16[384,256]{1,0:T(8,128)(2,1)} %pick.14.refs_6_.refs_11_.refs_16_) | copy-start | bytes 589828
  158.7 22.4 %copy-start.16 = (f32[1,32,4096]{2,1,0:T(8,128)S(1)}, f32[1,32,4096]{2,1,0:T(8,128)}, u32[]{:S(2)}) copy-start(f32[1,32,4096]{2,1,0:T(8,128)} %refs_2_.1) | copy-start | bytes 1572868
  158.7 22.4 %copy-start.17 = (f32[1,32,4096]{2,1,0:T(8,128)S(1)}, f32[1,32,4096]{2,1,0:T(8,128)}, u32[]{:S(2)}) copy-start(f32[1,32,4096]{2,1,0:T(8,128)} %refs_3_.1) | copy-start | bytes 1572868
  159.5 13.8 %collective-permute-start.24 = (bf16[8,2,32,256]{3,2,0,1:T(8,128)(2,1)}, bf16[8,2,32,256]{3,2,0,1:T(8,128)(2,1)S(1)}, u32[]{:S(2)}, u32[]{:S(2)}) collective-permute-start(bf16[8,2,32,256]{3,2,0,1:T(8,128)(2,1)} %copy.26), channel_id=1, source_target_pairs={{0,1},{1,0},{2,3},{3,2},{4,5},{5,4},{6,7},{7,6},{8,9},{9,8},{10,11... | collective-permute-start | bytes 786440 | tf_op jit(solution)/shard_map/ppermute | solution.py:716
  163.4 9.9 %collective-permute-start.14 = (bf16[384,256]{1,0:T(8,128)(2,1)}, bf16[384,256]{1,0:T(8,128)(2,1)}, u32[]{:S(2)}, u32[]{:S(2)}) collective-permute-start(bf16[384,256]{1,0:T(8,128)(2,1)} %collective-permute-done.12.refs_15_.refs_20_.refs_25_), channel_id=1, source_target_pairs={{0,4},{4,8},{8,12},{12,0},{1,5},{5,9},{9,13},{13,1},{2,6},{6,10},{... | collective-permute-start | bytes 589832 | tf_op jit(solution)/shard_map/ppermute | solution.py:681
  163.4 17.7 %collective-permute-start.23 = (bf16[1024,256]{1,0:T(8,128)(2,1)}, bf16[1024,256]{1,0:T(8,128)(2,1)}, u32[]{:S(2)}, u32[]{:S(2)}) collective-permute-start(bf16[1024,256]{1,0:T(8,128)(2,1)} %get-tuple-element.27), channel_id=1, source_target_pairs={{0,1},{1,0},{2,3},{3,2},{4,5},{5,4},{6,7},{7,6},{8,9},{9,8},{10,11... | collective-permute-start | bytes 1572872 | tf_op jit(solution)/shard_map/ppermute | solution.py:715
  164.1 15.6 %collective-permute-start.17 = (bf16[8,32,256]{2,1,0:T(8,128)(2,1)}, bf16[8,32,256]{2,1,0:T(8,128)(2,1)S(1)}, u32[]{:S(2)}, u32[]{:S(2)}) collective-permute-start(bf16[8,32,256]{2,1,0:T(8,128)(2,1)} %dynamic-slice_bitcast_fusion.2), channel_id=1, source_target_pairs={{0,2},{2,0},{1,3},{3,1},{4,6},{6,4},{5,7},{7,5},{8,10},{10,8},{9,1... | collective-permute-start | bytes 393224 | tf_op jit(solution)/shard_map/ppermute | solution.py:697
  165.4 14.2 %collective-permute-start.15 = (bf16[384,256]{1,0:T(8,128)(2,1)}, bf16[384,256]{1,0:T(8,128)(2,1)}, u32[]{:S(2)}, u32[]{:S(2)}) collective-permute-start(bf16[384,256]{1,0:T(8,128)(2,1)} %copy-done.21), channel_id=1, source_target_pairs={{0,4},{4,8},{8,12},{12,0},{1,5},{5,9},{9,13},{13,1},{2,6},{6,10},{... | collective-permute-start | bytes 589832 | tf_op jit(solution)/shard_map/ppermute | solution.py:681
  173.3 7.8 %collective-permute-start.16 = (bf16[384,256]{1,0:T(8,128)(2,1)}, bf16[384,256]{1,0:T(8,128)(2,1)}, u32[]{:S(2)}, u32[]{:S(2)}) collective-permute-start(bf16[384,256]{1,0:T(8,128)(2,1)} %collective-permute-done.14.refs_21_.refs_26_), channel_id=1, source_target_pairs={{0,4},{4,8},{8,12},{12,0},{1,5},{5,9},{9,13},{13,1},{2,6},{6,10},{... | collective-permute-start | bytes 589832 | tf_op jit(solution)/shard_map/ppermute | solution.py:681
  173.3 4.7 %copy-start.30 = (bf16[8,2,32,256]{3,2,0,1:T(8,128)(2,1)}, bf16[8,2,32,256]{3,2,0,1:T(8,128)(2,1)S(1)}, u32[]{:S(2)}) copy-start(bf16[8,2,32,256]{3,2,0,1:T(8,128)(2,1)S(1)} %collective-permute-done.24) | copy-start | bytes 786436
  175.0 6.0 %collective-permute-start.25 = (bf16[8,32,256]{2,1,0:T(8,128)(2,1)}, bf16[8,32,256]{2,1,0:T(8,128)(2,1)S(1)}, u32[]{:S(2)}, u32[]{:S(2)}) collective-permute-start(bf16[8,32,256]{2,1,0:T(8,128)(2,1)} %fusion), channel_id=1, source_target_pairs={{0,2},{2,0},{1,3},{3,1},{4,6},{6,4},{5,7},{7,5},{8,10},{10,8},{9,1... | collective-permute-start | bytes 393224 | tf_op jit(solution)/shard_map/ppermute | solution.py:721
  181.1 1.0 copy-start.19
  182.2 0.9 copy-start.22

commit v3 on v0

--- a/solution.py
+++ b/solution.py
@@ -1,6 +1,10 @@
+import functools
+
 import jax
 import jax.numpy as jnp
 from jax import lax
+from jax.experimental import pallas as pl
+from jax.experimental.pallas import tpu as pltpu
 from jax.sharding import PartitionSpec as P
 
 beta_one = 0.9
@@ -22,7 +26,7 @@
     return (updated.astype(jnp.bfloat16), first_new, second_new)
 
 
-def on_device(
+def on_device_any(
     tokens,
     grad_out,
     gate_up,
@@ -147,9 +151,699 @@
     )
 
 
+ANY = pl.BlockSpec(memory_space=pl.ANY)
+SMEM = pl.BlockSpec(memory_space=pltpu.SMEM)
+VMEM = pl.BlockSpec(memory_space=pltpu.VMEM)
+STAGGER = 2
+W_CHUNKS = 4
+M_CHUNKS = 8
+CHUNKS = W_CHUNKS + M_CHUNKS
+EARLY = 5
+GU_AT = 10
+DN_AT = 11
+BACK_AT = 13
+FAR_AT = 9
+SUM_AT = 15
+EARLY_AT = 16
+
+
+def grant(mib):
+    return pltpu.CompilerParams(vmem_limit_bytes=mib * 1024 * 1024)
+
+
+def cost(flops, moved):
+    return pl.CostEstimate(flops=flops, bytes_accessed=moved, transcendentals=0)
+
+
+def in_hbm(*arrays):
+    return [pltpu.with_memory_space_constraint(array, pltpu.HBM) for array in arrays]
+
+
+def in_vmem(*arrays):
+    return [pltpu.with_memory_space_constraint(array, pltpu.VMEM) for array in arrays]
+
+
+def after(value, *others):
+    return lax.optimization_barrier((value,) + others)[0]
+
+
+def mode_of(winner_ref, members):
+    member = lax.axis_index("member")
+    source = 0
+    for other in range(members):
+        source = jnp.where(winner_ref[other] != other, winner_ref[other], source)
+    return jnp.where(
+        winner_ref[member] == member, 0, lax.rem(member - source + members, members)
+    )
+
+
+def chip_and_core():
+    index = lax.axis_index("fsdp")
+    return index // 2, lax.rem(index, 2)
+
+
+def start_all(pairs, sems):
+    copies = [pltpu.make_async_copy(a, b, sems.at[n]) for n, (a, b) in enumerate(pairs)]
+    for copy in copies:
+        copy.start()
+    return copies
+
+
+def wait_all(copies):
+    for copy in copies:
+        copy.wait()
+
+
+def assemble(winner, own, held, pieces, out_shape):
+    members = winner.shape[0]
+    arrays = [array for array, _, _, _ in own]
+
+    def kernel(winner_ref, *refs):
+        own_refs, came = refs[: len(own)], refs[len(own) : len(own) + len(held)]
+        out, sems = refs[len(own) + len(held) :]
+        mode = mode_of(winner_ref, members)
+
+        def move(refs, places):
+            wait_all(
+                start_all(
+                    [
+                        (ref.at[pl.ds(start, rows)], out.at[pl.ds(to, rows)])
+                        for ref, (_, start, rows, to) in zip(refs, places)
+                    ],
+                    sems,
+                )
+            )
+
+        @pl.when(mode == 0)
+        def _():
+            move(own_refs, own)
+
+        for hop in range(members - 1):
+
+            @pl.when(mode == hop + 1)
+            def _():
+                move([came[place + STAGGER * hop] for place, _, _, _ in pieces], pieces)
+
+    return pl.pallas_call(
+        kernel,
+        out_shape=jax.ShapeDtypeStruct(out_shape, jnp.bfloat16),
+        in_specs=[SMEM] + [ANY] * (len(own) + len(held)),
+        out_specs=VMEM,
+        scratch_shapes=[pltpu.SemaphoreType.DMA((max(len(own), len(pieces)),))],
+        compiler_params=grant(4),
+        cost_estimate=cost(0, 4 * out_shape[0] * out_shape[1]),
+        name="assemble",
+    )(winner, *arrays, *held)
+
+
+def pack_moments(m1_gu, m2_gu, m1_dn, m2_dn):
+    _, rows_gu, cols = m1_gu.shape
+    _, rows_dn, width = m1_dn.shape
+    part = rows_gu // M_CHUNKS
+    wide = width // M_CHUNKS
+    blocks = wide // cols
+    each = part + blocks * rows_dn
+
+    def kernel(m1g, m2g, m1d, m2d, *refs):
+        outs, (gu, dn, sems) = refs[:M_CHUNKS], refs[M_CHUNKS:]
+        copies = []
+        for n in range(M_CHUNKS):
+            rows, columns = pl.ds(n * part, part), pl.ds(n * wide, wide)
+            copies.append(
+                start_all(
+                    [
+                        (m1g.at[0, rows], gu.at[0, rows]),
+                        (m2g.at[0, rows], gu.at[1, rows]),
+                        (m1d.at[0, :, columns], dn.at[0, :, columns]),
+                        (m2d.at[0, :, columns], dn.at[1, :, columns]),
+                    ],
+                    sems.at[n],
+                )
+            )
+        for n, out in enumerate(outs):
+            wait_all(copies[n])
+            for k in range(2):
+                base = k * each
+                out[base : base + part] = gu[k, n * part : (n + 1) * part].astype(out.dtype)
+                for b in range(blocks):
+                    at = (n * blocks + b) * cols
+                    to = base + part + b * rows_dn
+                    out[to : to + rows_dn] = dn[k, :, at : at + cols].astype(out.dtype)
+
+    return pl.pallas_call(
+        kernel,
+        out_shape=tuple(
+            jax.ShapeDtypeStruct((2 * each, cols), jnp.bfloat16) for _ in range(M_CHUNKS)
+        ),
+        in_specs=[ANY] * 4,
+        out_specs=(VMEM,) * M_CHUNKS,
+        scratch_shapes=[
+            pltpu.VMEM((2, rows_gu, cols), jnp.float32),
+            pltpu.VMEM((2, rows_dn, width), jnp.float32),
+            pltpu.SemaphoreType.DMA((M_CHUNKS, 4)),
+        ],
+        compiler_params=grant(8),
+        cost_estimate=cost(0, 12 * (m1_gu.size + m1_dn.size)),
+        name="pack_moments",
+    )(*in_hbm(m1_gu, m2_gu, m1_dn, m2_dn))
+
+
+def pack_weights(gate_up, down):
+    _, rows_gu, cols = gate_up.shape
+    _, rows_dn, width = down.shape
+    blocks = width // cols
+    total = rows_gu + blocks * rows_dn
+    size = total // W_CHUNKS
+
+    def kernel(gu_ref, down_ref, *refs):
+        outs, (buf, sems) = refs[:W_CHUNKS], refs[W_CHUNKS:]
+        pairs = [(down_ref.at[0], buf)]
+        for n, out in enumerate(outs):
+            low = max(n * size, blocks * rows_dn)
+            rows = (n + 1) * size - low
+            if rows > 0:
+                source = gu_ref.at[0, pl.ds(low - blocks * rows_dn, rows)]
+                pairs.append((source, out.at[pl.ds(low - n * size, rows)]))
+        copies = start_all(pairs, sems)
+        copies[0].wait()
+        for b in range(blocks):
+            n, to = divmod(b * rows_dn, size)
+            outs[n][to : to + rows_dn] = buf[:, b * cols : (b + 1) * cols]
+        wait_all(copies[1:])
+
+    return pl.pallas_call(
+        kernel,
+        out_shape=tuple(jax.ShapeDtypeStruct((size, cols), down.dtype) for _ in range(W_CHUNKS)),
+        in_specs=[ANY, ANY],
+        out_specs=(VMEM,) * W_CHUNKS,
+        scratch_shapes=[
+            pltpu.VMEM((rows_dn, width), down.dtype),
+            pltpu.SemaphoreType.DMA((W_CHUNKS + 1,)),
+        ],
+        compiler_params=grant(4),
+        cost_estimate=cost(0, 4 * total * cols),
+        name="pack_weights",
+    )(*in_hbm(gate_up, down))
+
+
+def partial(count, columns):
+    return (
+        jax.ShapeDtypeStruct((2 * count, columns), jnp.float32),
+        jax.ShapeDtypeStruct((2 * count, columns), jnp.bfloat16),
+    )
+
+
+def forward_gu(tokens, tok_near, gu, gu_mate):
+    _, count, width = tokens.shape
+    half = width // 2
+    rows, cols = gu.shape
+
+    def kernel(tok_r, tokn_r, gu_r, gum_r, out, sent, tok, gub, sems):
+        chip, core = chip_and_core()
+        mine = pl.ds(pl.multiple_of(chip * half, half), half)
+        first = pl.ds(pl.multiple_of(core * rows, rows), rows)
+        second = pl.ds(pl.multiple_of((1 - core) * rows, rows), rows)
+        pairs = [
+            (gu_r, gub.at[first]),
+            (gum_r, gub.at[second]),
+            (tok_r.at[0, :, mine], tok.at[pl.ds(0, count)]),
+            (tokn_r, tok.at[pl.ds(count, count)]),
+        ]
+        wait_all(start_all(pairs, sems))
+        pre = jnp.dot(tok[...], gub[...], preferred_element_type=jnp.float32)
+        out[...] = pre
+        sent[...] = pre.astype(sent.dtype)
+
+    return pl.pallas_call(
+        kernel,
+        out_shape=partial(count, cols),
+        in_specs=[ANY] * 4,
+        out_specs=(VMEM, VMEM),
+        scratch_shapes=[
+            pltpu.VMEM((2 * count, half), jnp.bfloat16),
+            pltpu.VMEM((half, cols), jnp.bfloat16),
+            pltpu.SemaphoreType.DMA((4,)),
+        ],
+        compiler_params=grant(8),
+        cost_estimate=cost(4 * count * half * cols, 3 * 1024 * 1024),
+        name="forward_gu",
+    )(*in_hbm(tokens), tok_near, gu, gu_mate)
+
+
+def forward_dn(grad_out, up_near, parts):
+    _, count, width = grad_out.shape
+    half = width // 2
+    blocks, rows, cols = parts[0].shape
+    units = 4 * rows
+
+    def kernel(up_r, upn_r, mine_r, near_r, mate_r, far_r, out, sent, up, dnb, sems):
+        chip, core = chip_and_core()
+        mine = pl.ds(pl.multiple_of(chip * half, half), half)
+        pairs = [
+            (up_r.at[0, :, mine], up.at[pl.ds(0, count)]),
+            (upn_r, up.at[pl.ds(count, count)]),
+            (mine_r, dnb.at[:, chip, core]),
+            (near_r, dnb.at[:, 1 - chip, core]),
+            (mate_r, dnb.at[:, chip, 1 - core]),
+            (far_r, dnb.at[:, 1 - chip, 1 - core]),
+        ]
+        wait_all(start_all(pairs, sems))
+        dh = jnp.zeros((2 * count, units), jnp.float32)
+        for b in range(blocks):
+            dh += lax.dot_general(
+                up[:, b * cols : (b + 1) * cols],
+                dnb[b].reshape(units, cols),
+                (((1,), (1,)), ((), ())),
+                preferred_element_type=jnp.float32,
+            )
+        out[...] = dh
+        sent[...] = dh.astype(sent.dtype)
+
+    return pl.pallas_call(
+        kernel,
+        out_shape=partial(count, units),
+        in_specs=[ANY] * 6,
+        out_specs=(VMEM, VMEM),
+        scratch_shapes=[
+            pltpu.VMEM((2 * count, half), jnp.bfloat16),
+            pltpu.VMEM((blocks, 2, 2, rows, cols), jnp.bfloat16),
+            pltpu.SemaphoreType.DMA((6,)),
+        ],
+        compiler_params=grant(8),
+        cost_estimate=cost(4 * count * half * units, 3 * 1024 * 1024),
+        name="forward_dn",
+    )(*in_hbm(grad_out), up_near, *parts)
+
+
+def backward(pre, pre_near, dh, dh_near, tokens, tok_near, grad_out, up_near, rows, rows_dn):
+    _, count, width = tokens.shape
+    half = width // 2
+    units = 4 * rows_dn
+    cols = 2 * units
+    blocks = half // cols
+
+    def kernel(pre_r, pren_r, dh_r, dhn_r, tok_r, tokn_r, up_r, upn_r, g_own, g_mate, d_own, d_mate, tok, tokm, up, res, sems):
+        chip, core = chip_and_core()
+        mine = pl.ds(pl.multiple_of(chip * half, half), half)
+        first = pl.multiple_of(core * rows, rows)
+        second = pl.multiple_of((1 - core) * rows, rows)
+        here = pl.multiple_of(chip * half, half)
+        pairs = [
+            (up_r.at[0, :, mine], up.at[pl.ds(0, count)]),
+            (upn_r, up.at[pl.ds(count, count)]),
+            (tok_r.at[0, :, pl.ds(here + second, rows)], tokm.at[pl.ds(0, count)]),
+            (tokn_r.at[:, pl.ds(second, rows)], tokm.at[pl.ds(count, count)]),
+            (tok_r.at[0, :, pl.ds(here + first, rows)], tok.at[pl.ds(0, count)]),
+            (tokn_r.at[:, pl.ds(first, rows)], tok.at[pl.ds(count, count)]),
+        ]
+        copies = start_all(pairs, sems)
+
+        def whole(own, near):
+            return own[...] + jnp.concatenate([near[count:], near[:count]]).astype(jnp.float32)
+
+        full = whole(pre_r, pren_r) * width ** (-0.5)
+        gate = full[:, :units]
+        upper = full[:, units:]
+        dhidden = whole(dh_r, dhn_r) * units ** (-0.5)
+        sigma = jax.nn.sigmoid(gate)
+        active = gate * sigma
+        hidden = (active * upper).astype(jnp.bfloat16)
+        dgate = dhidden * upper * (sigma * (1.0 + gate * (1.0 - sigma)))
+        dupper = dhidden * active
+        dpre = (jnp.concatenate([dgate, dupper], axis=1) * width ** (-0.5)).astype(jnp.bfloat16)
+        over_tokens = (((0,), (0,)), ((), ()))
+        wait_all(copies[:2])
+        for b in range(blocks):
+            res[b] = lax.dot_general(
+                hidden, up[:, b * cols : (b + 1) * cols], over_tokens, preferred_element_type=jnp.float32
+            ) * units ** (-0.5)
+        for b in range(blocks):
+            for x in range(2):
+                base = x * 2 * rows_dn
+                d_own[x, b] = res[b, pl.ds(pl.multiple_of(base + core * rows_dn, rows_dn), rows_dn)]
+                d_mate[x, b] = res[
+                    b, pl.ds(pl.multiple_of(base + (1 - core) * rows_dn, rows_dn), rows_dn)
+                ].astype(d_mate.dtype)
+        wait_all(copies[2:4])
+        g_mate[...] = lax.dot_general(
+            tokm[...], dpre, over_tokens, preferred_element_type=jnp.float32
+        ).astype(g_mate.dtype)
+        wait_all(copies[4:])
+        g_own[...] = lax.dot_general(tok[...], dpre, over_tokens, preferred_element_type=jnp.float32)
+
+    f32, bf16 = jnp.float32, jnp.bfloat16
+    dn_shape = (2, blocks, rows_dn, cols)
+    return pl.pallas_call(
+        kernel,
+        out_shape=(
+            pltpu.VMEM((rows, cols), f32),
+            pltpu.VMEM((rows, cols), bf16),
+            pltpu.VMEM(dn_shape, f32),
+            pltpu.VMEM(dn_shape, bf16),
+        ),
+        in_specs=[VMEM] * 4 + [ANY] * 4,
+        out_specs=(VMEM,) * 4,
+        scratch_shapes=[
+            pltpu.VMEM((2 * count, rows), bf16),
+            pltpu.VMEM((2 * count, rows), bf16),
+            pltpu.VMEM((2 * count, half), bf16),
+            pltpu.VMEM((blocks, units, cols), f32),
+            pltpu.SemaphoreType.DMA((6,)),
+        ],
+        compiler_params=grant(16),
+        cost_estimate=cost(4 * count * half * (cols + units), 6 * 1024 * 1024),
+        name="backward",
+    )(pre, pre_near, dh, dh_near, *in_hbm(tokens), tok_near, *in_hbm(grad_out), up_near)
+
+
+def adamw_part(weight, grad, first, second, rate):
+    first_new = beta_one * first + (1.0 - beta_one) * grad
+    second_new = beta_two * second + (1.0 - beta_two) * grad * grad
+    wide = weight.astype(jnp.float32)
+    updated = wide - rate * (first_new / (jnp.sqrt(second_new) + epsilon) + decay * wide)
+    return updated.astype(jnp.bfloat16), first_new, second_new
+
+
+def start_moments(mode, members, own_pairs, came_pairs, sems):
+    @pl.when(mode == 0)
+    def _():
+        for n, pairs in enumerate(own_pairs):
+            for k, (a, b) in enumerate(pairs):
+                pltpu.make_async_copy(a, b, sems.at[n, k]).start()
+
+    for hop in range(members - 1):
+
+        @pl.when(mode == hop + 1)
+        def _():
+            for n, pairs in enumerate(came_pairs[hop]):
+                for k, (a, b) in enumerate(pairs):
+                    pltpu.make_async_copy(a, b, sems.at[n, k]).start()
+
+
+def wait_moments(mode, n, own_pairs, came_pairs, sems):
+    @pl.when(mode == 0)
+    def _():
+        for k, (a, b) in enumerate(own_pairs[n]):
+            pltpu.make_async_copy(a, b, sems.at[n, k]).wait()
+
+    @pl.when(mode != 0)
+    def _():
+        for k, (a, b) in enumerate(came_pairs[0][n]):
+            pltpu.make_async_copy(a, b, sems.at[n, k]).wait()
+
+
+def update_gu(winner, learning, low, high, m1, m2, held, gu, g_own, g_got, done):
+    members = winner.shape[0]
+    _, rows, cols = m1.shape
+    part = rows // M_CHUNKS
+    each = held[0].shape[0] // 2
+    count = high - low
+    start, size = low * part, (high - low) * part
+    f32, bf16 = jnp.float32, jnp.bfloat16
+    span = pl.ds(start, size)
+
+    def kernel(winner_ref, rate_ref, m1_r, m2_r, gu_r, go_r, gm_r, *refs):
+        came = refs[: len(held)]
+        refs = refs[len(held) + len(done) :]
+        n_w, n_1, n_2, bgu, bgo, bgm, own, moved, o_w, o_1, o_2, sems, msems, osems = refs
+        mode = mode_of(winner_ref, members)
+        rate = rate_ref[winner_ref[lax.axis_index("member")]]
+        own_pairs = [
+            [
+                (m1_r.at[0, pl.ds(start + n * part, part)], own.at[0, pl.ds(n * part, part)]),
+                (m2_r.at[0, pl.ds(start + n * part, part)], own.at[1, pl.ds(n * part, part)]),
+            ]
+            for n in range(count)
+        ]
+        came_pairs = [
+            [
+                [
+                    (came[n + STAGGER * hop].at[pl.ds(0, part)], moved.at[n, 0]),
+                    (came[n + STAGGER * hop].at[pl.ds(each, part)], moved.at[n, 1]),
+                ]
+                for n in range(count)
+            ]
+            for hop in range(members - 1)
+        ]
+        copies = start_all([(gu_r.at[span], bgu), (go_r.at[span], bgo), (gm_r.at[span], bgm)], sems)
+        start_moments(mode, members, own_pairs, came_pairs, msems)
+        wait_all(copies)
+        outs = []
+        for n in range(count):
+            wait_moments(mode, n, own_pairs, came_pairs, msems)
+            at = slice(n * part, (n + 1) * part)
+            first = jnp.where(mode == 0, own[0, at], moved[n, 0].astype(f32))
+            second = jnp.where(mode == 0, own[1, at], moved[n, 1].astype(f32))
+            grad = bgo[at] + bgm[at].astype(f32)
+            o_w[at], o_1[at], o_2[at] = adamw_part(bgu[at], grad, first, second, rate)
+            here, there = pl.ds(n * part, part), pl.ds(start + n * part, part)
+            outs += start_all(
+                [
+                    (o_w.at[here], n_w.at[0, there]),
+                    (o_1.at[here], n_1.at[0, there]),
+                    (o_2.at[here], n_2.at[0, there]),
+                ],
+                osems.at[n],
+            )
+        wait_all(outs)
+
+    return pl.pallas_call(
+        kernel,
+        out_shape=tuple(jax.ShapeDtypeStruct((1, rows, cols), t) for t in (bf16, f32, f32)),
+        in_specs=[SMEM, SMEM] + [ANY] * (5 + len(held) + len(done)),
+        out_specs=(ANY,) * 3,
+        scratch_shapes=[
+            pltpu.VMEM((size, cols), bf16),
+            pltpu.VMEM((size, cols), f32),
+            pltpu.VMEM((size, cols), bf16),
+            pltpu.VMEM((2, size, cols), f32),
+            pltpu.VMEM((count, 2, part, cols), bf16),
+            pltpu.VMEM((size, cols), bf16),
+            pltpu.VMEM((size, cols), f32),
+            pltpu.VMEM((size, cols), f32),
+            pltpu.SemaphoreType.DMA((3,)),
+            pltpu.SemaphoreType.DMA((count, 2)),
+            pltpu.SemaphoreType.DMA((count, 3)),
+        ],
+        input_output_aliases={7 + len(held) + n: n for n in range(len(done))},
+        compiler_params=grant(12),
+        cost_estimate=cost(0, 22 * size * cols),
+        name="update_gu",
+    )(winner, learning, *in_hbm(m1, m2), *in_vmem(gu, g_own, g_got, *held), *done)
+
+
+def update_dn(winner, learning, m1, m2, held, dn, d_own, d_got, d_back):
+    members = winner.shape[0]
+    _, rows, width = m1.shape
+    _, blocks, _, cols = dn.shape
+    each = held[0].shape[0] // 2
+    per = 2 * blocks // M_CHUNKS
+    size = per * rows
+    base = each - size
+    f32, bf16 = jnp.float32, jnp.bfloat16
+
+    def kernel(winner_ref, rate_ref, m1_r, m2_r, dn_r, do_r, dm_r, gb_r, *refs):
+        came = refs[: len(held)]
+        n_w, n_1, n_2, bdn, bdo, bdm, bgb, grad, own, moved, o_w, o_1, o_2, sems, msems, osems = refs[len(held) :]
+        chip, _ = chip_and_core()
+        mode = mode_of(winner_ref, members)
+        rate = rate_ref[winner_ref[lax.axis_index("member")]]
+        own_pairs = [
+            [
+                (m1_r.at[0, :, pl.ds(n * per * cols, per * cols)], own.at[0, :, pl.ds(n * per * cols, per * cols)]),
+                (m2_r.at[0, :, pl.ds(n * per * cols, per * cols)], own.at[1, :, pl.ds(n * per * cols, per * cols)]),
+            ]
+            for n in range(M_CHUNKS)
+        ]
+        came_pairs = [
+            [
+                [
+                    (came[n + STAGGER * hop].at[pl.ds(base, size)], moved.at[n, 0]),
+                    (came[n + STAGGER * hop].at[pl.ds(each + base, size)], moved.at[n, 1]),
+                ]
+                for n in range(M_CHUNKS)
+            ]
+            for hop in range(members - 1)
+        ]
+        copies = start_all(
+            [
+                (dn_r, bdn),
+                (do_r.at[chip], bdo),
+                (dm_r.at[chip], bdm),
+                (gb_r, bgb),
+            ],
+            sems,
+        )
+        start_moments(mode, members, own_pairs, came_pairs, msems)
+        wait_all(copies)
+        grad[chip] = bdo[...] + bdm[...].astype(f32)
+        grad[1 - chip] = bgb[...].astype(f32)
+        outs = []
+        for n in range(M_CHUNKS):
+            wait_moments(mode, n, own_pairs, came_pairs, msems)
+            for i in range(per):
+                at = slice((n * per + i) * cols, (n * per + i + 1) * cols)
+                sub = slice(i * rows, (i + 1) * rows)
+                first = jnp.where(mode == 0, own[0, :, at], moved[n, 0, sub].astype(f32))
+                second = jnp.where(mode == 0, own[1, :, at], moved[n, 1, sub].astype(f32))
+                side, b = divmod(n * per + i, blocks)
+                o_w[:, at], o_1[:, at], o_2[:, at] = adamw_part(bdn[side, b], grad[side, b], first, second, rate)
+            if n % 4 == 3:
+                at = pl.ds((n - 3) * per * cols, 4 * per * cols)
+                outs += start_all(
+                    [
+                        (o_w.at[:, at], n_w.at[0, :, at]),
+                        (o_1.at[:, at], n_1.at[0, :, at]),
+                        (o_2.at[:, at], n_2.at[0, :, at]),
+                    ],
+                    osems.at[n // 4],
+                )
+        wait_all(outs)
+
+    half = (blocks, rows, cols)
+    return pl.pallas_call(
+        kernel,
+        out_shape=tuple(jax.ShapeDtypeStruct((1, rows, width), t) for t in (bf16, f32, f32)),
+        in_specs=[SMEM, SMEM] + [ANY] * (6 + len(held)),
+        out_specs=(ANY,) * 3,
+        scratch_shapes=[
+            pltpu.VMEM((2,) + half, bf16),
+            pltpu.VMEM(half, f32),
+            pltpu.VMEM(half, bf16),
+            pltpu.VMEM(half, bf16),
+            pltpu.VMEM((2,) + half, f32),
+            pltpu.VMEM((2, rows, width), f32),
+            pltpu.VMEM((M_CHUNKS, 2, size, cols), bf16),
+            pltpu.VMEM((rows, width), bf16),
+            pltpu.VMEM((rows, width), f32),
+            pltpu.VMEM((rows, width), f32),
+            pltpu.SemaphoreType.DMA((4,)),
+            pltpu.SemaphoreType.DMA((M_CHUNKS, 2)),
+            pltpu.SemaphoreType.DMA((M_CHUNKS // 4, 3)),
+        ],
+        compiler_params=grant(10),
+        cost_estimate=cost(0, 26 * rows * width),
+        name="update_dn",
+    )(winner, learning, *in_hbm(m1, m2), *in_vmem(dn, d_own, d_got, d_back, *held))
+
+
+def on_device_four(
+    tokens,
+    grad_out,
+    gate_up,
+    down,
+    mom1_gate_up,
+    mom2_gate_up,
+    mom1_down,
+    mom2_down,
+    learning,
+    winner,
+):
+    members = lax.axis_size("member")
+    member_index = lax.axis_index("member")
+    fsdp_index = lax.axis_index("fsdp")
+    chip = fsdp_index // 2
+    over_x = [(0, 2), (2, 0), (1, 3), (3, 1)]
+    over_core = [(0, 1), (1, 0), (2, 3), (3, 2)]
+    ring = [(i, (i + 1) % members) for i in range(members)]
+    half = tokens.shape[2] // 2
+    _, rows_gu, cols = gate_up.shape
+    rows_dn = down.shape[1]
+    rows_all = rows_gu + down.size // cols
+    w_rows = rows_all // W_CHUNKS
+
+    indices = jnp.arange(members, dtype=winner.dtype)
+    is_source = jnp.any((winner == member_index) & (indices != member_index))
+
+    def theirs(x):
+        return lax.dynamic_slice_in_dim(x[0], (1 - chip) * half, half, axis=1)
+
+    own = list(pack_weights(gate_up, down))
+    got = [lax.ppermute(chunk, "member", ring) for chunk in own[:STAGGER]]
+    tok_theirs = theirs(after(tokens, *own))
+    tok_near = lax.ppermute(tok_theirs, "fsdp", over_x)
+    up_theirs = theirs(after(grad_out, tok_theirs))
+    up_near = lax.ppermute(up_theirs, "fsdp", over_x)
+    got[0] = after(got[0], up_theirs)
+
+    def rows_from(low, high):
+        pieces = []
+        for c in range(low // w_rows, (high - 1) // w_rows + 1):
+            first, stop = max(low, c * w_rows), min(high, (c + 1) * w_rows)
+            pieces.append((c, first - c * w_rows, stop - first, first - low))
+        return pieces
+
+    def take(low, high):
+        pieces = rows_from(low, high)
+        kept = [(own[piece[0]],) + piece[1:] for piece in pieces]
+        return assemble(winner, kept, held[:], pieces, (high - low, cols))
+
+    rows_d = down.size // cols
+    held = []
+    last = STAGGER * (members - 2)
+    pre = dh = grads = first_gu = None
+    for step in range(STAGGER, CHUNKS + last + STAGGER):
+        back = got[step - STAGGER]
+        if step < CHUNKS:
+            back = jnp.where(is_source, own[step], back)
+        held.append(back)
+        if step < CHUNKS + last:
+            got.append(lax.ppermute(back, "member", ring))
+        if step == STAGGER:
+            own += pack_moments(after(mom1_gate_up, back), mom2_gate_up, mom1_down, mom2_down)
+        ready = len(held) - 1 - last
+        if ready == (rows_d - 1) // w_rows:
+            dn = take(0, rows_d).reshape(2, -1, rows_dn, cols)
+            dn_mine = lax.dynamic_index_in_dim(dn, chip, axis=0, keepdims=False)
+            dn_theirs = lax.dynamic_index_in_dim(dn, 1 - chip, axis=0, keepdims=False)
+            dn_near = lax.ppermute(dn_theirs, "fsdp", over_x)
+            dn_mate = lax.ppermute(dn_mine, "fsdp", over_core)
+        if step == FAR_AT:
+            dn_near = after(dn_near, back)
+            dn_far = lax.ppermute(dn_near, "fsdp", over_core)
+        if ready == W_CHUNKS - 1:
+            gu = take(rows_d, rows_all)
+            gu_mate = lax.ppermute(gu, "fsdp", over_core)
+        if step == GU_AT:
+            pre, pre_sent = forward_gu(tokens, tok_near, after(gu, back), gu_mate)
+            pre_near = lax.ppermute(pre_sent, "fsdp", over_x)
+        if step == DN_AT:
+            dh, dh_sent = forward_dn(
+                grad_out, up_near, (after(dn_mine, back), dn_near, dn_mate, dn_far)
+            )
+            dh_near = lax.ppermute(dh_sent, "fsdp", over_x)
+        if step == BACK_AT:
+            g_own, g_mate, d_own, d_mate = backward(
+                after(pre, back), pre_near, dh, dh_near, tokens, tok_near, grad_out, up_near, rows_gu, rows_dn
+            )
+            g_got = lax.ppermute(g_mate, "fsdp", over_core)
+            d_got = lax.ppermute(d_mate, "fsdp", over_core)
+        if step == SUM_AT:
+            d_there = (
+                lax.dynamic_index_in_dim(after(d_own, back), 1 - chip, axis=0, keepdims=False)
+                + lax.dynamic_index_in_dim(d_got, 1 - chip, axis=0, keepdims=False)
+            ).astype(jnp.bfloat16)
+            d_back = lax.ppermute(d_there, "fsdp", over_x)
+        if step == EARLY_AT:
+            first_gu = update_gu(
+                winner, learning, 0, EARLY, mom1_gate_up, mom2_gate_up,
+                held[W_CHUNKS : W_CHUNKS + EARLY + last], after(gu, back), g_own, g_got, ()
+            )
+
+    new_gu, new_first_gu, new_second_gu = update_gu(
+        winner, learning, EARLY, M_CHUNKS, mom1_gate_up, mom2_gate_up,
+        held[W_CHUNKS + EARLY :], gu, g_own, g_got, first_gu
+    )
+    new_dn, new_first_dn, new_second_dn = update_dn(
+        winner, learning, mom1_down, mom2_down, held[W_CHUNKS:], dn, d_own, d_got, d_back
+    )
+    return (new_gu, new_dn, new_first_gu, new_second_gu, new_first_dn, new_second_dn)
+
+
 def solution(mesh):
+    small = mesh.shape["member"] == 4 and mesh.shape["fsdp"] == 4
     return jax.shard_map(
-        on_device,
+        on_device_four if small else on_device_any,
         mesh=mesh,
         in_specs=(
             P(("groups", "member"), "fsdp", None),

time: 407 us -> 111 us (0.27)
  waiting for transfers between devices: 258 us -> 62.7 us
  local copies, waits for them, and re-layouts: 60.8 us -> 2.3 us
  other arithmetic: 38.8 us -> 7.37 us
  Pallas kernels: 0 us -> 23.1 us
  between operations: 17.6 us -> 0.92 us
  matrix products: 8.17 us -> 0 us
  starting transfers between devices: 19.2 us -> 14.2 us
    psum x4 -> x0, waiting for transfers between devices: 189 us -> none  [spread(): return lax.psum(block, axis)]
    ppermute x0 -> x27, waiting for transfers between devices: none -> 62.7 us  [the longest x14 55.9 us: on_device_four(): got.append(lax.ppermute(back, 'member', ring))]
    reduce_scatter x2 -> x0, waiting for transfers between devices: 34.8 us -> none  [the longest x1 30.8 us: on_device(): lax.psum_scatter(lax.dot_general(columns, dpreact, (((0,), (0,)), ((), ()...]
    all_to_all x4 -> x0, waiting for transfers between devices: 34.3 us -> none  [the longest x1 13.5 us: on_device(): lax.all_to_all(jnp.take(lax.all_to_all(joined(mom1_gate_up[0], mom1_down[...]
    unnamed x61 -> x6, local copies, waits for them, and re-layouts: 32 us -> 0.01 us
    pallas_call x0 -> x10, Pallas kernels: none -> 23.1 us  [the longest x2 7.15 us: update_gu(): pl.pallas_call(kernel, out_shape=tuple((jax.ShapeDtypeStruct((1, rows, co...]
    all_to_all x4 -> x0, starting transfers between devices: 18.5 us -> none  [the longest x1 6.45 us: on_device(): lax.all_to_all(joined(mom2_gate_up[0], mom2_down[0]).astype(jnp.bfloat16)...]
    ppermute x0 -> x27, starting transfers between devices: none -> 14.2 us  [the longest x2 4.65 us: on_device_four(): got = [lax.ppermute(chunk, 'member', ring) for chunk in own[:STAGGER]]]
  transfers between devices with their start and end apart: 12 -> 27, of which waited for: 9 -> 14; matrix products, arithmetic and copies ran while one was open for 22% -> 9% of each run, Pallas kernels for 0% -> 13%
where the time goes in v3:
time: 111 us
  waiting for transfers between devices  62.7 us (56%)
  Pallas kernels  23.1 us (21%)
  starting transfers between devices  14.2 us (13%)
  other arithmetic  7.37 us (7%)
  local copies, waits for them, and re-layouts  2.3 us (2%)
    ppermute x14, waiting for transfers between devices, on_device_four(): got.append(lax.ppermute(back, 'member', ring))  55.9 us
    pallas_call x2, Pallas kernels, update_gu(): pl.pallas_call(kernel, out_shape=tuple((jax.ShapeDtypeStruct((1, rows, co...  7.15 us
    select_n x10, other arithmetic, on_device_four(): back = jnp.where(is_source, own[step], back)  6.7 us
    ppermute x2, starting transfers between devices, on_device_four(): got = [lax.ppermute(chunk, 'member', ring) for chunk in own[:STAGGER]]  4.65 us
    ppermute x2, waiting for transfers between devices, on_device_four(): got = [lax.ppermute(chunk, 'member', ring) for chunk in own[:STAGGER]]  4.57 us
    pallas_call x1, Pallas kernels, update_dn(): pl.pallas_call(kernel, out_shape=tuple((jax.ShapeDtypeStruct((1, rows, wi...  3.48 us
    pallas_call x1, Pallas kernels, backward(): pl.pallas_call(kernel, out_shape=(pltpu.VMEM((rows, cols), f32), pltpu.VM...  3.22 us
    dynamic_slice x2, local copies, waits for them, and re-layouts, theirs(): return lax.dynamic_slice_in_dim(x[0], (1 - chip) * half, half, axis=1)  2.26 us
  transfers between devices with their start and end apart: 27, of which 14 were waited for; matrix products, arithmetic and copies ran while one was open for 9% of the time, Pallas kernels for 13%

profile of v3, /device:TPU:0, one launch (start us, length us, event | category | flops | bytes accessed | tf_op | source)
XLA Modules:
  0.0 110.6 jit_solution(1270309170887364688)
XLA Ops:
  0.6 1.2 %pack_weights.1 = (bf16[384,256]{1,0:T(8,128)(2,1)S(1)}, bf16[384,256]{1,0:T(8,128)(2,1)S(1)}, bf16[384,256]{1,0:T(8,128)(2,1)S(1)}, bf16[384,256]{1,0:T(8,128)(2,1)S(1)}) custom-call(bf16[1,1024,256]{2,1,0:T(8,128)(2,1)} %gu_ref.1, bf16[1,32,4096]{2,1,0:T(8,128)(2,1)} %down_ref.1), custom_call_target="tpu_custom_call" | custom-call | bytes 1572864 | tf_op jit(solution)/shard_map/pack_weights/pallas_call | solution.py:334
  1.8 3.1 %collective-permute-start = (bf16[384,256]{1,0:T(8,128)(2,1)S(1)}, bf16[384,256]{1,0:T(8,128)(2,1)S(1)}, u32[]{:S(2)}, u32[]{:S(2)}) collective-permute-start(bf16[384,256]{1,0:T(8,128)(2,1)S(1)} %get-tuple-element.48.refs_0_), channel_id=1, source_target_pairs={{0,4},{4,8},{8,12},{12,0},{1,5},{5,9},{9,13},{13,1},{2,6},{6,10},{... | collective-permute-start | bytes 589832 | tf_op jit(solution)/shard_map/ppermute | solution.py:762
  4.9 1.6 %collective-permute-start.1 = (bf16[384,256]{1,0:T(8,128)(2,1)S(1)}, bf16[384,256]{1,0:T(8,128)(2,1)S(1)}, u32[]{:S(2)}, u32[]{:S(2)}) collective-permute-start(bf16[384,256]{1,0:T(8,128)(2,1)S(1)} %get-tuple-element.45.refs_0_.refs_1_), channel_id=1, source_target_pairs={{0,4},{4,8},{8,12},{12,0},{1,5},{5,9},{9,13},{13,1},{2,6},{6,10},{... | collective-permute-start | bytes 589832 | tf_op jit(solution)/shard_map/ppermute | solution.py:762
  6.5 2.2 %dynamic-slice_bitcast_fusion.1 = bf16[192,2048]{1,0:T(8,128)(2,1)} fusion(bf16[1,192,4096]{2,1,0:T(8,128)(2,1)} %tok_r.3, s32[]{:T(128)S(6)} %select_n.66), kind=kLoop, calls=%fused_computation.1 | loop fusion | bytes 1572868 | tf_op jit(solution)/shard_map/dynamic_slice | solution.py:759
  8.7 1.5 %collective-permute-start.8 = (bf16[192,2048]{1,0:T(8,128)(2,1)}, bf16[192,2048]{1,0:T(8,128)(2,1)S(1)}, u32[]{:S(2)}, u32[]{:S(2)}) collective-permute-start(bf16[192,2048]{1,0:T(8,128)(2,1)} %dynamic-slice_bitcast_fusion.1), channel_id=1, source_target_pairs={{0,2},{2,0},{1,3},{3,1},{4,6},{6,4},{5,7},{7,5},{8,10},{10,8},{9,1... | collective-permute-start | bytes 2359304 | tf_op jit(solution)/shard_map/ppermute | solution.py:764
  10.2 0.1 dynamic-slice_bitcast_fusion
  10.3 0.6 collective-permute-start.14
  10.9 0.6 and_reduce_fusion
  11.5 4.6 %collective-permute-done.1 = bf16[384,256]{1,0:T(8,128)(2,1)S(1)} collective-permute-done((bf16[384,256]{1,0:T(8,128)(2,1)S(1)}, bf16[384,256]{1,0:T(8,128)(2,1)S(1)}, u32[]{:S(2)}, u32[]{:S(2)}) %collective-permute-start.1) | collective-permute-done | bytes 196640 | tf_op jit(solution)/shard_map/ppermute | solution.py:762
  16.1 0.7 broadcast_select_fusion.8.refs_4_.refs_3_
  16.7 0.1 collective-permute-start.3
  16.8 0.7 broadcast_select_fusion.9.refs_3_.refs_2_
  17.5 1.3 %collective-permute-start.2 = (bf16[384,256]{1,0:T(8,128)(2,1)S(1)}, bf16[384,256]{1,0:T(8,128)(2,1)S(1)}, u32[]{:S(2)}, u32[]{:S(2)}) collective-permute-start(bf16[384,256]{1,0:T(8,128)(2,1)S(1)} %broadcast_select_fusion.9.refs_3_.refs_2_), channel_id=1, source_target_pairs={{0,4},{4,8},{8,12},{12,0},{1,5},{5,9},{9,13},{13,1},{2,6},{6,10},{... | collective-permute-start | bytes 589832 | tf_op jit(solution)/shard_map/ppermute | solution.py:791
  18.8 2.2 %pack_moments.1 = (bf16[384,256]{1,0:T(8,128)(2,1)S(1)}, bf16[384,256]{1,0:T(8,128)(2,1)S(1)}, bf16[384,256]{1,0:T(8,128)(2,1)S(1)}, bf16[384,256]{1,0:T(8,128)(...) custom-call(f32[1,1024,256]{2,1,0:T(8,128)} %m1_r.4, ...), custom_call_target="tpu_custom_call" | custom-call | bytes 4718592 | tf_op jit(solution)/shard_map/pack_moments/pallas_call | solution.py:293
  21.0 5.4 %collective-permute-done.3 = bf16[384,256]{1,0:T(8,128)(2,1)S(1)} collective-permute-done((bf16[384,256]{1,0:T(8,128)(2,1)S(1)}, bf16[384,256]{1,0:T(8,128)(2,1)S(1)}, u32[]{:S(2)}, u32[]{:S(2)}) %collective-permute-start.3) | collective-permute-done | bytes 196640 | tf_op jit(solution)/shard_map/ppermute | solution.py:791
  26.4 0.7 broadcast_select_fusion.6.refs_6_.refs_5_
  27.1 0.1 collective-permute-start.5
  27.2 2.4 %collective-permute-done.2 = bf16[384,256]{1,0:T(8,128)(2,1)S(1)} collective-permute-done((bf16[384,256]{1,0:T(8,128)(2,1)S(1)}, bf16[384,256]{1,0:T(8,128)(2,1)S(1)}, u32[]{:S(2)}, u32[]{:S(2)}) %collective-permute-start.2) | collective-permute-done | bytes 196640 | tf_op jit(solution)/shard_map/ppermute | solution.py:791
  29.6 0.7 broadcast_select_fusion.7.refs_5_.refs_4_
  30.2 0.1 collective-permute-start.4
  30.3 6.4 %collective-permute-done.5 = bf16[384,256]{1,0:T(8,128)(2,1)S(1)} collective-permute-done((bf16[384,256]{1,0:T(8,128)(2,1)S(1)}, bf16[384,256]{1,0:T(8,128)(2,1)S(1)}, u32[]{:S(2)}, u32[]{:S(2)}) %collective-permute-start.5) | collective-permute-done | bytes 196640 | tf_op jit(solution)/shard_map/ppermute | solution.py:791
  36.7 0.7 broadcast_select_fusion.4.refs_8_.refs_7_.refs_1_
  37.4 0.1 collective-permute-start.7
  37.5 3.3 %collective-permute-done.4 = bf16[384,256]{1,0:T(8,128)(2,1)S(1)} collective-permute-done((bf16[384,256]{1,0:T(8,128)(2,1)S(1)}, bf16[384,256]{1,0:T(8,128)(2,1)S(1)}, u32[]{:S(2)}, u32[]{:S(2)}) %collective-permute-start.4) | collective-permute-done | bytes 196640 | tf_op jit(solution)/shard_map/ppermute | solution.py:791
  40.8 0.7 broadcast_select_fusion.5.refs_7_.refs_6_.refs_0_
  41.5 0.9 assemble.3
  42.4 0.1 collective-permute-start.6
  42.5 1.1 collective-permute-start.15
  43.6 3.5 %collective-permute-done.7 = bf16[384,256]{1,0:T(8,128)(2,1)S(1)} collective-permute-done((bf16[384,256]{1,0:T(8,128)(2,1)S(1)}, bf16[384,256]{1,0:T(8,128)(2,1)S(1)}, u32[]{:S(2)}, u32[]{:S(2)}) %collective-permute-start.7) | collective-permute-done | bytes 196640 | tf_op jit(solution)/shard_map/ppermute | solution.py:791
  47.0 0.7 broadcast_select_fusion.2.refs_10_.refs_3_
  47.7 0.1 collective-permute-start.11
  47.8 3.3 %collective-permute-done.6 = bf16[384,256]{1,0:T(8,128)(2,1)S(1)} collective-permute-done((bf16[384,256]{1,0:T(8,128)(2,1)S(1)}, bf16[384,256]{1,0:T(8,128)(2,1)S(1)}, u32[]{:S(2)}, u32[]{:S(2)}) %collective-permute-start.6) | collective-permute-done | bytes 196640 | tf_op jit(solution)/shard_map/ppermute | solution.py:791
  51.0 0.7 broadcast_select_fusion.3.refs_9_.refs_2_
  51.7 1.3 %assemble.2.gu_r = bf16[1024,256]{1,0:T(8,128)(2,1)S(1)} custom-call(s32[4]{0:T(128)S(1)} %copy-done, bf16[384,256]{1,0:T(8,128)(2,1)S(1)} %get-tuple-element.45.refs_0_.refs_1_, bf16[384,256]{1,0:T(8,128)(2,1)S(1)} %get-tuple-element.46.refs_1_, bf16[384,256]{1,0:T(8,128)(2,1)S(1)} %get-tuple-element.47.refs_2_, ...), custom_call_target="tpu_custom_call" | custom-call | bytes 1048576 | tf_op jit(solution)/shard_map/assemble/pallas_call | solution.py:247
  53.0 0.1 collective-permute-start.10
  53.1 0.0 collective-permute-done.15.near_r
  53.1 0.5 collective-permute-start.16
  53.6 1.7 %collective-permute-done.11 = bf16[384,256]{1,0:T(8,128)(2,1)S(1)} collective-permute-done((bf16[384,256]{1,0:T(8,128)(2,1)S(1)}, bf16[384,256]{1,0:T(8,128)(2,1)S(1)}, u32[]{:S(2)}, u32[]{:S(2)}) %collective-permute-start.11) | collective-permute-done | bytes 196640 | tf_op jit(solution)/shard_map/ppermute | solution.py:791
  55.2 0.0 collective-permute-start.9
  55.2 0.7 broadcast_select_fusion.refs_5_.refs_0_
  55.9 6.8 %collective-permute-done.9 = bf16[384,256]{1,0:T(8,128)(2,1)S(1)} collective-permute-done((bf16[384,256]{1,0:T(8,128)(2,1)S(1)}, bf16[384,256]{1,0:T(8,128)(2,1)S(1)}, u32[]{:S(2)}, u32[]{:S(2)}) %collective-permute-start.9) | collective-permute-done | bytes 196640 | tf_op jit(solution)/shard_map/ppermute | solution.py:791
  62.7 0.0 collective-permute-start.17
  62.7 0.7 broadcast_select_fusion.1.refs_4_
  63.4 0.0 collective-permute-done.8.tokn_r
  63.4 0.1 collective-permute-start.12
  63.5 0.0 collective-permute-done.10.gum_r
  63.5 1.8 %forward_gu.1 = (f32[384,256]{1,0:T(8,128)S(1)}, bf16[384,256]{1,0:T(8,128)(2,1)S(1)}) custom-call(bf16[1,192,4096]{2,1,0:T(8,128)(2,1)} %tok_r.3, bf16[192,2048]{1,0:T(8,128)(2,1)S(1)} %collective-permute-done.8.tokn_r, bf16[1024,256]{1,0:T(8,128)(2,1)S(1)} %assemble.2.gu_r, bf16[1024,256]{1,0:T(8,128)(2,1)S(1)} %collective-permute-done.10.gum_r), custom_call_target="tpu_custom_call" | custom-call | flops 402653184 | bytes 3145728 | tf_op jit(solution)/shard_map/forward_gu/pallas_call | solution.py:377
  65.3 1.0 collective-permute-start.13
  66.3 0.0 collective-permute-done.17.far_r
  66.3 1.8 %forward_dn.1 = (f32[384,128]{1,0:T(8,128)S(1)}, bf16[384,128]{1,0:T(8,128)(2,1)S(1)}) custom-call(bf16[1,192,4096]{2,1,0:T(8,128)(2,1)} %up_r.3, bf16[192,2048]{1,0:T(8,128)(2,1)S(1)} %collective-permute-done.14.upn_r, bf16[8,32,256]{2,1,0:T(8,128)(2,1)S(1)} %get-tuple-element.65.mine_r, bf16[8,32,256]{2,1,0:T(8,128)(2,1)S(1)} %collective-permute-done.15.near_r, ...), custom_call_target="tpu_custom_call" | custom-call | flops 201326592 | bytes 3145728 | tf_op jit(solution)/shard_map/forward_dn/pallas_call | solution.py:422
  68.1 1.1 %collective-permute-start.18 = (bf16[384,128]{1,0:T(8,128)(2,1)S(1)}, bf16[384,128]{1,0:T(8,128)(2,1)S(1)}, u32[]{:S(2)}, u32[]{:S(2)}) collective-permute-start(bf16[384,128]{1,0:T(8,128)(2,1)S(1)} %get-tuple-element.68), channel_id=1, source_target_pairs={{0,2},{2,0},{1,3},{3,1},{4,6},{6,4},{5,7},{7,5},{8,10},{10,8},{9,1... | collective-permute-start | bytes 294920 | tf_op jit(solution)/shard_map/ppermute | solution.py:814
  69.3 3.3 %collective-permute-done.12.refs_7_.refs_2_ = bf16[384,256]{1,0:T(8,128)(2,1)S(1)} collective-permute-done((bf16[384,256]{1,0:T(8,128)(2,1)S(1)}, bf16[384,256]{1,0:T(8,128)(2,1)S(1)}, u32[]{:S(2)}, u32[]{:S(2)}) %collective-permute-start.12) | collective-permute-done | bytes 196640 | tf_op jit(solution)/shard_map/ppermute | solution.py:791
  72.6 2.2 %collective-permute-done.18.dhn_r = bf16[384,128]{1,0:T(8,128)(2,1)S(1)} collective-permute-done((bf16[384,128]{1,0:T(8,128)(2,1)S(1)}, bf16[384,128]{1,0:T(8,128)(2,1)S(1)}, u32[]{:S(2)}, u32[]{:S(2)}) %collective-permute-start.18) | collective-permute-done | bytes 98336 | tf_op jit(solution)/shard_map/ppermute | solution.py:814
  74.8 3.2 %backward.1 = (f32[1024,256]{1,0:T(8,128)S(1)}, bf16[1024,256]{1,0:T(8,128)(2,1)S(1)}, f32[2,8,32,256]{3,2,1,0:T(8,128)S(1)}, bf16[2,8,32,256]{3,2,1,0:T(8,128)(2,1)S(1)}) custom-call(f32[384,256]{1,0:T(8,128)S(1)} %get-tuple-element.63.pre_r, bf16[384,256]{1,0:T(8,128)(2,1)S(1)} %collective-permute-done.13.pren_r, f32[384,128]{1,0:T(8,128)S(1)} %get-tuple-element.67.dh_r, ...), custom_call_target="tpu_custom_call" | custom-call | flops 603979776 | bytes 6291456 | tf_op jit(solution)/shard_map/backward/pallas_call | solution.py:496
  78.0 0.1 collective-permute-start.19
  78.1 0.5 collective-permute-start.25
  78.6 0.4 collective-permute-start.21
  79.0 9.2 %collective-permute-done.22.refs_4_.refs_9_ = bf16[384,256]{1,0:T(8,128)(2,1)S(1)} collective-permute-done((bf16[384,256]{1,0:T(8,128)(2,1)S(1)}, bf16[384,256]{1,0:T(8,128)(2,1)S(1)}, u32[]{:S(2)}, u32[]{:S(2)}) %collective-permute-start.22) | collective-permute-done | bytes 196640 | tf_op jit(solution)/shard_map/ppermute | solution.py:791
  88.2 3.9 %collective-permute-done.21.refs_8_.refs_3_ = bf16[384,256]{1,0:T(8,128)(2,1)S(1)} collective-permute-done((bf16[384,256]{1,0:T(8,128)(2,1)S(1)}, bf16[384,256]{1,0:T(8,128)(2,1)S(1)}, u32[]{:S(2)}, u32[]{:S(2)}) %collective-permute-start.21) | collective-permute-done | bytes 196640 | tf_op jit(solution)/shard_map/ppermute | solution.py:791
  92.1 1.0 collective-permute-start.26
  93.1 6.8 %collective-permute-done.23.refs_5_.refs_10_ = bf16[384,256]{1,0:T(8,128)(2,1)S(1)} collective-permute-done((bf16[384,256]{1,0:T(8,128)(2,1)S(1)}, bf16[384,256]{1,0:T(8,128)(2,1)S(1)}, u32[]{:S(2)}, u32[]{:S(2)}) %collective-permute-start.23) | collective-permute-done | bytes 196640 | tf_op jit(solution)/shard_map/ppermute | solution.py:791
  99.9 3.5 %update_dn.1 = (bf16[1,32,4096]{2,1,0:T(8,128)(2,1)}, f32[1,32,4096]{2,1,0:T(8,128)}, f32[1,32,4096]{2,1,0:T(8,128)}) custom-call(s32[4]{0:T(128)S(1)} %copy-done, f32[4]{0:T(128)S(1)} %copy-done.1, f32[1,32,4096]{2,1,0:T(8,128)} %m1_r.5, f32[1,32,4096]{2,1,0:T(8,128)} %m2_r.5, bf16[2,8,32,256]{3,2,1,0:T(8,128)(2,1)S(1)} %bitcast.12, ...), custom_call_target="tpu_custom_call" | custom-call | bytes 3407872 | tf_op jit(solution)/shard_map/update_dn/pallas_call | solution.py:704
  103.4 3.6 %update_gu.2 = (bf16[1,1024,256]{2,1,0:T(8,128)(2,1)}, f32[1,1024,256]{2,1,0:T(8,128)}, f32[1,1024,256]{2,1,0:T(8,128)}) custom-call(s32[4]{0:T(128)S(1)} %copy-done, f32[4]{0:T(128)S(1)} %copy-done.1, f32[1,1024,256]{2,1,0:T(8,128)} %m1_r.4, f32[1,1024,256]{2,1,0:T(8,128)} %m2_r.4, bf16[1024,256]{1,0:T(8,128)(2,1)S(1)} %assemble.2.gu_r, ...), custom_call_target="tpu_custom_call" | custom-call | bytes 3604480 | tf_op jit(solution)/shard_map/update_gu/pallas_call | solution.py:610
  107.1 3.5 %update_gu.3 = (bf16[1,1024,256]{2,1,0:T(8,128)(2,1)}, f32[1,1024,256]{2,1,0:T(8,128)}, f32[1,1024,256]{2,1,0:T(8,128)}) custom-call(s32[4]{0:T(128)S(1)} %copy-done, f32[4]{0:T(128)S(1)} %copy-done.1, f32[1,1024,256]{2,1,0:T(8,128)} %m1_r.4, f32[1,1024,256]{2,1,0:T(8,128)} %m2_r.4, ...), custom_call_target="tpu_custom_call", output_to_operand_aliasing={{0}: (14, {}), {1}: (15, {}), {2}: (16, {})} | custom-call | bytes 2162688 | tf_op jit(solution)/shard_map/update_gu/pallas_call | solution.py:610
  (21 shorter events, 0.1 us)
Async XLA Ops:
  1.8 15.0 %collective-permute-start = (bf16[384,256]{1,0:T(8,128)(2,1)S(1)}, bf16[384,256]{1,0:T(8,128)(2,1)S(1)}, u32[]{:S(2)}, u32[]{:S(2)}) collective-permute-start(bf16[384,256]{1,0:T(8,128)(2,1)S(1)} %get-tuple-element.48.refs_0_), channel_id=1, source_target_pairs={{0,4},{4,8},{8,12},{12,0},{1,5},{5,9},{9,13},{13,1},{2,6},{6,10},{... | collective-permute-start | bytes 589832 | tf_op jit(solution)/shard_map/ppermute | solution.py:762
  4.9 11.1 %collective-permute-start.1 = (bf16[384,256]{1,0:T(8,128)(2,1)S(1)}, bf16[384,256]{1,0:T(8,128)(2,1)S(1)}, u32[]{:S(2)}, u32[]{:S(2)}) collective-permute-start(bf16[384,256]{1,0:T(8,128)(2,1)S(1)} %get-tuple-element.45.refs_0_.refs_1_), channel_id=1, source_target_pairs={{0,4},{4,8},{8,12},{12,0},{1,5},{5,9},{9,13},{13,1},{2,6},{6,10},{... | collective-permute-start | bytes 589832 | tf_op jit(solution)/shard_map/ppermute | solution.py:762
  6.5 3.7 %copy-start.2 = (bf16[1,192,4096]{2,1,0:T(8,128)(2,1)S(1)}, bf16[1,192,4096]{2,1,0:T(8,128)(2,1)}, u32[]{:S(2)}) copy-start(bf16[1,192,4096]{2,1,0:T(8,128)(2,1)} %up_r.3) | copy-start | bytes 4718596
  6.5 4.4 %copy-start = (s32[4]{0:T(128)S(1)}, s32[4]{0:T(128)}, u32[]{:S(2)}) copy-start(s32[4]{0:T(128)} %winner_ref.9) | copy-start | bytes 52
  8.7 54.7 %collective-permute-start.8 = (bf16[192,2048]{1,0:T(8,128)(2,1)}, bf16[192,2048]{1,0:T(8,128)(2,1)S(1)}, u32[]{:S(2)}, u32[]{:S(2)}) collective-permute-start(bf16[192,2048]{1,0:T(8,128)(2,1)} %dynamic-slice_bitcast_fusion.1), channel_id=1, source_target_pairs={{0,2},{2,0},{1,3},{3,1},{4,6},{6,4},{5,7},{7,5},{8,10},{10,8},{9,1... | collective-permute-start | bytes 2359304 | tf_op jit(solution)/shard_map/ppermute | solution.py:764
  10.3 56.1 %collective-permute-start.14 = (bf16[192,2048]{1,0:T(8,128)(2,1)S(1)}, bf16[192,2048]{1,0:T(8,128)(2,1)S(1)}, u32[]{:S(2)}, u32[]{:S(2)}) collective-permute-start(bf16[192,2048]{1,0:T(8,128)(2,1)S(1)} %dynamic-slice_bitcast_fusion), channel_id=1, source_target_pairs={{0,2},{2,0},{1,3},{3,1},{4,6},{6,4},{5,7},{7,5},{8,10},{10,8},{9,1... | collective-permute-start | bytes 2359304 | tf_op jit(solution)/shard_map/ppermute | solution.py:766
  16.7 9.7 %collective-permute-start.3 = (bf16[384,256]{1,0:T(8,128)(2,1)S(1)}, bf16[384,256]{1,0:T(8,128)(2,1)S(1)}, u32[]{:S(2)}, u32[]{:S(2)}) collective-permute-start(bf16[384,256]{1,0:T(8,128)(2,1)S(1)} %broadcast_select_fusion.8.refs_4_.refs_3_), channel_id=1, source_target_pairs={{0,4},{4,8},{8,12},{12,0},{1,5},{5,9},{9,13},{13,1},{2,6},{6,10},{... | collective-permute-start | bytes 589832 | tf_op jit(solution)/shard_map/ppermute | solution.py:791
  17.5 12.1 %collective-permute-start.2 = (bf16[384,256]{1,0:T(8,128)(2,1)S(1)}, bf16[384,256]{1,0:T(8,128)(2,1)S(1)}, u32[]{:S(2)}, u32[]{:S(2)}) collective-permute-start(bf16[384,256]{1,0:T(8,128)(2,1)S(1)} %broadcast_select_fusion.9.refs_3_.refs_2_), channel_id=1, source_target_pairs={{0,4},{4,8},{8,12},{12,0},{1,5},{5,9},{9,13},{13,1},{2,6},{6,10},{... | collective-permute-start | bytes 589832 | tf_op jit(solution)/shard_map/ppermute | solution.py:791
  27.1 9.6 %collective-permute-start.5 = (bf16[384,256]{1,0:T(8,128)(2,1)S(1)}, bf16[384,256]{1,0:T(8,128)(2,1)S(1)}, u32[]{:S(2)}, u32[]{:S(2)}) collective-permute-start(bf16[384,256]{1,0:T(8,128)(2,1)S(1)} %broadcast_select_fusion.6.refs_6_.refs_5_), channel_id=1, source_target_pairs={{0,4},{4,8},{8,12},{12,0},{1,5},{5,9},{9,13},{13,1},{2,6},{6,10},{... | collective-permute-start | bytes 589832 | tf_op jit(solution)/shard_map/ppermute | solution.py:791
  30.2 10.6 %collective-permute-start.4 = (bf16[384,256]{1,0:T(8,128)(2,1)S(1)}, bf16[384,256]{1,0:T(8,128)(2,1)S(1)}, u32[]{:S(2)}, u32[]{:S(2)}) collective-permute-start(bf16[384,256]{1,0:T(8,128)(2,1)S(1)} %broadcast_select_fusion.7.refs_5_.refs_4_), channel_id=1, source_target_pairs={{0,4},{4,8},{8,12},{12,0},{1,5},{5,9},{9,13},{13,1},{2,6},{6,10},{... | collective-permute-start | bytes 589832 | tf_op jit(solution)/shard_map/ppermute | solution.py:791
  37.4 9.6 %collective-permute-start.7 = (bf16[384,256]{1,0:T(8,128)(2,1)S(1)}, bf16[384,256]{1,0:T(8,128)(2,1)S(1)}, u32[]{:S(2)}, u32[]{:S(2)}) collective-permute-start(bf16[384,256]{1,0:T(8,128)(2,1)S(1)} %broadcast_select_fusion.4.refs_8_.refs_7_.refs_1_), channel_id=1, source_target_pairs={{0,4},{4,8},{8,12},{12,0},{1,5},{5,9},{9,13},{13,1},{2,6},{6,10},{... | collective-permute-start | bytes 589832 | tf_op jit(solution)/shard_map/ppermute | solution.py:791
  42.4 8.6 %collective-permute-start.6 = (bf16[384,256]{1,0:T(8,128)(2,1)S(1)}, bf16[384,256]{1,0:T(8,128)(2,1)S(1)}, u32[]{:S(2)}, u32[]{:S(2)}) collective-permute-start(bf16[384,256]{1,0:T(8,128)(2,1)S(1)} %broadcast_select_fusion.5.refs_7_.refs_6_.refs_0_), channel_id=1, source_target_pairs={{0,4},{4,8},{8,12},{12,0},{1,5},{5,9},{9,13},{13,1},{2,6},{6,10},{... | collective-permute-start | bytes 589832 | tf_op jit(solution)/shard_map/ppermute | solution.py:791
  42.5 10.6 %collective-permute-start.15 = (bf16[8,32,256]{2,1,0:T(8,128)(2,1)S(1)}, bf16[8,32,256]{2,1,0:T(8,128)(2,1)S(1)}, u32[]{:S(2)}, u32[]{:S(2)}) collective-permute-start(bf16[8,32,256]{2,1,0:T(8,128)(2,1)S(1)} %get-tuple-element.84), channel_id=1, source_target_pairs={{0,2},{2,0},{1,3},{3,1},{4,6},{6,4},{5,7},{7,5},{8,10},{10,8},{9,1... | collective-permute-start | bytes 393224 | tf_op jit(solution)/shard_map/ppermute | solution.py:799
  47.7 7.5 %collective-permute-start.11 = (bf16[384,256]{1,0:T(8,128)(2,1)S(1)}, bf16[384,256]{1,0:T(8,128)(2,1)S(1)}, u32[]{:S(2)}, u32[]{:S(2)}) collective-permute-start(bf16[384,256]{1,0:T(8,128)(2,1)S(1)} %broadcast_select_fusion.2.refs_10_.refs_3_), channel_id=1, source_target_pairs={{0,4},{4,8},{8,12},{12,0},{1,5},{5,9},{9,13},{13,1},{2,6},{6,10},{... | collective-permute-start | bytes 589832 | tf_op jit(solution)/shard_map/ppermute | solution.py:791
  53.0 10.5 %collective-permute-start.10 = (bf16[1024,256]{1,0:T(8,128)(2,1)S(1)}, bf16[1024,256]{1,0:T(8,128)(2,1)S(1)}, u32[]{:S(2)}, u32[]{:S(2)}) collective-permute-start(bf16[1024,256]{1,0:T(8,128)(2,1)S(1)} %assemble.2.gu_r), channel_id=1, source_target_pairs={{0,1},{1,0},{2,3},{3,2},{4,5},{5,4},{6,7},{7,6},{8,9},{9,8},{10,11... | collective-permute-start | bytes 1572872 | tf_op jit(solution)/shard_map/ppermute | solution.py:806
  53.1 13.2 %collective-permute-start.16 = (bf16[8,32,256]{2,1,0:T(8,128)(2,1)S(1)}, bf16[8,32,256]{2,1,0:T(8,128)(2,1)S(1)}, u32[]{:S(2)}, u32[]{:S(2)}) collective-permute-start(bf16[8,32,256]{2,1,0:T(8,128)(2,1)S(1)} %get-tuple-element.65.mine_r), channel_id=1, source_target_pairs={{0,1},{1,0},{2,3},{3,2},{4,5},{5,4},{6,7},{7,6},{8,9},{9,8},{10,11... | collective-permute-start | bytes 393224 | tf_op jit(solution)/shard_map/ppermute | solution.py:800
  55.2 7.5 %collective-permute-start.9 = (bf16[384,256]{1,0:T(8,128)(2,1)S(1)}, bf16[384,256]{1,0:T(8,128)(2,1)S(1)}, u32[]{:S(2)}, u32[]{:S(2)}) collective-permute-start(bf16[384,256]{1,0:T(8,128)(2,1)S(1)} %broadcast_select_fusion.3.refs_9_.refs_2_), channel_id=1, source_target_pairs={{0,4},{4,8},{8,12},{12,0},{1,5},{5,9},{9,13},{13,1},{2,6},{6,10},{... | collective-permute-start | bytes 589832 | tf_op jit(solution)/shard_map/ppermute | solution.py:791
  62.7 3.6 %collective-permute-start.17 = (bf16[8,32,256]{2,1,0:T(8,128)(2,1)S(1)}, bf16[8,32,256]{2,1,0:T(8,128)(2,1)S(1)}, u32[]{:S(2)}, u32[]{:S(2)}) collective-permute-start(bf16[8,32,256]{2,1,0:T(8,128)(2,1)S(1)} %collective-permute-done.15.near_r), channel_id=1, source_target_pairs={{0,1},{1,0},{2,3},{3,2},{4,5},{5,4},{6,7},{7,6},{8,9},{9,8},{10,11... | collective-permute-start | bytes 393224 | tf_op jit(solution)/shard_map/ppermute | solution.py:803
  63.4 9.2 %collective-permute-start.12 = (bf16[384,256]{1,0:T(8,128)(2,1)S(1)}, bf16[384,256]{1,0:T(8,128)(2,1)S(1)}, u32[]{:S(2)}, u32[]{:S(2)}) collective-permute-start(bf16[384,256]{1,0:T(8,128)(2,1)S(1)} %broadcast_select_fusion.refs_5_.refs_0_), channel_id=1, source_target_pairs={{0,4},{4,8},{8,12},{12,0},{1,5},{5,9},{9,13},{13,1},{2,6},{6,10},{... | collective-permute-start | bytes 589832 | tf_op jit(solution)/shard_map/ppermute | solution.py:791
  65.3 9.5 %collective-permute-start.13 = (bf16[384,256]{1,0:T(8,128)(2,1)S(1)}, bf16[384,256]{1,0:T(8,128)(2,1)S(1)}, u32[]{:S(2)}, u32[]{:S(2)}) collective-permute-start(bf16[384,256]{1,0:T(8,128)(2,1)S(1)} %get-tuple-element.64), channel_id=1, source_target_pairs={{0,2},{2,0},{1,3},{3,1},{4,6},{6,4},{5,7},{7,5},{8,10},{10,8},{9,1... | collective-permute-start | bytes 589832 | tf_op jit(solution)/shard_map/ppermute | solution.py:809
  68.1 6.7 %collective-permute-start.18 = (bf16[384,128]{1,0:T(8,128)(2,1)S(1)}, bf16[384,128]{1,0:T(8,128)(2,1)S(1)}, u32[]{:S(2)}, u32[]{:S(2)}) collective-permute-start(bf16[384,128]{1,0:T(8,128)(2,1)S(1)} %get-tuple-element.68), channel_id=1, source_target_pairs={{0,2},{2,0},{1,3},{3,1},{4,6},{6,4},{5,7},{7,5},{8,10},{10,8},{9,1... | collective-permute-start | bytes 294920 | tf_op jit(solution)/shard_map/ppermute | solution.py:814
  69.3 9.3 %collective-permute-start.20 = (bf16[384,256]{1,0:T(8,128)(2,1)S(1)}, bf16[384,256]{1,0:T(8,128)(2,1)S(1)}, u32[]{:S(2)}, u32[]{:S(2)}) collective-permute-start(bf16[384,256]{1,0:T(8,128)(2,1)S(1)} %broadcast_select_fusion.1.refs_4_), channel_id=1, source_target_pairs={{0,4},{4,8},{8,12},{12,0},{1,5},{5,9},{9,13},{13,1},{2,6},{6,10},{... | collective-permute-start | bytes 589832 | tf_op jit(solution)/shard_map/ppermute | solution.py:791
  74.8 25.1 %copy-start.1 = (f32[4]{0:T(128)S(1)}, f32[4]{0:T(128)}, u32[]{:S(2)}) copy-start(f32[4]{0:T(128)} %rate_ref.5) | copy-start | bytes 52
  78.0 25.4 %collective-permute-start.19 = (bf16[1024,256]{1,0:T(8,128)(2,1)S(1)}, bf16[1024,256]{1,0:T(8,128)(2,1)S(1)}, u32[]{:S(2)}, u32[]{:S(2)}) collective-permute-start(bf16[1024,256]{1,0:T(8,128)(2,1)S(1)} %get-tuple-element.70), channel_id=1, source_target_pairs={{0,1},{1,0},{2,3},{3,2},{4,5},{5,4},{6,7},{7,6},{8,9},{9,8},{10,11... | collective-permute-start | bytes 1572872 | tf_op jit(solution)/shard_map/ppermute | solution.py:819
  78.1 13.9 %collective-permute-start.25 = (bf16[2,8,32,256]{3,2,1,0:T(8,128)(2,1)S(1)}, bf16[2,8,32,256]{3,2,1,0:T(8,128)(2,1)S(1)}, u32[]{:S(2)}, u32[]{:S(2)}) collective-permute-start(bf16[2,8,32,256]{3,2,1,0:T(8,128)(2,1)S(1)} %get-tuple-element.77), channel_id=1, source_target_pairs={{0,1},{1,0},{2,3},{3,2},{4,5},{5,4},{6,7},{7,6},{8,9},{9,8},{10,11... | collective-permute-start | bytes 786440 | tf_op jit(solution)/shard_map/ppermute | solution.py:820
  78.6 9.6 %collective-permute-start.22 = (bf16[384,256]{1,0:T(8,128)(2,1)S(1)}, bf16[384,256]{1,0:T(8,128)(2,1)S(1)}, u32[]{:S(2)}, u32[]{:S(2)}) collective-permute-start(bf16[384,256]{1,0:T(8,128)(2,1)S(1)} %collective-permute-done.12.refs_7_.refs_2_), channel_id=1, source_target_pairs={{0,4},{4,8},{8,12},{12,0},{1,5},{5,9},{9,13},{13,1},{2,6},{6,10},{... | collective-permute-start | bytes 589832 | tf_op jit(solution)/shard_map/ppermute | solution.py:791
  78.6 13.4 %collective-permute-start.21 = (bf16[384,256]{1,0:T(8,128)(2,1)S(1)}, bf16[384,256]{1,0:T(8,128)(2,1)S(1)}, u32[]{:S(2)}, u32[]{:S(2)}) collective-permute-start(bf16[384,256]{1,0:T(8,128)(2,1)S(1)} %collective-permute-done.20.refs_6_.refs_1_), channel_id=1, source_target_pairs={{0,4},{4,8},{8,12},{12,0},{1,5},{5,9},{9,13},{13,1},{2,6},{6,10},{... | collective-permute-start | bytes 589832 | tf_op jit(solution)/shard_map/ppermute | solution.py:791
  88.2 11.8 %collective-permute-start.24 = (bf16[384,256]{1,0:T(8,128)(2,1)S(1)}, bf16[384,256]{1,0:T(8,128)(2,1)S(1)}, u32[]{:S(2)}, u32[]{:S(2)}) collective-permute-start(bf16[384,256]{1,0:T(8,128)(2,1)S(1)} %collective-permute-done.22.refs_4_.refs_9_), channel_id=1, source_target_pairs={{0,4},{4,8},{8,12},{12,0},{1,5},{5,9},{9,13},{13,1},{2,6},{6,10},{... | collective-permute-start | bytes 589832 | tf_op jit(solution)/shard_map/ppermute | solution.py:791
  92.0 7.9 %collective-permute-start.23 = (bf16[384,256]{1,0:T(8,128)(2,1)S(1)}, bf16[384,256]{1,0:T(8,128)(2,1)S(1)}, u32[]{:S(2)}, u32[]{:S(2)}) collective-permute-start(bf16[384,256]{1,0:T(8,128)(2,1)S(1)} %collective-permute-done.21.refs_8_.refs_3_), channel_id=1, source_target_pairs={{0,4},{4,8},{8,12},{12,0},{1,5},{5,9},{9,13},{13,1},{2,6},{6,10},{... | collective-permute-start | bytes 589832 | tf_op jit(solution)/shard_map/ppermute | solution.py:791
  92.1 7.9 %collective-permute-start.26 = (bf16[8,32,256]{2,1,0:T(8,128)(2,1)S(1)}, bf16[8,32,256]{2,1,0:T(8,128)(2,1)S(1)}, u32[]{:S(2)}, u32[]{:S(2)}) collective-permute-start(bf16[8,32,256]{2,1,0:T(8,128)(2,1)S(1)} %fusion), channel_id=1, source_target_pairs={{0,2},{2,0},{1,3},{3,1},{4,6},{6,4},{5,7},{7,5},{8,10},{10,8},{9,1... | collective-permute-start | bytes 393224 | tf_op jit(solution)/shard_map/ppermute | solution.py:826

commit v4 on v3

--- a/solution.py
+++ b/solution.py
@@ -159,12 +159,12 @@
 M_CHUNKS = 8
 CHUNKS = W_CHUNKS + M_CHUNKS
 EARLY = 5
+NEAR_AT = 8
 GU_AT = 10
 DN_AT = 11
-BACK_AT = 13
-FAR_AT = 9
+BACK_AT = 14
 SUM_AT = 15
-EARLY_AT = 16
+EARLY_AT = 15
 
 
 def grant(mib):
@@ -552,52 +552,45 @@
             pltpu.make_async_copy(a, b, sems.at[n, k]).wait()
 
 
-def update_gu(winner, learning, low, high, m1, m2, held, gu, g_own, g_got, done):
-    members = winner.shape[0]
-    _, rows, cols = m1.shape
-    part = rows // M_CHUNKS
-    each = held[0].shape[0] // 2
-    count = high - low
-    start, size = low * part, (high - low) * part
-    f32, bf16 = jnp.float32, jnp.bfloat16
-    span = pl.ds(start, size)
-
-    def kernel(winner_ref, rate_ref, m1_r, m2_r, gu_r, go_r, gm_r, *refs):
-        came = refs[: len(held)]
-        refs = refs[len(held) + len(done) :]
-        n_w, n_1, n_2, bgu, bgo, bgm, own, moved, o_w, o_1, o_2, sems, msems, osems = refs
-        mode = mode_of(winner_ref, members)
-        rate = rate_ref[winner_ref[lax.axis_index("member")]]
-        own_pairs = [
+def gate_up_rows(mode, rate, members, low, high, each, ins, came, outs, scratch):
+    m1_r, m2_r, gu_r, go_r, gm_r = ins
+    n_w, n_1, n_2 = outs
+    bgu, bgo, bgm, own, moved, o_w, o_1, o_2, sems, msems, osems = scratch
+    part = m1_r.shape[1] // M_CHUNKS
+    start, count = low * part, high - low
+    span = pl.ds(start, count * part)
+    own_pairs = [
+        [
+            (m1_r.at[0, pl.ds(start + n * part, part)], own.at[0, pl.ds(n * part, part)]),
+            (m2_r.at[0, pl.ds(start + n * part, part)], own.at[1, pl.ds(n * part, part)]),
+        ]
+        for n in range(count)
+    ]
+    came_pairs = [
+        [
             [
-                (m1_r.at[0, pl.ds(start + n * part, part)], own.at[0, pl.ds(n * part, part)]),
-                (m2_r.at[0, pl.ds(start + n * part, part)], own.at[1, pl.ds(n * part, part)]),
+                (came[low + n + STAGGER * hop].at[pl.ds(0, part)], moved.at[n, 0]),
+                (came[low + n + STAGGER * hop].at[pl.ds(each, part)], moved.at[n, 1]),
             ]
             for n in range(count)
         ]
-        came_pairs = [
-            [
-                [
-                    (came[n + STAGGER * hop].at[pl.ds(0, part)], moved.at[n, 0]),
-                    (came[n + STAGGER * hop].at[pl.ds(each, part)], moved.at[n, 1]),
-                ]
-                for n in range(count)
-            ]
-            for hop in range(members - 1)
-        ]
-        copies = start_all([(gu_r.at[span], bgu), (go_r.at[span], bgo), (gm_r.at[span], bgm)], sems)
-        start_moments(mode, members, own_pairs, came_pairs, msems)
+        for hop in range(members - 1)
+    ]
+    copies = start_all([(gu_r.at[span], bgu), (go_r.at[span], bgo), (gm_r.at[span], bgm)], sems)
+    start_moments(mode, members, own_pairs, came_pairs, msems)
+
+    def finish():
         wait_all(copies)
-        outs = []
+        sent = []
         for n in range(count):
             wait_moments(mode, n, own_pairs, came_pairs, msems)
             at = slice(n * part, (n + 1) * part)
-            first = jnp.where(mode == 0, own[0, at], moved[n, 0].astype(f32))
-            second = jnp.where(mode == 0, own[1, at], moved[n, 1].astype(f32))
-            grad = bgo[at] + bgm[at].astype(f32)
+            first = jnp.where(mode == 0, own[0, at], moved[n, 0].astype(jnp.float32))
+            second = jnp.where(mode == 0, own[1, at], moved[n, 1].astype(jnp.float32))
+            grad = bgo[at] + bgm[at].astype(jnp.float32)
             o_w[at], o_1[at], o_2[at] = adamw_part(bgu[at], grad, first, second, rate)
             here, there = pl.ds(n * part, part), pl.ds(start + n * part, part)
-            outs += start_all(
+            sent += start_all(
                 [
                     (o_w.at[here], n_w.at[0, there]),
                     (o_1.at[here], n_1.at[0, there]),
@@ -605,126 +598,143 @@
                 ],
                 osems.at[n],
             )
-        wait_all(outs)
-
-    return pl.pallas_call(
-        kernel,
-        out_shape=tuple(jax.ShapeDtypeStruct((1, rows, cols), t) for t in (bf16, f32, f32)),
-        in_specs=[SMEM, SMEM] + [ANY] * (5 + len(held) + len(done)),
-        out_specs=(ANY,) * 3,
-        scratch_shapes=[
-            pltpu.VMEM((size, cols), bf16),
-            pltpu.VMEM((size, cols), f32),
-            pltpu.VMEM((size, cols), bf16),
-            pltpu.VMEM((2, size, cols), f32),
-            pltpu.VMEM((count, 2, part, cols), bf16),
-            pltpu.VMEM((size, cols), bf16),
-            pltpu.VMEM((size, cols), f32),
-            pltpu.VMEM((size, cols), f32),
-            pltpu.SemaphoreType.DMA((3,)),
-            pltpu.SemaphoreType.DMA((count, 2)),
-            pltpu.SemaphoreType.DMA((count, 3)),
-        ],
-        input_output_aliases={7 + len(held) + n: n for n in range(len(done))},
-        compiler_params=grant(12),
-        cost_estimate=cost(0, 22 * size * cols),
-        name="update_gu",
-    )(winner, learning, *in_hbm(m1, m2), *in_vmem(gu, g_own, g_got, *held), *done)
-
-
-def update_dn(winner, learning, m1, m2, held, dn, d_own, d_got, d_back):
-    members = winner.shape[0]
-    _, rows, width = m1.shape
-    _, blocks, _, cols = dn.shape
-    each = held[0].shape[0] // 2
+        return sent
+
+    return finish
+
+
+def down_rows(mode, rate, members, each, ins, came, outs, scratch):
+    m1_r, m2_r, dn_r, do_r, dm_r, gb_r = ins
+    n_w, n_1, n_2 = outs
+    bdn, bdo, bdm, bgb, grad, own, moved, o_w, o_1, o_2, sems, msems, osems = scratch
+    _, rows, width = m1_r.shape
+    _, blocks, _, cols = dn_r.shape
     per = 2 * blocks // M_CHUNKS
     size = per * rows
     base = each - size
-    f32, bf16 = jnp.float32, jnp.bfloat16
-
-    def kernel(winner_ref, rate_ref, m1_r, m2_r, dn_r, do_r, dm_r, gb_r, *refs):
-        came = refs[: len(held)]
-        n_w, n_1, n_2, bdn, bdo, bdm, bgb, grad, own, moved, o_w, o_1, o_2, sems, msems, osems = refs[len(held) :]
-        chip, _ = chip_and_core()
-        mode = mode_of(winner_ref, members)
-        rate = rate_ref[winner_ref[lax.axis_index("member")]]
-        own_pairs = [
+    chip, _ = chip_and_core()
+    spans = [pl.ds(n * per * cols, per * cols) for n in range(M_CHUNKS)]
+    own_pairs = [
+        [(m1_r.at[0, :, span], own.at[0, :, span]), (m2_r.at[0, :, span], own.at[1, :, span])]
+        for span in spans
+    ]
+    came_pairs = [
+        [
             [
-                (m1_r.at[0, :, pl.ds(n * per * cols, per * cols)], own.at[0, :, pl.ds(n * per * cols, per * cols)]),
-                (m2_r.at[0, :, pl.ds(n * per * cols, per * cols)], own.at[1, :, pl.ds(n * per * cols, per * cols)]),
+                (came[n + STAGGER * hop].at[pl.ds(base, size)], moved.at[n, 0]),
+                (came[n + STAGGER * hop].at[pl.ds(each + base, size)], moved.at[n, 1]),
             ]
             for n in range(M_CHUNKS)
         ]
-        came_pairs = [
-            [
-                [
-                    (came[n + STAGGER * hop].at[pl.ds(base, size)], moved.at[n, 0]),
-                    (came[n + STAGGER * hop].at[pl.ds(each + base, size)], moved.at[n, 1]),
-                ]
-                for n in range(M_CHUNKS)
-            ]
-            for hop in range(members - 1)
-        ]
-        copies = start_all(
-            [
-                (dn_r, bdn),
-                (do_r.at[chip], bdo),
-                (dm_r.at[chip], bdm),
-                (gb_r, bgb),
-            ],
-            sems,
-        )
-        start_moments(mode, members, own_pairs, came_pairs, msems)
+        for hop in range(members - 1)
+    ]
+    copies = start_all([(dn_r, bdn), (do_r.at[chip], bdo), (dm_r.at[chip], bdm), (gb_r, bgb)], sems)
+    start_moments(mode, members, own_pairs, came_pairs, msems)
+
+    def finish():
         wait_all(copies)
-        grad[chip] = bdo[...] + bdm[...].astype(f32)
-        grad[1 - chip] = bgb[...].astype(f32)
-        outs = []
+        grad[chip] = bdo[...] + bdm[...].astype(jnp.float32)
+        grad[1 - chip] = bgb[...].astype(jnp.float32)
+        sent = []
         for n in range(M_CHUNKS):
             wait_moments(mode, n, own_pairs, came_pairs, msems)
             for i in range(per):
                 at = slice((n * per + i) * cols, (n * per + i + 1) * cols)
                 sub = slice(i * rows, (i + 1) * rows)
-                first = jnp.where(mode == 0, own[0, :, at], moved[n, 0, sub].astype(f32))
-                second = jnp.where(mode == 0, own[1, :, at], moved[n, 1, sub].astype(f32))
+                first = jnp.where(mode == 0, own[0, :, at], moved[n, 0, sub].astype(jnp.float32))
+                second = jnp.where(mode == 0, own[1, :, at], moved[n, 1, sub].astype(jnp.float32))
                 side, b = divmod(n * per + i, blocks)
-                o_w[:, at], o_1[:, at], o_2[:, at] = adamw_part(bdn[side, b], grad[side, b], first, second, rate)
-            if n % 4 == 3:
-                at = pl.ds((n - 3) * per * cols, 4 * per * cols)
-                outs += start_all(
+                o_w[:, at], o_1[:, at], o_2[:, at] = adamw_part(
+                    bdn[side, b], grad[side, b], first, second, rate
+                )
+            if n % 2 == 1:
+                at = pl.ds((n - 1) * per * cols, 2 * per * cols)
+                sent += start_all(
                     [
                         (o_w.at[:, at], n_w.at[0, :, at]),
                         (o_1.at[:, at], n_1.at[0, :, at]),
                         (o_2.at[:, at], n_2.at[0, :, at]),
                     ],
-                    osems.at[n // 4],
+                    osems.at[n // 2],
                 )
-        wait_all(outs)
-
-    half = (blocks, rows, cols)
-    return pl.pallas_call(
-        kernel,
-        out_shape=tuple(jax.ShapeDtypeStruct((1, rows, width), t) for t in (bf16, f32, f32)),
-        in_specs=[SMEM, SMEM] + [ANY] * (6 + len(held)),
-        out_specs=(ANY,) * 3,
-        scratch_shapes=[
+        return sent
+
+    return finish
+
+
+def update(winner, learning, low, high, held, gate_up_side, done=(), down_side=()):
+    members = winner.shape[0]
+    m1, m2, gu, g_own, g_got = gate_up_side
+    _, rows, cols = m1.shape
+    part = rows // M_CHUNKS
+    each = held[0].shape[0] // 2
+    count = high - low
+    size = count * part
+    f32, bf16 = jnp.float32, jnp.bfloat16
+    scratch = [
+        pltpu.VMEM((size, cols), bf16),
+        pltpu.VMEM((size, cols), f32),
+        pltpu.VMEM((size, cols), bf16),
+        pltpu.VMEM((2, size, cols), f32),
+        pltpu.VMEM((count, 2, part, cols), bf16),
+        pltpu.VMEM((size, cols), bf16),
+        pltpu.VMEM((size, cols), f32),
+        pltpu.VMEM((size, cols), f32),
+        pltpu.SemaphoreType.DMA((3,)),
+        pltpu.SemaphoreType.DMA((count, 2)),
+        pltpu.SemaphoreType.DMA((count, 3)),
+    ]
+    shapes = [jax.ShapeDtypeStruct((1, rows, cols), t) for t in (bf16, f32, f32)]
+    operands = [*in_hbm(m1, m2), *in_vmem(gu, g_own, g_got)]
+    if down_side:
+        n1, n2, dn, d_own, d_got, d_back = down_side
+        _, rows_dn, width = n1.shape
+        half = dn.shape[1:]
+        moved = (width // cols // M_CHUNKS) * rows_dn
+        scratch += [
             pltpu.VMEM((2,) + half, bf16),
             pltpu.VMEM(half, f32),
             pltpu.VMEM(half, bf16),
             pltpu.VMEM(half, bf16),
             pltpu.VMEM((2,) + half, f32),
-            pltpu.VMEM((2, rows, width), f32),
-            pltpu.VMEM((M_CHUNKS, 2, size, cols), bf16),
-            pltpu.VMEM((rows, width), bf16),
-            pltpu.VMEM((rows, width), f32),
-            pltpu.VMEM((rows, width), f32),
+            pltpu.VMEM((2, rows_dn, width), f32),
+            pltpu.VMEM((M_CHUNKS, 2, moved, cols), bf16),
+            pltpu.VMEM((rows_dn, width), bf16),
+            pltpu.VMEM((rows_dn, width), f32),
+            pltpu.VMEM((rows_dn, width), f32),
             pltpu.SemaphoreType.DMA((4,)),
             pltpu.SemaphoreType.DMA((M_CHUNKS, 2)),
-            pltpu.SemaphoreType.DMA((M_CHUNKS // 4, 3)),
-        ],
-        compiler_params=grant(10),
-        cost_estimate=cost(0, 26 * rows * width),
-        name="update_dn",
-    )(winner, learning, *in_hbm(m1, m2), *in_vmem(dn, d_own, d_got, d_back, *held))
+            pltpu.SemaphoreType.DMA((M_CHUNKS // 2, 3)),
+        ]
+        shapes += [jax.ShapeDtypeStruct((1, rows_dn, width), t) for t in (bf16, f32, f32)]
+        operands += [*in_hbm(n1, n2), *in_vmem(dn, d_own, d_got, d_back)]
+    fixed = len(operands)
+
+    def kernel(winner_ref, rate_ref, *refs):
+        ins, refs = refs[:fixed], refs[fixed:]
+        came, refs = refs[: len(held)], refs[len(held) + len(done) :]
+        outs, temps = refs[: len(shapes)], refs[len(shapes) :]
+        mode = mode_of(winner_ref, members)
+        rate = rate_ref[winner_ref[lax.axis_index("member")]]
+        finish = [
+            gate_up_rows(mode, rate, members, low, high, each, ins[:5], came, outs[:3], temps[:11])
+        ]
+        if down_side:
+            finish.append(down_rows(mode, rate, members, each, ins[5:], came, outs[3:], temps[11:]))
+        sent = [copy for part in finish for copy in part()]
+        wait_all(sent)
+
+    return pl.pallas_call(
+        kernel,
+        out_shape=tuple(shapes),
+        in_specs=[SMEM, SMEM] + [ANY] * (fixed + len(held) + len(done)),
+        out_specs=(ANY,) * len(shapes),
+        scratch_shapes=scratch,
+        input_output_aliases={2 + fixed + len(held) + n: n for n in range(len(done))},
+        compiler_params=grant(16),
+        cost_estimate=cost(0, 22 * size * cols),
+        name="update",
+    )(winner, learning, *operands, *in_vmem(*held), *done)
 
 
 def on_device_four(
@@ -745,6 +755,7 @@
     chip = fsdp_index // 2
     over_x = [(0, 2), (2, 0), (1, 3), (3, 1)]
     over_core = [(0, 1), (1, 0), (2, 3), (3, 2)]
+    over_both = [(0, 3), (3, 0), (1, 2), (2, 1)]
     ring = [(i, (i + 1) % members) for i in range(members)]
     half = tokens.shape[2] // 2
     _, rows_gu, cols = gate_up.shape
@@ -764,7 +775,6 @@
     tok_near = lax.ppermute(tok_theirs, "fsdp", over_x)
     up_theirs = theirs(after(grad_out, tok_theirs))
     up_near = lax.ppermute(up_theirs, "fsdp", over_x)
-    got[0] = after(got[0], up_theirs)
 
     def rows_from(low, high):
         pieces = []
@@ -780,13 +790,16 @@
 
     rows_d = down.size // cols
     held = []
+    gap = [up_theirs]
     last = STAGGER * (members - 2)
     pre = dh = grads = first_gu = None
     for step in range(STAGGER, CHUNKS + last + STAGGER):
-        back = got[step - STAGGER]
+        back = after(got[step - STAGGER], *gap)
+        gap = []
         if step < CHUNKS:
             back = jnp.where(is_source, own[step], back)
         held.append(back)
+        gap = [back]
         if step < CHUNKS + last:
             got.append(lax.ppermute(back, "member", ring))
         if step == STAGGER:
@@ -798,9 +811,9 @@
             dn_theirs = lax.dynamic_index_in_dim(dn, 1 - chip, axis=0, keepdims=False)
             dn_near = lax.ppermute(dn_theirs, "fsdp", over_x)
             dn_mate = lax.ppermute(dn_mine, "fsdp", over_core)
-        if step == FAR_AT:
-            dn_near = after(dn_near, back)
-            dn_far = lax.ppermute(dn_near, "fsdp", over_core)
+            dn_far = lax.ppermute(dn_theirs, "fsdp", over_both)
+        if step == NEAR_AT:
+            gap += [dn_near, dn_far, dn_mate]
         if ready == W_CHUNKS - 1:
             gu = take(rows_d, rows_all)
             gu_mate = lax.ppermute(gu, "fsdp", over_core)
@@ -825,17 +838,25 @@
             ).astype(jnp.bfloat16)
             d_back = lax.ppermute(d_there, "fsdp", over_x)
         if step == EARLY_AT:
-            first_gu = update_gu(
-                winner, learning, 0, EARLY, mom1_gate_up, mom2_gate_up,
-                held[W_CHUNKS : W_CHUNKS + EARLY + last], after(gu, back), g_own, g_got, ()
+            first_gu = update(
+                winner,
+                learning,
+                0,
+                EARLY,
+                held[W_CHUNKS : W_CHUNKS + EARLY + last],
+                (mom1_gate_up, mom2_gate_up, after(gu, back), g_own, g_got),
             )
-
-    new_gu, new_first_gu, new_second_gu = update_gu(
-        winner, learning, EARLY, M_CHUNKS, mom1_gate_up, mom2_gate_up,
-        held[W_CHUNKS + EARLY :], gu, g_own, g_got, first_gu
-    )
-    new_dn, new_first_dn, new_second_dn = update_dn(
-        winner, learning, mom1_down, mom2_down, held[W_CHUNKS:], dn, d_own, d_got, d_back
+            gap = list(first_gu)
+
+    new_gu, new_first_gu, new_second_gu, new_dn, new_first_dn, new_second_dn = update(
+        winner,
+        learning,
+        EARLY,
+        M_CHUNKS,
+        held[W_CHUNKS:],
+        (mom1_gate_up, mom2_gate_up, gu, g_own, g_got),
+        first_gu,
+        (mom1_down, mom2_down, dn, d_own, d_got, d_back),
     )
     return (new_gu, new_dn, new_first_gu, new_second_gu, new_first_dn, new_second_dn)
 

time: 111 us -> 99.6 us (0.90)
  waiting for transfers between devices: 62.7 us -> 49.9 us
  starting transfers between devices: 14.2 us -> 17.6 us
  Pallas kernels: 23.1 us -> 21.3 us
    ppermute x14, waiting for transfers between devices: 55.9 us -> 39.3 us  [on_device_four(): got.append(lax.ppermute(back, 'member', ring))]
    ppermute x1, waiting for transfers between devices: 0.01 us -> 3.39 us  [on_device_four(): dn_near = lax.ppermute(dn_theirs, 'fsdp', over_x)]
    ppermute x14, starting transfers between devices: 2.09 us -> 4.23 us  [on_device_four(): got.append(lax.ppermute(back, 'member', ring))]
    pallas_call x3 -> x2, Pallas kernels: 10.6 us -> 8.71 us  [update(): pl.pallas_call(kernel, out_shape=tuple(shapes), in_specs=[SMEM, SMEM] + [...]
    ppermute x1, waiting for transfers between devices: 2.24 us -> 1.1 us  [on_device_four(): dh_near = lax.ppermute(dh_sent, 'fsdp', over_x)]
  transfers between devices with their start and end apart: 27 -> 27, of which waited for: 14 -> 17; matrix products, arithmetic and copies ran while one was open for 9% -> 10% of each run, Pallas kernels for 13% -> 12%
where the time goes in v4:
time: 99.6 us; the launch traced here: 99.2 us
  waiting for transfers between devices  49.9 us (50%)
  Pallas kernels  21.3 us (21%)
  starting transfers between devices  17.6 us (18%)
  other arithmetic  7.36 us (7%)
  local copies, waits for them, and re-layouts  2.18 us (2%)
    ppermute x14, waiting for transfers between devices, on_device_four(): got.append(lax.ppermute(back, 'member', ring))  39.3 us
    pallas_call x2, Pallas kernels, update(): pl.pallas_call(kernel, out_shape=tuple(shapes), in_specs=[SMEM, SMEM] + [...  8.71 us
    select_n x10, other arithmetic, on_device_four(): back = jnp.where(is_source, own[step], back)  6.7 us
    ppermute x2, starting transfers between devices, on_device_four(): got = [lax.ppermute(chunk, 'member', ring) for chunk in own[:STAGGER]]  4.65 us
    ppermute x2, waiting for transfers between devices, on_device_four(): got = [lax.ppermute(chunk, 'member', ring) for chunk in own[:STAGGER]]  4.52 us
    ppermute x14, starting transfers between devices, on_device_four(): got.append(lax.ppermute(back, 'member', ring))  4.23 us
    ppermute x1, waiting for transfers between devices, on_device_four(): dn_near = lax.ppermute(dn_theirs, 'fsdp', over_x)  3.39 us
    pallas_call x1, Pallas kernels, backward(): pl.pallas_call(kernel, out_shape=(pltpu.VMEM((rows, cols), f32), pltpu.VM...  3.22 us
  transfers between devices with their start and end apart: 27, of which 17 were waited for; matrix products, arithmetic and copies ran while one was open for 10% of the time, Pallas kernels for 12%

profile of v4, /device:TPU:0, one launch (start us, length us, event | category | flops | bytes accessed | tf_op | source)
XLA Modules:
  0.0 99.2 jit_solution(9534227055342920842)
XLA Ops:
  0.6 0.0 copy-start.2
  0.7 1.3 %pack_weights.1 = (bf16[384,256]{1,0:T(8,128)(2,1)S(1)}, bf16[384,256]{1,0:T(8,128)(2,1)S(1)}, bf16[384,256]{1,0:T(8,128)(2,1)S(1)}, bf16[384,256]{1,0:T(8,128)(2,1)S(1)}) custom-call(bf16[1,1024,256]{2,1,0:T(8,128)(2,1)} %gu_ref.1, bf16[1,32,4096]{2,1,0:T(8,128)(2,1)} %down_ref.1), custom_call_target="tpu_custom_call" | custom-call | bytes 1572864 | tf_op jit(solution)/shard_map/pack_weights/pallas_call | solution.py:334
  2.0 3.1 %collective-permute-start = (bf16[384,256]{1,0:T(8,128)(2,1)S(1)}, bf16[384,256]{1,0:T(8,128)(2,1)S(1)}, u32[]{:S(2)}, u32[]{:S(2)}) collective-permute-start(bf16[384,256]{1,0:T(8,128)(2,1)S(1)} %get-tuple-element.62.refs_0_), channel_id=1, source_target_pairs={{0,4},{4,8},{8,12},{12,0},{1,5},{5,9},{9,13},{13,1},{2,6},{6,10},{... | collective-permute-start | bytes 589832 | tf_op jit(solution)/shard_map/ppermute | solution.py:773
  5.1 1.6 %collective-permute-start.1 = (bf16[384,256]{1,0:T(8,128)(2,1)S(1)}, bf16[384,256]{1,0:T(8,128)(2,1)S(1)}, u32[]{:S(2)}, u32[]{:S(2)}) collective-permute-start(bf16[384,256]{1,0:T(8,128)(2,1)S(1)} %get-tuple-element.59.refs_1_.refs_0_), channel_id=1, source_target_pairs={{0,4},{4,8},{8,12},{12,0},{1,5},{5,9},{9,13},{13,1},{2,6},{6,10},{... | collective-permute-start | bytes 589832 | tf_op jit(solution)/shard_map/ppermute | solution.py:773
  6.6 2.1 %dynamic-slice_bitcast_fusion.1 = bf16[192,2048]{1,0:T(8,128)(2,1)} fusion(bf16[1,192,4096]{2,1,0:T(8,128)(2,1)} %tok_r.3, s32[]{:T(128)S(6)} %select_n.66), kind=kLoop, calls=%fused_computation.1 | loop fusion | bytes 1572868 | tf_op jit(solution)/shard_map/dynamic_slice | solution.py:770
  8.7 1.5 %collective-permute-start.11 = (bf16[192,2048]{1,0:T(8,128)(2,1)}, bf16[192,2048]{1,0:T(8,128)(2,1)S(1)}, u32[]{:S(2)}, u32[]{:S(2)}) collective-permute-start(bf16[192,2048]{1,0:T(8,128)(2,1)} %dynamic-slice_bitcast_fusion.1), channel_id=1, source_target_pairs={{0,2},{2,0},{1,3},{3,1},{4,6},{6,4},{5,7},{7,5},{8,10},{10,8},{9,1... | collective-permute-start | bytes 2359304 | tf_op jit(solution)/shard_map/ppermute | solution.py:775
  10.2 0.6 and_reduce_fusion
  10.9 0.1 dynamic-slice_bitcast_fusion
  10.9 1.9 %collective-permute-done = bf16[384,256]{1,0:T(8,128)(2,1)S(1)} collective-permute-done((bf16[384,256]{1,0:T(8,128)(2,1)S(1)}, bf16[384,256]{1,0:T(8,128)(2,1)S(1)}, u32[]{:S(2)}, u32[]{:S(2)}) %collective-permute-start) | collective-permute-done | bytes 196640 | tf_op jit(solution)/shard_map/ppermute | solution.py:773
  12.8 0.7 broadcast_select_fusion.9.refs_2_.refs_3_
  13.5 0.1 collective-permute-start.2
  13.6 2.6 %collective-permute-done.1 = bf16[384,256]{1,0:T(8,128)(2,1)S(1)} collective-permute-done((bf16[384,256]{1,0:T(8,128)(2,1)S(1)}, bf16[384,256]{1,0:T(8,128)(2,1)S(1)}, u32[]{:S(2)}, u32[]{:S(2)}) %collective-permute-start.1) | collective-permute-done | bytes 196640 | tf_op jit(solution)/shard_map/ppermute | solution.py:773
  16.2 0.7 broadcast_select_fusion.8.refs_3_.refs_4_
  16.9 0.7 collective-permute-start.3
  17.6 2.2 %pack_moments.1 = (bf16[384,256]{1,0:T(8,128)(2,1)S(1)}, bf16[384,256]{1,0:T(8,128)(2,1)S(1)}, bf16[384,256]{1,0:T(8,128)(2,1)S(1)}, bf16[384,256]{1,0:T(8,128)(...) custom-call(f32[1,1024,256]{2,1,0:T(8,128)} %refs_0_.3, ...), custom_call_target="tpu_custom_call" | custom-call | bytes 4718592 | tf_op jit(solution)/shard_map/pack_moments/pallas_call | solution.py:293
  19.8 1.5 %collective-permute-done.2 = bf16[384,256]{1,0:T(8,128)(2,1)S(1)} collective-permute-done((bf16[384,256]{1,0:T(8,128)(2,1)S(1)}, bf16[384,256]{1,0:T(8,128)(2,1)S(1)}, u32[]{:S(2)}, u32[]{:S(2)}) %collective-permute-start.2) | collective-permute-done | bytes 196640 | tf_op jit(solution)/shard_map/ppermute | solution.py:804
  21.4 0.7 broadcast_select_fusion.7.refs_4_.refs_5_
  22.0 0.3 collective-permute-start.4
  22.3 4.3 %collective-permute-done.3 = bf16[384,256]{1,0:T(8,128)(2,1)S(1)} collective-permute-done((bf16[384,256]{1,0:T(8,128)(2,1)S(1)}, bf16[384,256]{1,0:T(8,128)(2,1)S(1)}, u32[]{:S(2)}, u32[]{:S(2)}) %collective-permute-start.3) | collective-permute-done | bytes 196640 | tf_op jit(solution)/shard_map/ppermute | solution.py:804
  26.6 0.7 broadcast_select_fusion.6.refs_5_.refs_6_
  27.2 0.1 collective-permute-start.5
  27.3 2.6 %collective-permute-done.4 = bf16[384,256]{1,0:T(8,128)(2,1)S(1)} collective-permute-done((bf16[384,256]{1,0:T(8,128)(2,1)S(1)}, bf16[384,256]{1,0:T(8,128)(2,1)S(1)}, u32[]{:S(2)}, u32[]{:S(2)}) %collective-permute-start.4) | collective-permute-done | bytes 196640 | tf_op jit(solution)/shard_map/ppermute | solution.py:804
  29.9 0.7 broadcast_select_fusion.5.refs_6_.refs_7_.refs_5_.refs_11_
  30.6 0.1 collective-permute-start.6
  30.7 5.8 %collective-permute-done.5 = bf16[384,256]{1,0:T(8,128)(2,1)S(1)} collective-permute-done((bf16[384,256]{1,0:T(8,128)(2,1)S(1)}, bf16[384,256]{1,0:T(8,128)(2,1)S(1)}, u32[]{:S(2)}, u32[]{:S(2)}) %collective-permute-start.5) | collective-permute-done | bytes 196640 | tf_op jit(solution)/shard_map/ppermute | solution.py:804
  36.5 0.7 broadcast_select_fusion.4.refs_7_.refs_8_.refs_6_.refs_12_
  37.2 0.9 assemble.2
  38.1 0.1 collective-permute-start.7
  38.2 0.1 collective-permute-start.9
  38.3 1.8 %collective-permute-start.8 = (bf16[8,32,256]{2,1,0:T(8,128)(2,1)S(1)}, bf16[8,32,256]{2,1,0:T(8,128)(2,1)S(1)}, u32[]{:S(2)}, u32[]{:S(2)}) collective-permute-start(bf16[8,32,256]{2,1,0:T(8,128)(2,1)S(1)} %get-tuple-element.113), channel_id=1, source_target_pairs={{0,2},{2,0},{1,3},{3,1},{4,6},{6,4},{5,7},{7,5},{8,10},{10,8},{9,1... | collective-permute-start | bytes 393224 | tf_op jit(solution)/shard_map/ppermute | solution.py:812
  40.1 0.1 collective-permute-start.10
  40.2 0.7 broadcast_select_fusion.3.refs_9_.refs_7_.refs_13_
  40.8 0.6 collective-permute-done.10.mate_r
  41.4 1.4 %collective-permute-start.19 = (bf16[192,2048]{1,0:T(8,128)(2,1)S(1)}, bf16[192,2048]{1,0:T(8,128)(2,1)S(1)}, u32[]{:S(2)}, u32[]{:S(2)}) collective-permute-start(bf16[192,2048]{1,0:T(8,128)(2,1)S(1)} %dynamic-slice_bitcast_fusion), channel_id=1, source_target_pairs={{0,2},{2,0},{1,3},{3,1},{4,6},{6,4},{5,7},{7,5},{8,10},{10,8},{9,1... | collective-permute-start | bytes 2359304 | tf_op jit(solution)/shard_map/ppermute | solution.py:777
  42.9 0.9 collective-permute-done.9.far_r
  43.8 3.4 %collective-permute-done.8.near_r = bf16[8,32,256]{2,1,0:T(8,128)(2,1)S(1)} collective-permute-done((bf16[8,32,256]{2,1,0:T(8,128)(2,1)S(1)}, bf16[8,32,256]{2,1,0:T(8,128)(2,1)S(1)}, u32[]{:S(2)}, u32[]{:S(2)}) %collective-permute-start.8) | collective-permute-done | bytes 131104 | tf_op jit(solution)/shard_map/ppermute | solution.py:812
  47.2 0.7 broadcast_select_fusion.2.refs_10_.refs_8_.refs_14_
  47.9 1.3 %assemble.3.gu_r.refs_2_ = bf16[1024,256]{1,0:T(8,128)(2,1)S(1)} custom-call(s32[4]{0:T(128)S(1)} %copy-done, bf16[384,256]{1,0:T(8,128)(2,1)S(1)} %get-tuple-element.59.refs_1_.refs_0_, bf16[384,256]{1,0:T(8,128)(2,1)S(1)} %get-tuple-element.60.refs_1_, bf16[384,256]{1,0:T(8,128)(2,1)S(1)} %get-tuple-element.61.refs_2_, ...), custom_call_target="tpu_custom_call" | custom-call | bytes 1048576 | tf_op jit(solution)/shard_map/assemble/pallas_call | solution.py:247
  49.1 0.1 collective-permute-start.13
  49.2 0.1 collective-permute-start.15
  49.3 3.8 %collective-permute-done.12 = bf16[384,256]{1,0:T(8,128)(2,1)S(1)} collective-permute-done((bf16[384,256]{1,0:T(8,128)(2,1)S(1)}, bf16[384,256]{1,0:T(8,128)(2,1)S(1)}, u32[]{:S(2)}, u32[]{:S(2)}) %collective-permute-start.12) | collective-permute-done | bytes 196640 | tf_op jit(solution)/shard_map/ppermute | solution.py:804
  53.1 0.7 broadcast_select_fusion.1.refs_9_.refs_15_
  53.8 0.1 collective-permute-start.14
  53.8 5.0 %collective-permute-done.15 = bf16[384,256]{1,0:T(8,128)(2,1)S(1)} collective-permute-done((bf16[384,256]{1,0:T(8,128)(2,1)S(1)}, bf16[384,256]{1,0:T(8,128)(2,1)S(1)}, u32[]{:S(2)}, u32[]{:S(2)}) %collective-permute-start.15) | collective-permute-done | bytes 196640 | tf_op jit(solution)/shard_map/ppermute | solution.py:804
  58.8 0.7 broadcast_select_fusion.refs_10_.refs_16_
  59.5 0.1 collective-permute-start.17
  59.6 3.2 %collective-permute-done.14.refs_11_.refs_17_ = bf16[384,256]{1,0:T(8,128)(2,1)S(1)} collective-permute-done((bf16[384,256]{1,0:T(8,128)(2,1)S(1)}, bf16[384,256]{1,0:T(8,128)(2,1)S(1)}, u32[]{:S(2)}, u32[]{:S(2)}) %collective-permute-start.14) | collective-permute-done | bytes 196640 | tf_op jit(solution)/shard_map/ppermute | solution.py:804
  62.8 1.8 %forward_gu.1 = (f32[384,256]{1,0:T(8,128)S(1)}, bf16[384,256]{1,0:T(8,128)(2,1)S(1)}) custom-call(bf16[1,192,4096]{2,1,0:T(8,128)(2,1)} %tok_r.3, bf16[192,2048]{1,0:T(8,128)(2,1)S(1)} %collective-permute-done.11.tokn_r, bf16[1024,256]{1,0:T(8,128)(2,1)S(1)} %assemble.3.gu_r.refs_2_, bf16[1024,256]{1,0:T(8,128)(2,1)S(1)} %collective-permute-done.13.gum_r), custom_call_target="tpu_custom_call" | custom-call | flops 402653184 | bytes 3145728 | tf_op jit(solution)/shard_map/forward_gu/pallas_call | solution.py:377
  64.6 1.0 collective-permute-start.18
  65.6 1.8 %forward_dn.1 = (f32[384,128]{1,0:T(8,128)S(1)}, bf16[384,128]{1,0:T(8,128)(2,1)S(1)}) custom-call(bf16[1,192,4096]{2,1,0:T(8,128)(2,1)} %up_r.3, bf16[192,2048]{1,0:T(8,128)(2,1)S(1)} %collective-permute-done.19.upn_r, bf16[8,32,256]{2,1,0:T(8,128)(2,1)S(1)} %get-tuple-element.91.mine_r, bf16[8,32,256]{2,1,0:T(8,128)(2,1)S(1)} %collective-permute-done.8.near_r, ...), custom_call_target="tpu_custom_call" | custom-call | flops 201326592 | bytes 3145728 | tf_op jit(solution)/shard_map/forward_dn/pallas_call | solution.py:422
  67.4 1.2 %collective-permute-start.20 = (bf16[384,128]{1,0:T(8,128)(2,1)S(1)}, bf16[384,128]{1,0:T(8,128)(2,1)S(1)}, u32[]{:S(2)}, u32[]{:S(2)}) collective-permute-start(bf16[384,128]{1,0:T(8,128)(2,1)S(1)} %get-tuple-element.93), channel_id=1, source_target_pairs={{0,2},{2,0},{1,3},{3,1},{4,6},{6,4},{5,7},{7,5},{8,10},{10,8},{9,1... | collective-permute-start | bytes 294920 | tf_op jit(solution)/shard_map/ppermute | solution.py:827
  68.6 0.2 collective-permute-done.17.refs_12_.refs_18_
  68.8 3.2 %collective-permute-done.16.refs_13_.refs_19_ = bf16[384,256]{1,0:T(8,128)(2,1)S(1)} collective-permute-done((bf16[384,256]{1,0:T(8,128)(2,1)S(1)}, bf16[384,256]{1,0:T(8,128)(2,1)S(1)}, u32[]{:S(2)}, u32[]{:S(2)}) %collective-permute-start.16) | collective-permute-done | bytes 196640 | tf_op jit(solution)/shard_map/ppermute | solution.py:804
  72.0 1.1 %collective-permute-done.20.dhn_r = bf16[384,128]{1,0:T(8,128)(2,1)S(1)} collective-permute-done((bf16[384,128]{1,0:T(8,128)(2,1)S(1)}, bf16[384,128]{1,0:T(8,128)(2,1)S(1)}, u32[]{:S(2)}, u32[]{:S(2)}) %collective-permute-start.20) | collective-permute-done | bytes 98336 | tf_op jit(solution)/shard_map/ppermute | solution.py:827
  73.1 3.2 %backward.1 = (f32[1024,256]{1,0:T(8,128)S(1)}, bf16[1024,256]{1,0:T(8,128)(2,1)S(1)}, f32[2,8,32,256]{3,2,1,0:T(8,128)S(1)}, bf16[2,8,32,256]{3,2,1,0:T(8,128)(2,1)S(1)}) custom-call(f32[384,256]{1,0:T(8,128)S(1)} %get-tuple-element.89.pre_r, bf16[384,256]{1,0:T(8,128)(2,1)S(1)} %collective-permute-done.18.pren_r, f32[384,128]{1,0:T(8,128)S(1)} %get-tuple-element.92.dh_r, ...), custom_call_target="tpu_custom_call" | custom-call | flops 603979776 | bytes 6291456 | tf_op jit(solution)/shard_map/backward/pallas_call | solution.py:496
  76.3 0.1 collective-permute-start.21
  76.4 0.5 collective-permute-start.22
  76.9 0.3 collective-permute-start.23
  77.2 2.5 %collective-permute-start.25 = (bf16[384,256]{1,0:T(8,128)(2,1)S(1)}, bf16[384,256]{1,0:T(8,128)(2,1)S(1)}, u32[]{:S(2)}, u32[]{:S(2)}) collective-permute-start(bf16[384,256]{1,0:T(8,128)(2,1)S(1)} %collective-permute-done.16.refs_13_.refs_19_), channel_id=1, source_target_pairs={{0,4},{4,8},{8,12},{12,0},{1,5},{5,9},{9,13},{13,1},{2,6},{6,10},{... | collective-permute-start | bytes 589832 | tf_op jit(solution)/shard_map/ppermute | solution.py:804
  79.7 6.8 %collective-permute-done.23.refs_20_ = bf16[384,256]{1,0:T(8,128)(2,1)S(1)} collective-permute-done((bf16[384,256]{1,0:T(8,128)(2,1)S(1)}, bf16[384,256]{1,0:T(8,128)(2,1)S(1)}, u32[]{:S(2)}, u32[]{:S(2)}) %collective-permute-start.23) | collective-permute-done | bytes 196640 | tf_op jit(solution)/shard_map/ppermute | solution.py:804
  86.5 1.1 %collective-permute-start.24 = (bf16[8,32,256]{2,1,0:T(8,128)(2,1)S(1)}, bf16[8,32,256]{2,1,0:T(8,128)(2,1)S(1)}, u32[]{:S(2)}, u32[]{:S(2)}) collective-permute-start(bf16[8,32,256]{2,1,0:T(8,128)(2,1)S(1)} %fusion), channel_id=1, source_target_pairs={{0,2},{2,0},{1,3},{3,1},{4,6},{6,4},{5,7},{7,5},{8,10},{10,8},{9,1... | collective-permute-start | bytes 393224 | tf_op jit(solution)/shard_map/ppermute | solution.py:839
  87.6 3.5 %update.2 = (bf16[1,1024,256]{2,1,0:T(8,128)(2,1)}, f32[1,1024,256]{2,1,0:T(8,128)}, f32[1,1024,256]{2,1,0:T(8,128)}) custom-call(s32[4]{0:T(128)S(1)} %copy-done, f32[4]{0:T(128)S(1)} %copy-done.1, f32[1,1024,256]{2,1,0:T(8,128)} %refs_0_.3, f32[1,1024,256]{2,1,0:T(8,128)} %refs_1_.3, bf16[1024,256]{1,0:T(8,128)(2,1)S(1)} %assemble.3.gu_r.refs_2_, ...), custom_call_target="tpu_custom_call" | custom-call | bytes 3604480 | tf_op jit(solution)/shard_map/update/pallas_call | solution.py:727
  91.1 2.9 %collective-permute-done.26.refs_22_ = bf16[384,256]{1,0:T(8,128)(2,1)S(1)} collective-permute-done((bf16[384,256]{1,0:T(8,128)(2,1)S(1)}, bf16[384,256]{1,0:T(8,128)(2,1)S(1)}, u32[]{:S(2)}, u32[]{:S(2)}) %collective-permute-start.26) | collective-permute-done | bytes 196640 | tf_op jit(solution)/shard_map/ppermute | solution.py:804
  94.0 5.2 %update.3 = (bf16[1,1024,256]{2,1,0:T(8,128)(2,1)}, f32[1,1024,256]{2,1,0:T(8,128)}, f32[1,1024,256]{2,1,0:T(8,128)}, bf16[1,32,4096]{2,1,0:T(8,128)(2,1)}, f32[...) custom-call(s32[4]{0:T(128)S(1)} %copy-done, ...), custom_call_target="tpu_custom_call", output_to_operand_aliasing={{0}: (25, {}), {1}: (26, {}), {2}: (27, {})} | custom-call | bytes 2162688 | tf_op jit(solution)/shard_map/update/pallas_call | solution.py:727
  (20 shorter events, 0.1 us)
Async XLA Ops:
  0.6 10.2 %copy-start.2 = (bf16[1,192,4096]{2,1,0:T(8,128)(2,1)S(1)}, bf16[1,192,4096]{2,1,0:T(8,128)(2,1)}, u32[]{:S(2)}) copy-start(bf16[1,192,4096]{2,1,0:T(8,128)(2,1)} %up_r.3) | copy-start | bytes 4718596
  0.6 9.6 %copy-start = (s32[4]{0:T(128)S(1)}, s32[4]{0:T(128)}, u32[]{:S(2)}) copy-start(s32[4]{0:T(128)} %winner_ref.7) | copy-start | bytes 52
  2.0 10.8 %collective-permute-start = (bf16[384,256]{1,0:T(8,128)(2,1)S(1)}, bf16[384,256]{1,0:T(8,128)(2,1)S(1)}, u32[]{:S(2)}, u32[]{:S(2)}) collective-permute-start(bf16[384,256]{1,0:T(8,128)(2,1)S(1)} %get-tuple-element.62.refs_0_), channel_id=1, source_target_pairs={{0,4},{4,8},{8,12},{12,0},{1,5},{5,9},{9,13},{13,1},{2,6},{6,10},{... | collective-permute-start | bytes 589832 | tf_op jit(solution)/shard_map/ppermute | solution.py:773
  5.1 11.1 %collective-permute-start.1 = (bf16[384,256]{1,0:T(8,128)(2,1)S(1)}, bf16[384,256]{1,0:T(8,128)(2,1)S(1)}, u32[]{:S(2)}, u32[]{:S(2)}) collective-permute-start(bf16[384,256]{1,0:T(8,128)(2,1)S(1)} %get-tuple-element.59.refs_1_.refs_0_), channel_id=1, source_target_pairs={{0,4},{4,8},{8,12},{12,0},{1,5},{5,9},{9,13},{13,1},{2,6},{6,10},{... | collective-permute-start | bytes 589832 | tf_op jit(solution)/shard_map/ppermute | solution.py:773
  8.7 54.1 %collective-permute-start.11 = (bf16[192,2048]{1,0:T(8,128)(2,1)}, bf16[192,2048]{1,0:T(8,128)(2,1)S(1)}, u32[]{:S(2)}, u32[]{:S(2)}) collective-permute-start(bf16[192,2048]{1,0:T(8,128)(2,1)} %dynamic-slice_bitcast_fusion.1), channel_id=1, source_target_pairs={{0,2},{2,0},{1,3},{3,1},{4,6},{6,4},{5,7},{7,5},{8,10},{10,8},{9,1... | collective-permute-start | bytes 2359304 | tf_op jit(solution)/shard_map/ppermute | solution.py:775
  13.5 7.9 %collective-permute-start.2 = (bf16[384,256]{1,0:T(8,128)(2,1)S(1)}, bf16[384,256]{1,0:T(8,128)(2,1)S(1)}, u32[]{:S(2)}, u32[]{:S(2)}) collective-permute-start(bf16[384,256]{1,0:T(8,128)(2,1)S(1)} %broadcast_select_fusion.9.refs_2_.refs_3_), channel_id=1, source_target_pairs={{0,4},{4,8},{8,12},{12,0},{1,5},{5,9},{9,13},{13,1},{2,6},{6,10},{... | collective-permute-start | bytes 589832 | tf_op jit(solution)/shard_map/ppermute | solution.py:804
  16.9 9.7 %collective-permute-start.3 = (bf16[384,256]{1,0:T(8,128)(2,1)S(1)}, bf16[384,256]{1,0:T(8,128)(2,1)S(1)}, u32[]{:S(2)}, u32[]{:S(2)}) collective-permute-start(bf16[384,256]{1,0:T(8,128)(2,1)S(1)} %broadcast_select_fusion.8.refs_3_.refs_4_), channel_id=1, source_target_pairs={{0,4},{4,8},{8,12},{12,0},{1,5},{5,9},{9,13},{13,1},{2,6},{6,10},{... | collective-permute-start | bytes 589832 | tf_op jit(solution)/shard_map/ppermute | solution.py:804
  22.0 7.9 %collective-permute-start.4 = (bf16[384,256]{1,0:T(8,128)(2,1)S(1)}, bf16[384,256]{1,0:T(8,128)(2,1)S(1)}, u32[]{:S(2)}, u32[]{:S(2)}) collective-permute-start(bf16[384,256]{1,0:T(8,128)(2,1)S(1)} %broadcast_select_fusion.7.refs_4_.refs_5_), channel_id=1, source_target_pairs={{0,4},{4,8},{8,12},{12,0},{1,5},{5,9},{9,13},{13,1},{2,6},{6,10},{... | collective-permute-start | bytes 589832 | tf_op jit(solution)/shard_map/ppermute | solution.py:804
  27.2 9.2 %collective-permute-start.5 = (bf16[384,256]{1,0:T(8,128)(2,1)S(1)}, bf16[384,256]{1,0:T(8,128)(2,1)S(1)}, u32[]{:S(2)}, u32[]{:S(2)}) collective-permute-start(bf16[384,256]{1,0:T(8,128)(2,1)S(1)} %broadcast_select_fusion.6.refs_5_.refs_6_), channel_id=1, source_target_pairs={{0,4},{4,8},{8,12},{12,0},{1,5},{5,9},{9,13},{13,1},{2,6},{6,10},{... | collective-permute-start | bytes 589832 | tf_op jit(solution)/shard_map/ppermute | solution.py:804
  30.6 9.5 %collective-permute-start.6 = (bf16[384,256]{1,0:T(8,128)(2,1)S(1)}, bf16[384,256]{1,0:T(8,128)(2,1)S(1)}, u32[]{:S(2)}, u32[]{:S(2)}) collective-permute-start(bf16[384,256]{1,0:T(8,128)(2,1)S(1)} %broadcast_select_fusion.5.refs_6_.refs_7_.refs_5_.refs_11_), channel_id=1, source_target_pairs={{0,4},{4,8},{8,12},{12,0},{1,5},{5,9},{9,13},{13,1},{2,6},{6,10},{... | collective-permute-start | bytes 589832 | tf_op jit(solution)/shard_map/ppermute | solution.py:804
  38.1 9.1 %collective-permute-start.7 = (bf16[384,256]{1,0:T(8,128)(2,1)S(1)}, bf16[384,256]{1,0:T(8,128)(2,1)S(1)}, u32[]{:S(2)}, u32[]{:S(2)}) collective-permute-start(bf16[384,256]{1,0:T(8,128)(2,1)S(1)} %broadcast_select_fusion.4.refs_7_.refs_8_.refs_6_.refs_12_), channel_id=1, source_target_pairs={{0,4},{4,8},{8,12},{12,0},{1,5},{5,9},{9,13},{13,1},{2,6},{6,10},{... | collective-permute-start | bytes 589832 | tf_op jit(solution)/shard_map/ppermute | solution.py:804
  38.2 5.6 %collective-permute-start.9 = (bf16[8,32,256]{2,1,0:T(8,128)(2,1)S(1)}, bf16[8,32,256]{2,1,0:T(8,128)(2,1)S(1)}, u32[]{:S(2)}, u32[]{:S(2)}) collective-permute-start(bf16[8,32,256]{2,1,0:T(8,128)(2,1)S(1)} %get-tuple-element.113), channel_id=1, source_target_pairs={{0,3},{3,0},{1,2},{2,1},{4,7},{7,4},{5,6},{6,5},{8,11},{11,8},{9,1... | collective-permute-start | bytes 393224 | tf_op jit(solution)/shard_map/ppermute | solution.py:814
  38.3 8.9 %collective-permute-start.8 = (bf16[8,32,256]{2,1,0:T(8,128)(2,1)S(1)}, bf16[8,32,256]{2,1,0:T(8,128)(2,1)S(1)}, u32[]{:S(2)}, u32[]{:S(2)}) collective-permute-start(bf16[8,32,256]{2,1,0:T(8,128)(2,1)S(1)} %get-tuple-element.113), channel_id=1, source_target_pairs={{0,2},{2,0},{1,3},{3,1},{4,6},{6,4},{5,7},{7,5},{8,10},{10,8},{9,1... | collective-permute-start | bytes 393224 | tf_op jit(solution)/shard_map/ppermute | solution.py:812
  40.1 1.3 %collective-permute-start.10 = (bf16[8,32,256]{2,1,0:T(8,128)(2,1)S(1)}, bf16[8,32,256]{2,1,0:T(8,128)(2,1)S(1)}, u32[]{:S(2)}, u32[]{:S(2)}) collective-permute-start(bf16[8,32,256]{2,1,0:T(8,128)(2,1)S(1)} %get-tuple-element.91.mine_r), channel_id=1, source_target_pairs={{0,1},{1,0},{2,3},{3,2},{4,5},{5,4},{6,7},{7,6},{8,9},{9,8},{10,11... | collective-permute-start | bytes 393224 | tf_op jit(solution)/shard_map/ppermute | solution.py:813
  41.4 24.2 %collective-permute-start.19 = (bf16[192,2048]{1,0:T(8,128)(2,1)S(1)}, bf16[192,2048]{1,0:T(8,128)(2,1)S(1)}, u32[]{:S(2)}, u32[]{:S(2)}) collective-permute-start(bf16[192,2048]{1,0:T(8,128)(2,1)S(1)} %dynamic-slice_bitcast_fusion), channel_id=1, source_target_pairs={{0,2},{2,0},{1,3},{3,1},{4,6},{6,4},{5,7},{7,5},{8,10},{10,8},{9,1... | collective-permute-start | bytes 2359304 | tf_op jit(solution)/shard_map/ppermute | solution.py:777
  43.8 9.3 %collective-permute-start.12 = (bf16[384,256]{1,0:T(8,128)(2,1)S(1)}, bf16[384,256]{1,0:T(8,128)(2,1)S(1)}, u32[]{:S(2)}, u32[]{:S(2)}) collective-permute-start(bf16[384,256]{1,0:T(8,128)(2,1)S(1)} %broadcast_select_fusion.3.refs_9_.refs_7_.refs_13_), channel_id=1, source_target_pairs={{0,4},{4,8},{8,12},{12,0},{1,5},{5,9},{9,13},{13,1},{2,6},{6,10},{... | collective-permute-start | bytes 589832 | tf_op jit(solution)/shard_map/ppermute | solution.py:804
  49.1 13.7 %collective-permute-start.13 = (bf16[1024,256]{1,0:T(8,128)(2,1)S(1)}, bf16[1024,256]{1,0:T(8,128)(2,1)S(1)}, u32[]{:S(2)}, u32[]{:S(2)}) collective-permute-start(bf16[1024,256]{1,0:T(8,128)(2,1)S(1)} %assemble.3.gu_r.refs_2_), channel_id=1, source_target_pairs={{0,1},{1,0},{2,3},{3,2},{4,5},{5,4},{6,7},{7,6},{8,9},{9,8},{10,11... | collective-permute-start | bytes 1572872 | tf_op jit(solution)/shard_map/ppermute | solution.py:819
  49.2 9.6 %collective-permute-start.15 = (bf16[384,256]{1,0:T(8,128)(2,1)S(1)}, bf16[384,256]{1,0:T(8,128)(2,1)S(1)}, u32[]{:S(2)}, u32[]{:S(2)}) collective-permute-start(bf16[384,256]{1,0:T(8,128)(2,1)S(1)} %broadcast_select_fusion.2.refs_10_.refs_8_.refs_14_), channel_id=1, source_target_pairs={{0,4},{4,8},{8,12},{12,0},{1,5},{5,9},{9,13},{13,1},{2,6},{6,10},{... | collective-permute-start | bytes 589832 | tf_op jit(solution)/shard_map/ppermute | solution.py:804
  53.8 9.0 %collective-permute-start.14 = (bf16[384,256]{1,0:T(8,128)(2,1)S(1)}, bf16[384,256]{1,0:T(8,128)(2,1)S(1)}, u32[]{:S(2)}, u32[]{:S(2)}) collective-permute-start(bf16[384,256]{1,0:T(8,128)(2,1)S(1)} %broadcast_select_fusion.1.refs_9_.refs_15_), channel_id=1, source_target_pairs={{0,4},{4,8},{8,12},{12,0},{1,5},{5,9},{9,13},{13,1},{2,6},{6,10},{... | collective-permute-start | bytes 589832 | tf_op jit(solution)/shard_map/ppermute | solution.py:804
  59.5 9.3 %collective-permute-start.17 = (bf16[384,256]{1,0:T(8,128)(2,1)S(1)}, bf16[384,256]{1,0:T(8,128)(2,1)S(1)}, u32[]{:S(2)}, u32[]{:S(2)}) collective-permute-start(bf16[384,256]{1,0:T(8,128)(2,1)S(1)} %broadcast_select_fusion.refs_10_.refs_16_), channel_id=1, source_target_pairs={{0,4},{4,8},{8,12},{12,0},{1,5},{5,9},{9,13},{13,1},{2,6},{6,10},{... | collective-permute-start | bytes 589832 | tf_op jit(solution)/shard_map/ppermute | solution.py:804
  62.8 9.2 %collective-permute-start.16 = (bf16[384,256]{1,0:T(8,128)(2,1)S(1)}, bf16[384,256]{1,0:T(8,128)(2,1)S(1)}, u32[]{:S(2)}, u32[]{:S(2)}) collective-permute-start(bf16[384,256]{1,0:T(8,128)(2,1)S(1)} %collective-permute-done.14.refs_11_.refs_17_), channel_id=1, source_target_pairs={{0,4},{4,8},{8,12},{12,0},{1,5},{5,9},{9,13},{13,1},{2,6},{6,10},{... | collective-permute-start | bytes 589832 | tf_op jit(solution)/shard_map/ppermute | solution.py:804
  64.6 8.4 %collective-permute-start.18 = (bf16[384,256]{1,0:T(8,128)(2,1)S(1)}, bf16[384,256]{1,0:T(8,128)(2,1)S(1)}, u32[]{:S(2)}, u32[]{:S(2)}) collective-permute-start(bf16[384,256]{1,0:T(8,128)(2,1)S(1)} %get-tuple-element.90), channel_id=1, source_target_pairs={{0,2},{2,0},{1,3},{3,1},{4,6},{6,4},{5,7},{7,5},{8,10},{10,8},{9,1... | collective-permute-start | bytes 589832 | tf_op jit(solution)/shard_map/ppermute | solution.py:822
  67.4 5.7 %collective-permute-start.20 = (bf16[384,128]{1,0:T(8,128)(2,1)S(1)}, bf16[384,128]{1,0:T(8,128)(2,1)S(1)}, u32[]{:S(2)}, u32[]{:S(2)}) collective-permute-start(bf16[384,128]{1,0:T(8,128)(2,1)S(1)} %get-tuple-element.93), channel_id=1, source_target_pairs={{0,2},{2,0},{1,3},{3,1},{4,6},{6,4},{5,7},{7,5},{8,10},{10,8},{9,1... | collective-permute-start | bytes 294920 | tf_op jit(solution)/shard_map/ppermute | solution.py:827
  73.1 14.5 %copy-start.1 = (f32[4]{0:T(128)S(1)}, f32[4]{0:T(128)}, u32[]{:S(2)}) copy-start(f32[4]{0:T(128)} %rate_ref.3) | copy-start | bytes 52
  76.3 11.3 %collective-permute-start.21 = (bf16[1024,256]{1,0:T(8,128)(2,1)S(1)}, bf16[1024,256]{1,0:T(8,128)(2,1)S(1)}, u32[]{:S(2)}, u32[]{:S(2)}) collective-permute-start(bf16[1024,256]{1,0:T(8,128)(2,1)S(1)} %get-tuple-element.95), channel_id=1, source_target_pairs={{0,1},{1,0},{2,3},{3,2},{4,5},{5,4},{6,7},{7,6},{8,9},{9,8},{10,11... | collective-permute-start | bytes 1572872 | tf_op jit(solution)/shard_map/ppermute | solution.py:832
  76.4 10.1 %collective-permute-start.22 = (bf16[2,8,32,256]{3,2,1,0:T(8,128)(2,1)S(1)}, bf16[2,8,32,256]{3,2,1,0:T(8,128)(2,1)S(1)}, u32[]{:S(2)}, u32[]{:S(2)}) collective-permute-start(bf16[2,8,32,256]{3,2,1,0:T(8,128)(2,1)S(1)} %get-tuple-element.97), channel_id=1, source_target_pairs={{0,1},{1,0},{2,3},{3,2},{4,5},{5,4},{6,7},{7,6},{8,9},{9,8},{10,11... | collective-permute-start | bytes 786440 | tf_op jit(solution)/shard_map/ppermute | solution.py:833
  76.9 9.6 %collective-permute-start.23 = (bf16[384,256]{1,0:T(8,128)(2,1)S(1)}, bf16[384,256]{1,0:T(8,128)(2,1)S(1)}, u32[]{:S(2)}, u32[]{:S(2)}) collective-permute-start(bf16[384,256]{1,0:T(8,128)(2,1)S(1)} %collective-permute-done.17.refs_12_.refs_18_), channel_id=1, source_target_pairs={{0,4},{4,8},{8,12},{12,0},{1,5},{5,9},{9,13},{13,1},{2,6},{6,10},{... | collective-permute-start | bytes 589832 | tf_op jit(solution)/shard_map/ppermute | solution.py:804
  77.2 13.9 %collective-permute-start.25 = (bf16[384,256]{1,0:T(8,128)(2,1)S(1)}, bf16[384,256]{1,0:T(8,128)(2,1)S(1)}, u32[]{:S(2)}, u32[]{:S(2)}) collective-permute-start(bf16[384,256]{1,0:T(8,128)(2,1)S(1)} %collective-permute-done.16.refs_13_.refs_19_), channel_id=1, source_target_pairs={{0,4},{4,8},{8,12},{12,0},{1,5},{5,9},{9,13},{13,1},{2,6},{6,10},{... | collective-permute-start | bytes 589832 | tf_op jit(solution)/shard_map/ppermute | solution.py:804
  86.4 7.6 %collective-permute-start.26 = (bf16[384,256]{1,0:T(8,128)(2,1)S(1)}, bf16[384,256]{1,0:T(8,128)(2,1)S(1)}, u32[]{:S(2)}, u32[]{:S(2)}) collective-permute-start(bf16[384,256]{1,0:T(8,128)(2,1)S(1)} %collective-permute-done.23.refs_20_), channel_id=1, source_target_pairs={{0,4},{4,8},{8,12},{12,0},{1,5},{5,9},{9,13},{13,1},{2,6},{6,10},{... | collective-permute-start | bytes 589832 | tf_op jit(solution)/shard_map/ppermute | solution.py:804
  86.5 7.5 %collective-permute-start.24 = (bf16[8,32,256]{2,1,0:T(8,128)(2,1)S(1)}, bf16[8,32,256]{2,1,0:T(8,128)(2,1)S(1)}, u32[]{:S(2)}, u32[]{:S(2)}) collective-permute-start(bf16[8,32,256]{2,1,0:T(8,128)(2,1)S(1)} %fusion), channel_id=1, source_target_pairs={{0,2},{2,0},{1,3},{3,1},{4,6},{6,4},{5,7},{7,5},{8,10},{10,8},{9,1... | collective-permute-start | bytes 393224 | tf_op jit(solution)/shard_map/ppermute | solution.py:839

commit v5 on v4

--- a/solution.py
+++ b/solution.py
@@ -158,13 +158,14 @@
 W_CHUNKS = 4
 M_CHUNKS = 8
 CHUNKS = W_CHUNKS + M_CHUNKS
-EARLY = 5
+EARLY = 6
 NEAR_AT = 8
+SEND_AT = 14
 GU_AT = 10
 DN_AT = 11
-BACK_AT = 14
+BACK_AT = 13
 SUM_AT = 15
-EARLY_AT = 15
+EARLY_AT = 16
 
 
 def grant(mib):
@@ -792,9 +793,12 @@
     held = []
     gap = [up_theirs]
     last = STAGGER * (members - 2)
-    pre = dh = grads = first_gu = None
     for step in range(STAGGER, CHUNKS + last + STAGGER):
-        back = after(got[step - STAGGER], *gap)
+        back = got[step - STAGGER]
+        if step == SEND_AT:
+            d_got = lax.ppermute(after(d_mate, back), "fsdp", over_core)
+            g_got = lax.ppermute(after(g_mate, back), "fsdp", over_core)
+        back = after(back, *gap)
         gap = []
         if step < CHUNKS:
             back = jnp.where(is_source, own[step], back)
@@ -813,7 +817,7 @@
             dn_mate = lax.ppermute(dn_mine, "fsdp", over_core)
             dn_far = lax.ppermute(dn_theirs, "fsdp", over_both)
         if step == NEAR_AT:
-            gap += [dn_near, dn_far, dn_mate]
+            gap += [dn_near, dn_mate, dn_far]
         if ready == W_CHUNKS - 1:
             gu = take(rows_d, rows_all)
             gu_mate = lax.ppermute(gu, "fsdp", over_core)
@@ -829,8 +833,6 @@
             g_own, g_mate, d_own, d_mate = backward(
                 after(pre, back), pre_near, dh, dh_near, tokens, tok_near, grad_out, up_near, rows_gu, rows_dn
             )
-            g_got = lax.ppermute(g_mate, "fsdp", over_core)
-            d_got = lax.ppermute(d_mate, "fsdp", over_core)
         if step == SUM_AT:
             d_there = (
                 lax.dynamic_index_in_dim(after(d_own, back), 1 - chip, axis=0, keepdims=False)

time: 99.6 us -> 96.4 us (0.968)
  waiting for transfers between devices: 49.9 us -> 46.2 us
  starting transfers between devices: 17.6 us -> 18.7 us
  Pallas kernels: 21.3 us -> 20.3 us
    ppermute x14, waiting for transfers between devices: 39.3 us -> 35 us  [on_device_four(): got.append(lax.ppermute(back, 'member', ring))]
    ppermute x14, starting transfers between devices: 4.23 us -> 6.08 us  [on_device_four(): got.append(lax.ppermute(back, 'member', ring))]
  transfers between devices with their start and end apart: 27 -> 27, of which waited for: 17 -> 17; matrix products, arithmetic and copies ran while one was open for 10% -> 10% of each run, Pallas kernels for 12% -> 16%
where the time goes in v5:
time: 96.4 us; the launch traced here: 95.7 us
  waiting for transfers between devices  46.2 us (48%)
  Pallas kernels  20.3 us (21%)
  starting transfers between devices  18.7 us (19%)
  other arithmetic  7.35 us (8%)
  local copies, waits for them, and re-layouts  2.18 us (2%)
    ppermute x14, waiting for transfers between devices, on_device_four(): got.append(lax.ppermute(back, 'member', ring))  35 us
    pallas_call x2, Pallas kernels, update(): pl.pallas_call(kernel, out_shape=tuple(shapes), in_specs=[SMEM, SMEM] + [...  7.8 us
    select_n x10, other arithmetic, on_device_four(): back = jnp.where(is_source, own[step], back)  6.69 us
    ppermute x14, starting transfers between devices, on_device_four(): got.append(lax.ppermute(back, 'member', ring))  6.08 us
    ppermute x2, starting transfers between devices, on_device_four(): got = [lax.ppermute(chunk, 'member', ring) for chunk in own[:STAGGER]]  4.65 us
    ppermute x2, waiting for transfers between devices, on_device_four(): got = [lax.ppermute(chunk, 'member', ring) for chunk in own[:STAGGER]]  4.52 us
    ppermute x1, waiting for transfers between devices, on_device_four(): dn_near = lax.ppermute(dn_theirs, 'fsdp', over_x)  3.39 us
    pallas_call x1, Pallas kernels, backward(): pl.pallas_call(kernel, out_shape=(pltpu.VMEM((rows, cols), f32), pltpu.VM...  3.22 us
  transfers between devices with their start and end apart: 27, of which 17 were waited for; matrix products, arithmetic and copies ran while one was open for 10% of the time, Pallas kernels for 16%

profile of v5, /device:TPU:0, one launch (start us, length us, event | category | flops | bytes accessed | tf_op | source)
XLA Modules:
  0.0 95.7 jit_solution(16700233935907491239)
XLA Ops:
  0.7 1.3 %pack_weights.1 = (bf16[384,256]{1,0:T(8,128)(2,1)S(1)}, bf16[384,256]{1,0:T(8,128)(2,1)S(1)}, bf16[384,256]{1,0:T(8,128)(2,1)S(1)}, bf16[384,256]{1,0:T(8,128)(2,1)S(1)}) custom-call(bf16[1,1024,256]{2,1,0:T(8,128)(2,1)} %gu_ref.1, bf16[1,32,4096]{2,1,0:T(8,128)(2,1)} %down_ref.1), custom_call_target="tpu_custom_call" | custom-call | bytes 1572864 | tf_op jit(solution)/shard_map/pack_weights/pallas_call | solution.py:335
  2.0 3.1 %collective-permute-start = (bf16[384,256]{1,0:T(8,128)(2,1)S(1)}, bf16[384,256]{1,0:T(8,128)(2,1)S(1)}, u32[]{:S(2)}, u32[]{:S(2)}) collective-permute-start(bf16[384,256]{1,0:T(8,128)(2,1)S(1)} %get-tuple-element.64.refs_0_), channel_id=1, source_target_pairs={{0,4},{4,8},{8,12},{12,0},{1,5},{5,9},{9,13},{13,1},{2,6},{6,10},{... | collective-permute-start | bytes 589832 | tf_op jit(solution)/shard_map/ppermute | solution.py:774
  5.1 1.6 %collective-permute-start.1 = (bf16[384,256]{1,0:T(8,128)(2,1)S(1)}, bf16[384,256]{1,0:T(8,128)(2,1)S(1)}, u32[]{:S(2)}, u32[]{:S(2)}) collective-permute-start(bf16[384,256]{1,0:T(8,128)(2,1)S(1)} %get-tuple-element.61.refs_1_.refs_0_), channel_id=1, source_target_pairs={{0,4},{4,8},{8,12},{12,0},{1,5},{5,9},{9,13},{13,1},{2,6},{6,10},{... | collective-permute-start | bytes 589832 | tf_op jit(solution)/shard_map/ppermute | solution.py:774
  6.6 2.1 %dynamic-slice_bitcast_fusion.1 = bf16[192,2048]{1,0:T(8,128)(2,1)} fusion(bf16[1,192,4096]{2,1,0:T(8,128)(2,1)} %tok_r.3, s32[]{:T(128)S(6)} %select_n.66), kind=kLoop, calls=%fused_computation.1 | loop fusion | bytes 1572868 | tf_op jit(solution)/shard_map/dynamic_slice | solution.py:771
  8.7 1.5 %collective-permute-start.11 = (bf16[192,2048]{1,0:T(8,128)(2,1)}, bf16[192,2048]{1,0:T(8,128)(2,1)S(1)}, u32[]{:S(2)}, u32[]{:S(2)}) collective-permute-start(bf16[192,2048]{1,0:T(8,128)(2,1)} %dynamic-slice_bitcast_fusion.1), channel_id=1, source_target_pairs={{0,2},{2,0},{1,3},{3,1},{4,6},{6,4},{5,7},{7,5},{8,10},{10,8},{9,1... | collective-permute-start | bytes 2359304 | tf_op jit(solution)/shard_map/ppermute | solution.py:776
  10.2 0.6 and_reduce_fusion
  10.9 1.9 %collective-permute-done = bf16[384,256]{1,0:T(8,128)(2,1)S(1)} collective-permute-done((bf16[384,256]{1,0:T(8,128)(2,1)S(1)}, bf16[384,256]{1,0:T(8,128)(2,1)S(1)}, u32[]{:S(2)}, u32[]{:S(2)}) %collective-permute-start) | collective-permute-done | bytes 196640 | tf_op jit(solution)/shard_map/ppermute | solution.py:774
  12.8 0.7 broadcast_select_fusion.9.refs_2_.refs_3_
  13.5 0.1 collective-permute-start.2
  13.6 2.6 %collective-permute-done.1 = bf16[384,256]{1,0:T(8,128)(2,1)S(1)} collective-permute-done((bf16[384,256]{1,0:T(8,128)(2,1)S(1)}, bf16[384,256]{1,0:T(8,128)(2,1)S(1)}, u32[]{:S(2)}, u32[]{:S(2)}) %collective-permute-start.1) | collective-permute-done | bytes 196640 | tf_op jit(solution)/shard_map/ppermute | solution.py:774
  16.2 0.7 broadcast_select_fusion.8.refs_3_.refs_4_
  16.9 0.7 collective-permute-start.3
  17.6 2.2 %pack_moments.1 = (bf16[384,256]{1,0:T(8,128)(2,1)S(1)}, bf16[384,256]{1,0:T(8,128)(2,1)S(1)}, bf16[384,256]{1,0:T(8,128)(2,1)S(1)}, bf16[384,256]{1,0:T(8,128)(...) custom-call(f32[1,1024,256]{2,1,0:T(8,128)} %refs_0_.3, ...), custom_call_target="tpu_custom_call" | custom-call | bytes 4718592 | tf_op jit(solution)/shard_map/pack_moments/pallas_call | solution.py:294
  19.8 1.5 %collective-permute-done.2 = bf16[384,256]{1,0:T(8,128)(2,1)S(1)} collective-permute-done((bf16[384,256]{1,0:T(8,128)(2,1)S(1)}, bf16[384,256]{1,0:T(8,128)(2,1)S(1)}, u32[]{:S(2)}, u32[]{:S(2)}) %collective-permute-start.2) | collective-permute-done | bytes 196640 | tf_op jit(solution)/shard_map/ppermute | solution.py:808
  21.4 0.7 broadcast_select_fusion.7.refs_4_.refs_5_
  22.0 0.3 collective-permute-start.4
  22.3 4.3 %collective-permute-done.3 = bf16[384,256]{1,0:T(8,128)(2,1)S(1)} collective-permute-done((bf16[384,256]{1,0:T(8,128)(2,1)S(1)}, bf16[384,256]{1,0:T(8,128)(2,1)S(1)}, u32[]{:S(2)}, u32[]{:S(2)}) %collective-permute-start.3) | collective-permute-done | bytes 196640 | tf_op jit(solution)/shard_map/ppermute | solution.py:808
  26.6 0.7 broadcast_select_fusion.6.refs_5_.refs_6_
  27.2 0.1 collective-permute-start.5
  27.3 2.6 %collective-permute-done.4 = bf16[384,256]{1,0:T(8,128)(2,1)S(1)} collective-permute-done((bf16[384,256]{1,0:T(8,128)(2,1)S(1)}, bf16[384,256]{1,0:T(8,128)(2,1)S(1)}, u32[]{:S(2)}, u32[]{:S(2)}) %collective-permute-start.4) | collective-permute-done | bytes 196640 | tf_op jit(solution)/shard_map/ppermute | solution.py:808
  29.9 0.7 broadcast_select_fusion.5.refs_6_.refs_7_.refs_5_.refs_11_
  30.6 0.1 collective-permute-start.6
  30.7 5.8 %collective-permute-done.5 = bf16[384,256]{1,0:T(8,128)(2,1)S(1)} collective-permute-done((bf16[384,256]{1,0:T(8,128)(2,1)S(1)}, bf16[384,256]{1,0:T(8,128)(2,1)S(1)}, u32[]{:S(2)}, u32[]{:S(2)}) %collective-permute-start.5) | collective-permute-done | bytes 196640 | tf_op jit(solution)/shard_map/ppermute | solution.py:808
  36.5 0.7 broadcast_select_fusion.4.refs_7_.refs_8_.refs_6_.refs_12_
  37.2 0.9 assemble.2
  38.1 0.1 collective-permute-start.7
  38.2 0.1 collective-permute-start.10
  38.3 1.8 %collective-permute-start.8 = (bf16[8,32,256]{2,1,0:T(8,128)(2,1)S(1)}, bf16[8,32,256]{2,1,0:T(8,128)(2,1)S(1)}, u32[]{:S(2)}, u32[]{:S(2)}) collective-permute-start(bf16[8,32,256]{2,1,0:T(8,128)(2,1)S(1)} %get-tuple-element.117), channel_id=1, source_target_pairs={{0,2},{2,0},{1,3},{3,1},{4,6},{6,4},{5,7},{7,5},{8,10},{10,8},{9,1... | collective-permute-start | bytes 393224 | tf_op jit(solution)/shard_map/ppermute | solution.py:816
  40.1 0.1 collective-permute-start.9
  40.2 0.7 broadcast_select_fusion.3.refs_9_.refs_7_.refs_13_
  40.8 0.6 collective-permute-done.9.mate_r
  41.4 1.4 %collective-permute-start.18 = (bf16[192,2048]{1,0:T(8,128)(2,1)S(1)}, bf16[192,2048]{1,0:T(8,128)(2,1)S(1)}, u32[]{:S(2)}, u32[]{:S(2)}) collective-permute-start(bf16[192,2048]{1,0:T(8,128)(2,1)S(1)} %dynamic-slice_bitcast_fusion), channel_id=1, source_target_pairs={{0,2},{2,0},{1,3},{3,1},{4,6},{6,4},{5,7},{7,5},{8,10},{10,8},{9,1... | collective-permute-start | bytes 2359304 | tf_op jit(solution)/shard_map/ppermute | solution.py:778
  42.9 0.9 collective-permute-done.10.far_r
  43.8 3.4 %collective-permute-done.8.near_r = bf16[8,32,256]{2,1,0:T(8,128)(2,1)S(1)} collective-permute-done((bf16[8,32,256]{2,1,0:T(8,128)(2,1)S(1)}, bf16[8,32,256]{2,1,0:T(8,128)(2,1)S(1)}, u32[]{:S(2)}, u32[]{:S(2)}) %collective-permute-start.8) | collective-permute-done | bytes 131104 | tf_op jit(solution)/shard_map/ppermute | solution.py:816
  47.2 0.7 broadcast_select_fusion.2.refs_10_.refs_8_.refs_14_
  47.9 1.3 %assemble.3.gu_r.refs_2_ = bf16[1024,256]{1,0:T(8,128)(2,1)S(1)} custom-call(s32[4]{0:T(128)S(1)} %copy-done, bf16[384,256]{1,0:T(8,128)(2,1)S(1)} %get-tuple-element.61.refs_1_.refs_0_, bf16[384,256]{1,0:T(8,128)(2,1)S(1)} %get-tuple-element.62.refs_1_, bf16[384,256]{1,0:T(8,128)(2,1)S(1)} %get-tuple-element.63.refs_2_, ...), custom_call_target="tpu_custom_call" | custom-call | bytes 1048576 | tf_op jit(solution)/shard_map/assemble/pallas_call | solution.py:248
  49.1 0.1 collective-permute-start.13
  49.2 0.1 collective-permute-start.14
  49.3 3.8 %collective-permute-done.12 = bf16[384,256]{1,0:T(8,128)(2,1)S(1)} collective-permute-done((bf16[384,256]{1,0:T(8,128)(2,1)S(1)}, bf16[384,256]{1,0:T(8,128)(2,1)S(1)}, u32[]{:S(2)}, u32[]{:S(2)}) %collective-permute-start.12) | collective-permute-done | bytes 196640 | tf_op jit(solution)/shard_map/ppermute | solution.py:808
  53.1 0.7 broadcast_select_fusion.1.refs_9_.refs_15_
  53.8 0.1 collective-permute-start.16
  53.8 5.0 %collective-permute-done.14 = bf16[384,256]{1,0:T(8,128)(2,1)S(1)} collective-permute-done((bf16[384,256]{1,0:T(8,128)(2,1)S(1)}, bf16[384,256]{1,0:T(8,128)(2,1)S(1)}, u32[]{:S(2)}, u32[]{:S(2)}) %collective-permute-start.14) | collective-permute-done | bytes 196640 | tf_op jit(solution)/shard_map/ppermute | solution.py:808
  58.8 0.7 broadcast_select_fusion.refs_10_.refs_16_
  59.5 0.1 collective-permute-start.15
  59.6 1.8 %forward_gu.1 = (f32[384,256]{1,0:T(8,128)S(1)}, bf16[384,256]{1,0:T(8,128)(2,1)S(1)}) custom-call(bf16[1,192,4096]{2,1,0:T(8,128)(2,1)} %tok_r.3, bf16[192,2048]{1,0:T(8,128)(2,1)S(1)} %collective-permute-done.11.tokn_r, bf16[1024,256]{1,0:T(8,128)(2,1)S(1)} %assemble.3.gu_r.refs_2_, bf16[1024,256]{1,0:T(8,128)(2,1)S(1)} %collective-permute-done.13.gum_r), custom_call_target="tpu_custom_call" | custom-call | flops 402653184 | bytes 3145728 | tf_op jit(solution)/shard_map/forward_gu/pallas_call | solution.py:378
  61.4 1.3 %collective-permute-start.17 = (bf16[384,256]{1,0:T(8,128)(2,1)S(1)}, bf16[384,256]{1,0:T(8,128)(2,1)S(1)}, u32[]{:S(2)}, u32[]{:S(2)}) collective-permute-start(bf16[384,256]{1,0:T(8,128)(2,1)S(1)} %get-tuple-element.91), channel_id=1, source_target_pairs={{0,2},{2,0},{1,3},{3,1},{4,6},{6,4},{5,7},{7,5},{8,10},{10,8},{9,1... | collective-permute-start | bytes 589832 | tf_op jit(solution)/shard_map/ppermute | solution.py:826
  62.8 0.6 collective-permute-start.20
  63.4 0.3 collective-permute-done.18.upn_r
  63.7 1.8 %forward_dn.1 = (f32[384,128]{1,0:T(8,128)S(1)}, bf16[384,128]{1,0:T(8,128)(2,1)S(1)}) custom-call(bf16[1,192,4096]{2,1,0:T(8,128)(2,1)} %up_r.3, bf16[192,2048]{1,0:T(8,128)(2,1)S(1)} %collective-permute-done.18.upn_r, bf16[8,32,256]{2,1,0:T(8,128)(2,1)S(1)} %get-tuple-element.92.mine_r, bf16[8,32,256]{2,1,0:T(8,128)(2,1)S(1)} %collective-permute-done.8.near_r, ...), custom_call_target="tpu_custom_call" | custom-call | flops 201326592 | bytes 3145728 | tf_op jit(solution)/shard_map/forward_dn/pallas_call | solution.py:423
  65.5 0.4 collective-permute-start.19
  65.9 2.9 %collective-permute-done.15.refs_12_.refs_18_ = bf16[384,256]{1,0:T(8,128)(2,1)S(1)} collective-permute-done((bf16[384,256]{1,0:T(8,128)(2,1)S(1)}, bf16[384,256]{1,0:T(8,128)(2,1)S(1)}, u32[]{:S(2)}, u32[]{:S(2)}) %collective-permute-start.15) | collective-permute-done | bytes 196640 | tf_op jit(solution)/shard_map/ppermute | solution.py:808
  68.8 1.4 %collective-permute-done.19.dhn_r = bf16[384,128]{1,0:T(8,128)(2,1)S(1)} collective-permute-done((bf16[384,128]{1,0:T(8,128)(2,1)S(1)}, bf16[384,128]{1,0:T(8,128)(2,1)S(1)}, u32[]{:S(2)}, u32[]{:S(2)}) %collective-permute-start.19) | collective-permute-done | bytes 98336 | tf_op jit(solution)/shard_map/ppermute | solution.py:831
  70.2 3.2 %backward.1 = (f32[1024,256]{1,0:T(8,128)S(1)}, bf16[1024,256]{1,0:T(8,128)(2,1)S(1)}, f32[2,8,32,256]{3,2,1,0:T(8,128)S(1)}, bf16[2,8,32,256]{3,2,1,0:T(8,128)(2,1)S(1)}) custom-call(f32[384,256]{1,0:T(8,128)S(1)} %get-tuple-element.90.pre_r, bf16[384,256]{1,0:T(8,128)(2,1)S(1)} %collective-permute-done.17.pren_r, f32[384,128]{1,0:T(8,128)S(1)} %get-tuple-element.93.dh_r, ...), custom_call_target="tpu_custom_call" | custom-call | flops 603979776 | bytes 6291456 | tf_op jit(solution)/shard_map/backward/pallas_call | solution.py:497
  73.4 0.1 collective-permute-start.21
  73.5 0.5 collective-permute-start.22
  74.0 2.1 %collective-permute-start.23 = (bf16[384,256]{1,0:T(8,128)(2,1)S(1)}, bf16[384,256]{1,0:T(8,128)(2,1)S(1)}, u32[]{:S(2)}, u32[]{:S(2)}) collective-permute-start(bf16[384,256]{1,0:T(8,128)(2,1)S(1)} %collective-permute-done.15.refs_12_.refs_18_), channel_id=1, source_target_pairs={{0,4},{4,8},{8,12},{12,0},{1,5},{5,9},{9,13},{13,1},{2,6},{6,10},{... | collective-permute-start | bytes 589832 | tf_op jit(solution)/shard_map/ppermute | solution.py:808
  76.2 1.8 %collective-permute-start.25 = (bf16[384,256]{1,0:T(8,128)(2,1)S(1)}, bf16[384,256]{1,0:T(8,128)(2,1)S(1)}, u32[]{:S(2)}, u32[]{:S(2)}) collective-permute-start(bf16[384,256]{1,0:T(8,128)(2,1)S(1)} %collective-permute-done.20.refs_13_.refs_19_), channel_id=1, source_target_pairs={{0,4},{4,8},{8,12},{12,0},{1,5},{5,9},{9,13},{13,1},{2,6},{6,10},{... | collective-permute-start | bytes 589832 | tf_op jit(solution)/shard_map/ppermute | solution.py:808
  77.9 5.9 %collective-permute-done.23.refs_14_.refs_20_ = bf16[384,256]{1,0:T(8,128)(2,1)S(1)} collective-permute-done((bf16[384,256]{1,0:T(8,128)(2,1)S(1)}, bf16[384,256]{1,0:T(8,128)(2,1)S(1)}, u32[]{:S(2)}, u32[]{:S(2)}) %collective-permute-start.23) | collective-permute-done | bytes 196640 | tf_op jit(solution)/shard_map/ppermute | solution.py:808
  83.8 0.1 collective-permute-start.26
  83.9 0.7 collective-permute-start.24
  84.7 3.0 %collective-permute-done.25.refs_21_ = bf16[384,256]{1,0:T(8,128)(2,1)S(1)} collective-permute-done((bf16[384,256]{1,0:T(8,128)(2,1)S(1)}, bf16[384,256]{1,0:T(8,128)(2,1)S(1)}, u32[]{:S(2)}, u32[]{:S(2)}) %collective-permute-start.25) | collective-permute-done | bytes 196640 | tf_op jit(solution)/shard_map/ppermute | solution.py:808
  87.7 3.8 %update.2 = (bf16[1,1024,256]{2,1,0:T(8,128)(2,1)}, f32[1,1024,256]{2,1,0:T(8,128)}, f32[1,1024,256]{2,1,0:T(8,128)}) custom-call(s32[4]{0:T(128)S(1)} %copy-done, f32[4]{0:T(128)S(1)} %copy-done.1, f32[1,1024,256]{2,1,0:T(8,128)} %refs_0_.3, f32[1,1024,256]{2,1,0:T(8,128)} %refs_1_.3, bf16[1024,256]{1,0:T(8,128)(2,1)S(1)} %assemble.3.gu_r.refs_2_, ...), custom_call_target="tpu_custom_call" | custom-call | bytes 4325376 | tf_op jit(solution)/shard_map/update/pallas_call | solution.py:728
  91.5 0.2 collective-permute-done.26.refs_22_
  91.7 4.0 %update.3 = (bf16[1,1024,256]{2,1,0:T(8,128)(2,1)}, f32[1,1024,256]{2,1,0:T(8,128)}, f32[1,1024,256]{2,1,0:T(8,128)}, bf16[1,32,4096]{2,1,0:T(8,128)(2,1)}, f32[...) custom-call(s32[4]{0:T(128)S(1)} %copy-done, ...), custom_call_target="tpu_custom_call", output_to_operand_aliasing={{0}: (25, {}), {1}: (26, {}), {2}: (27, {})} | custom-call | bytes 1441792 | tf_op jit(solution)/shard_map/update/pallas_call | solution.py:728
  (20 shorter events, 0.2 us)
Async XLA Ops:
  0.6 10.2 %copy-start.2 = (bf16[1,192,4096]{2,1,0:T(8,128)(2,1)S(1)}, bf16[1,192,4096]{2,1,0:T(8,128)(2,1)}, u32[]{:S(2)}) copy-start(bf16[1,192,4096]{2,1,0:T(8,128)(2,1)} %up_r.3) | copy-start | bytes 4718596
  0.6 9.6 %copy-start = (s32[4]{0:T(128)S(1)}, s32[4]{0:T(128)}, u32[]{:S(2)}) copy-start(s32[4]{0:T(128)} %winner_ref.7) | copy-start | bytes 52
  2.0 10.8 %collective-permute-start = (bf16[384,256]{1,0:T(8,128)(2,1)S(1)}, bf16[384,256]{1,0:T(8,128)(2,1)S(1)}, u32[]{:S(2)}, u32[]{:S(2)}) collective-permute-start(bf16[384,256]{1,0:T(8,128)(2,1)S(1)} %get-tuple-element.64.refs_0_), channel_id=1, source_target_pairs={{0,4},{4,8},{8,12},{12,0},{1,5},{5,9},{9,13},{13,1},{2,6},{6,10},{... | collective-permute-start | bytes 589832 | tf_op jit(solution)/shard_map/ppermute | solution.py:774
  5.1 11.1 %collective-permute-start.1 = (bf16[384,256]{1,0:T(8,128)(2,1)S(1)}, bf16[384,256]{1,0:T(8,128)(2,1)S(1)}, u32[]{:S(2)}, u32[]{:S(2)}) collective-permute-start(bf16[384,256]{1,0:T(8,128)(2,1)S(1)} %get-tuple-element.61.refs_1_.refs_0_), channel_id=1, source_target_pairs={{0,4},{4,8},{8,12},{12,0},{1,5},{5,9},{9,13},{13,1},{2,6},{6,10},{... | collective-permute-start | bytes 589832 | tf_op jit(solution)/shard_map/ppermute | solution.py:774
  8.7 50.9 %collective-permute-start.11 = (bf16[192,2048]{1,0:T(8,128)(2,1)}, bf16[192,2048]{1,0:T(8,128)(2,1)S(1)}, u32[]{:S(2)}, u32[]{:S(2)}) collective-permute-start(bf16[192,2048]{1,0:T(8,128)(2,1)} %dynamic-slice_bitcast_fusion.1), channel_id=1, source_target_pairs={{0,2},{2,0},{1,3},{3,1},{4,6},{6,4},{5,7},{7,5},{8,10},{10,8},{9,1... | collective-permute-start | bytes 2359304 | tf_op jit(solution)/shard_map/ppermute | solution.py:776
  13.5 7.9 %collective-permute-start.2 = (bf16[384,256]{1,0:T(8,128)(2,1)S(1)}, bf16[384,256]{1,0:T(8,128)(2,1)S(1)}, u32[]{:S(2)}, u32[]{:S(2)}) collective-permute-start(bf16[384,256]{1,0:T(8,128)(2,1)S(1)} %broadcast_select_fusion.9.refs_2_.refs_3_), channel_id=1, source_target_pairs={{0,4},{4,8},{8,12},{12,0},{1,5},{5,9},{9,13},{13,1},{2,6},{6,10},{... | collective-permute-start | bytes 589832 | tf_op jit(solution)/shard_map/ppermute | solution.py:808
  16.9 9.7 %collective-permute-start.3 = (bf16[384,256]{1,0:T(8,128)(2,1)S(1)}, bf16[384,256]{1,0:T(8,128)(2,1)S(1)}, u32[]{:S(2)}, u32[]{:S(2)}) collective-permute-start(bf16[384,256]{1,0:T(8,128)(2,1)S(1)} %broadcast_select_fusion.8.refs_3_.refs_4_), channel_id=1, source_target_pairs={{0,4},{4,8},{8,12},{12,0},{1,5},{5,9},{9,13},{13,1},{2,6},{6,10},{... | collective-permute-start | bytes 589832 | tf_op jit(solution)/shard_map/ppermute | solution.py:808
  22.0 7.9 %collective-permute-start.4 = (bf16[384,256]{1,0:T(8,128)(2,1)S(1)}, bf16[384,256]{1,0:T(8,128)(2,1)S(1)}, u32[]{:S(2)}, u32[]{:S(2)}) collective-permute-start(bf16[384,256]{1,0:T(8,128)(2,1)S(1)} %broadcast_select_fusion.7.refs_4_.refs_5_), channel_id=1, source_target_pairs={{0,4},{4,8},{8,12},{12,0},{1,5},{5,9},{9,13},{13,1},{2,6},{6,10},{... | collective-permute-start | bytes 589832 | tf_op jit(solution)/shard_map/ppermute | solution.py:808
  27.2 9.2 %collective-permute-start.5 = (bf16[384,256]{1,0:T(8,128)(2,1)S(1)}, bf16[384,256]{1,0:T(8,128)(2,1)S(1)}, u32[]{:S(2)}, u32[]{:S(2)}) collective-permute-start(bf16[384,256]{1,0:T(8,128)(2,1)S(1)} %broadcast_select_fusion.6.refs_5_.refs_6_), channel_id=1, source_target_pairs={{0,4},{4,8},{8,12},{12,0},{1,5},{5,9},{9,13},{13,1},{2,6},{6,10},{... | collective-permute-start | bytes 589832 | tf_op jit(solution)/shard_map/ppermute | solution.py:808
  30.6 9.5 %collective-permute-start.6 = (bf16[384,256]{1,0:T(8,128)(2,1)S(1)}, bf16[384,256]{1,0:T(8,128)(2,1)S(1)}, u32[]{:S(2)}, u32[]{:S(2)}) collective-permute-start(bf16[384,256]{1,0:T(8,128)(2,1)S(1)} %broadcast_select_fusion.5.refs_6_.refs_7_.refs_5_.refs_11_), channel_id=1, source_target_pairs={{0,4},{4,8},{8,12},{12,0},{1,5},{5,9},{9,13},{13,1},{2,6},{6,10},{... | collective-permute-start | bytes 589832 | tf_op jit(solution)/shard_map/ppermute | solution.py:808
  38.1 9.1 %collective-permute-start.7 = (bf16[384,256]{1,0:T(8,128)(2,1)S(1)}, bf16[384,256]{1,0:T(8,128)(2,1)S(1)}, u32[]{:S(2)}, u32[]{:S(2)}) collective-permute-start(bf16[384,256]{1,0:T(8,128)(2,1)S(1)} %broadcast_select_fusion.4.refs_7_.refs_8_.refs_6_.refs_12_), channel_id=1, source_target_pairs={{0,4},{4,8},{8,12},{12,0},{1,5},{5,9},{9,13},{13,1},{2,6},{6,10},{... | collective-permute-start | bytes 589832 | tf_op jit(solution)/shard_map/ppermute | solution.py:808
  38.2 5.6 %collective-permute-start.10 = (bf16[8,32,256]{2,1,0:T(8,128)(2,1)S(1)}, bf16[8,32,256]{2,1,0:T(8,128)(2,1)S(1)}, u32[]{:S(2)}, u32[]{:S(2)}) collective-permute-start(bf16[8,32,256]{2,1,0:T(8,128)(2,1)S(1)} %get-tuple-element.117), channel_id=1, source_target_pairs={{0,3},{3,0},{1,2},{2,1},{4,7},{7,4},{5,6},{6,5},{8,11},{11,8},{9,1... | collective-permute-start | bytes 393224 | tf_op jit(solution)/shard_map/ppermute | solution.py:818
  38.3 8.9 %collective-permute-start.8 = (bf16[8,32,256]{2,1,0:T(8,128)(2,1)S(1)}, bf16[8,32,256]{2,1,0:T(8,128)(2,1)S(1)}, u32[]{:S(2)}, u32[]{:S(2)}) collective-permute-start(bf16[8,32,256]{2,1,0:T(8,128)(2,1)S(1)} %get-tuple-element.117), channel_id=1, source_target_pairs={{0,2},{2,0},{1,3},{3,1},{4,6},{6,4},{5,7},{7,5},{8,10},{10,8},{9,1... | collective-permute-start | bytes 393224 | tf_op jit(solution)/shard_map/ppermute | solution.py:816
  40.1 1.3 %collective-permute-start.9 = (bf16[8,32,256]{2,1,0:T(8,128)(2,1)S(1)}, bf16[8,32,256]{2,1,0:T(8,128)(2,1)S(1)}, u32[]{:S(2)}, u32[]{:S(2)}) collective-permute-start(bf16[8,32,256]{2,1,0:T(8,128)(2,1)S(1)} %get-tuple-element.92.mine_r), channel_id=1, source_target_pairs={{0,1},{1,0},{2,3},{3,2},{4,5},{5,4},{6,7},{7,6},{8,9},{9,8},{10,11... | collective-permute-start | bytes 393224 | tf_op jit(solution)/shard_map/ppermute | solution.py:817
  41.4 22.3 %collective-permute-start.18 = (bf16[192,2048]{1,0:T(8,128)(2,1)S(1)}, bf16[192,2048]{1,0:T(8,128)(2,1)S(1)}, u32[]{:S(2)}, u32[]{:S(2)}) collective-permute-start(bf16[192,2048]{1,0:T(8,128)(2,1)S(1)} %dynamic-slice_bitcast_fusion), channel_id=1, source_target_pairs={{0,2},{2,0},{1,3},{3,1},{4,6},{6,4},{5,7},{7,5},{8,10},{10,8},{9,1... | collective-permute-start | bytes 2359304 | tf_op jit(solution)/shard_map/ppermute | solution.py:778
  43.8 9.3 %collective-permute-start.12 = (bf16[384,256]{1,0:T(8,128)(2,1)S(1)}, bf16[384,256]{1,0:T(8,128)(2,1)S(1)}, u32[]{:S(2)}, u32[]{:S(2)}) collective-permute-start(bf16[384,256]{1,0:T(8,128)(2,1)S(1)} %broadcast_select_fusion.3.refs_9_.refs_7_.refs_13_), channel_id=1, source_target_pairs={{0,4},{4,8},{8,12},{12,0},{1,5},{5,9},{9,13},{13,1},{2,6},{6,10},{... | collective-permute-start | bytes 589832 | tf_op jit(solution)/shard_map/ppermute | solution.py:808
  49.1 10.5 %collective-permute-start.13 = (bf16[1024,256]{1,0:T(8,128)(2,1)S(1)}, bf16[1024,256]{1,0:T(8,128)(2,1)S(1)}, u32[]{:S(2)}, u32[]{:S(2)}) collective-permute-start(bf16[1024,256]{1,0:T(8,128)(2,1)S(1)} %assemble.3.gu_r.refs_2_), channel_id=1, source_target_pairs={{0,1},{1,0},{2,3},{3,2},{4,5},{5,4},{6,7},{7,6},{8,9},{9,8},{10,11... | collective-permute-start | bytes 1572872 | tf_op jit(solution)/shard_map/ppermute | solution.py:823
  49.2 9.6 %collective-permute-start.14 = (bf16[384,256]{1,0:T(8,128)(2,1)S(1)}, bf16[384,256]{1,0:T(8,128)(2,1)S(1)}, u32[]{:S(2)}, u32[]{:S(2)}) collective-permute-start(bf16[384,256]{1,0:T(8,128)(2,1)S(1)} %broadcast_select_fusion.2.refs_10_.refs_8_.refs_14_), channel_id=1, source_target_pairs={{0,4},{4,8},{8,12},{12,0},{1,5},{5,9},{9,13},{13,1},{2,6},{6,10},{... | collective-permute-start | bytes 589832 | tf_op jit(solution)/shard_map/ppermute | solution.py:808
  53.8 9.0 %collective-permute-start.16 = (bf16[384,256]{1,0:T(8,128)(2,1)S(1)}, bf16[384,256]{1,0:T(8,128)(2,1)S(1)}, u32[]{:S(2)}, u32[]{:S(2)}) collective-permute-start(bf16[384,256]{1,0:T(8,128)(2,1)S(1)} %broadcast_select_fusion.1.refs_9_.refs_15_), channel_id=1, source_target_pairs={{0,4},{4,8},{8,12},{12,0},{1,5},{5,9},{9,13},{13,1},{2,6},{6,10},{... | collective-permute-start | bytes 589832 | tf_op jit(solution)/shard_map/ppermute | solution.py:808
  59.5 9.3 %collective-permute-start.15 = (bf16[384,256]{1,0:T(8,128)(2,1)S(1)}, bf16[384,256]{1,0:T(8,128)(2,1)S(1)}, u32[]{:S(2)}, u32[]{:S(2)}) collective-permute-start(bf16[384,256]{1,0:T(8,128)(2,1)S(1)} %broadcast_select_fusion.refs_10_.refs_16_), channel_id=1, source_target_pairs={{0,4},{4,8},{8,12},{12,0},{1,5},{5,9},{9,13},{13,1},{2,6},{6,10},{... | collective-permute-start | bytes 589832 | tf_op jit(solution)/shard_map/ppermute | solution.py:808
  61.4 8.7 %collective-permute-start.17 = (bf16[384,256]{1,0:T(8,128)(2,1)S(1)}, bf16[384,256]{1,0:T(8,128)(2,1)S(1)}, u32[]{:S(2)}, u32[]{:S(2)}) collective-permute-start(bf16[384,256]{1,0:T(8,128)(2,1)S(1)} %get-tuple-element.91), channel_id=1, source_target_pairs={{0,2},{2,0},{1,3},{3,1},{4,6},{6,4},{5,7},{7,5},{8,10},{10,8},{9,1... | collective-permute-start | bytes 589832 | tf_op jit(solution)/shard_map/ppermute | solution.py:826
  62.8 10.6 %collective-permute-start.20 = (bf16[384,256]{1,0:T(8,128)(2,1)S(1)}, bf16[384,256]{1,0:T(8,128)(2,1)S(1)}, u32[]{:S(2)}, u32[]{:S(2)}) collective-permute-start(bf16[384,256]{1,0:T(8,128)(2,1)S(1)} %collective-permute-done.16.refs_11_.refs_17_), channel_id=1, source_target_pairs={{0,4},{4,8},{8,12},{12,0},{1,5},{5,9},{9,13},{13,1},{2,6},{6,10},{... | collective-permute-start | bytes 589832 | tf_op jit(solution)/shard_map/ppermute | solution.py:808
  65.5 4.7 %collective-permute-start.19 = (bf16[384,128]{1,0:T(8,128)(2,1)S(1)}, bf16[384,128]{1,0:T(8,128)(2,1)S(1)}, u32[]{:S(2)}, u32[]{:S(2)}) collective-permute-start(bf16[384,128]{1,0:T(8,128)(2,1)S(1)} %get-tuple-element.94), channel_id=1, source_target_pairs={{0,2},{2,0},{1,3},{3,1},{4,6},{6,4},{5,7},{7,5},{8,10},{10,8},{9,1... | collective-permute-start | bytes 294920 | tf_op jit(solution)/shard_map/ppermute | solution.py:831
  70.2 17.5 %copy-start.1 = (f32[4]{0:T(128)S(1)}, f32[4]{0:T(128)}, u32[]{:S(2)}) copy-start(f32[4]{0:T(128)} %rate_ref.3) | copy-start | bytes 52
  73.4 14.2 %collective-permute-start.21 = (bf16[1024,256]{1,0:T(8,128)(2,1)S(1)}, bf16[1024,256]{1,0:T(8,128)(2,1)S(1)}, u32[]{:S(2)}, u32[]{:S(2)}) collective-permute-start(bf16[1024,256]{1,0:T(8,128)(2,1)S(1)} %get-tuple-element.97), channel_id=1, source_target_pairs={{0,1},{1,0},{2,3},{3,2},{4,5},{5,4},{6,7},{7,6},{8,9},{9,8},{10,11... | collective-permute-start | bytes 1572872 | tf_op jit(solution)/shard_map/ppermute | solution.py:800
  73.5 10.4 %collective-permute-start.22 = (bf16[2,8,32,256]{3,2,1,0:T(8,128)(2,1)S(1)}, bf16[2,8,32,256]{3,2,1,0:T(8,128)(2,1)S(1)}, u32[]{:S(2)}, u32[]{:S(2)}) collective-permute-start(bf16[2,8,32,256]{3,2,1,0:T(8,128)(2,1)S(1)} %get-tuple-element.100), channel_id=1, source_target_pairs={{0,1},{1,0},{2,3},{3,2},{4,5},{5,4},{6,7},{7,6},{8,9},{9,8},{10,11... | collective-permute-start | bytes 786440 | tf_op jit(solution)/shard_map/ppermute | solution.py:799
  74.0 9.8 %collective-permute-start.23 = (bf16[384,256]{1,0:T(8,128)(2,1)S(1)}, bf16[384,256]{1,0:T(8,128)(2,1)S(1)}, u32[]{:S(2)}, u32[]{:S(2)}) collective-permute-start(bf16[384,256]{1,0:T(8,128)(2,1)S(1)} %collective-permute-done.15.refs_12_.refs_18_), channel_id=1, source_target_pairs={{0,4},{4,8},{8,12},{12,0},{1,5},{5,9},{9,13},{13,1},{2,6},{6,10},{... | collective-permute-start | bytes 589832 | tf_op jit(solution)/shard_map/ppermute | solution.py:808
  76.2 11.5 %collective-permute-start.25 = (bf16[384,256]{1,0:T(8,128)(2,1)S(1)}, bf16[384,256]{1,0:T(8,128)(2,1)S(1)}, u32[]{:S(2)}, u32[]{:S(2)}) collective-permute-start(bf16[384,256]{1,0:T(8,128)(2,1)S(1)} %collective-permute-done.20.refs_13_.refs_19_), channel_id=1, source_target_pairs={{0,4},{4,8},{8,12},{12,0},{1,5},{5,9},{9,13},{13,1},{2,6},{6,10},{... | collective-permute-start | bytes 589832 | tf_op jit(solution)/shard_map/ppermute | solution.py:808
  83.8 7.9 %collective-permute-start.26 = (bf16[384,256]{1,0:T(8,128)(2,1)S(1)}, bf16[384,256]{1,0:T(8,128)(2,1)S(1)}, u32[]{:S(2)}, u32[]{:S(2)}) collective-permute-start(bf16[384,256]{1,0:T(8,128)(2,1)S(1)} %collective-permute-done.23.refs_14_.refs_20_), channel_id=1, source_target_pairs={{0,4},{4,8},{8,12},{12,0},{1,5},{5,9},{9,13},{13,1},{2,6},{6,10},{... | collective-permute-start | bytes 589832 | tf_op jit(solution)/shard_map/ppermute | solution.py:808
  83.9 7.7 %collective-permute-start.24 = (bf16[8,32,256]{2,1,0:T(8,128)(2,1)S(1)}, bf16[8,32,256]{2,1,0:T(8,128)(2,1)S(1)}, u32[]{:S(2)}, u32[]{:S(2)}) collective-permute-start(bf16[8,32,256]{2,1,0:T(8,128)(2,1)S(1)} %fusion), channel_id=1, source_target_pairs={{0,2},{2,0},{1,3},{3,1},{4,6},{6,4},{5,7},{7,5},{8,10},{10,8},{9,1... | collective-permute-start | bytes 393224 | tf_op jit(solution)/shard_map/ppermute | solution.py:841

commit v6 on v5

--- a/solution.py
+++ b/solution.py
@@ -388,7 +388,7 @@
         compiler_params=grant(8),
         cost_estimate=cost(4 * count * half * cols, 3 * 1024 * 1024),
         name="forward_gu",
-    )(*in_hbm(tokens), tok_near, gu, gu_mate)
+    )(*in_hbm(tokens), tok_near, *in_vmem(gu, gu_mate))
 
 
 def forward_dn(grad_out, up_near, parts):
@@ -433,7 +433,7 @@
         compiler_params=grant(8),
         cost_estimate=cost(4 * count * half * units, 3 * 1024 * 1024),
         name="forward_dn",
-    )(*in_hbm(grad_out), up_near, *parts)
+    )(*in_hbm(grad_out), up_near, *in_vmem(*parts))
 
 
 def backward(pre, pre_near, dh, dh_near, tokens, tok_near, grad_out, up_near, rows, rows_dn):
@@ -791,7 +791,7 @@
 
     rows_d = down.size // cols
     held = []
-    gap = [up_theirs]
+    gap = []
     last = STAGGER * (members - 2)
     for step in range(STAGGER, CHUNKS + last + STAGGER):
         back = got[step - STAGGER]

time: 96.4 us -> 96.4 us (level)
  no operation moved by 1% of the time
where the time goes in v6:
time: 96.4 us; the launch traced here: 95.7 us
  waiting for transfers between devices  46.2 us (48%)
  Pallas kernels  20.3 us (21%)
  starting transfers between devices  18.7 us (19%)
  other arithmetic  7.35 us (8%)
  local copies, waits for them, and re-layouts  2.18 us (2%)
    ppermute x14, waiting for transfers between devices, on_device_four(): got.append(lax.ppermute(back, 'member', ring))  35 us
    pallas_call x2, Pallas kernels, update(): pl.pallas_call(kernel, out_shape=tuple(shapes), in_specs=[SMEM, SMEM] + [...  7.8 us
    select_n x10, other arithmetic, on_device_four(): back = jnp.where(is_source, own[step], back)  6.69 us
    ppermute x14, starting transfers between devices, on_device_four(): got.append(lax.ppermute(back, 'member', ring))  6.08 us
    ppermute x2, starting transfers between devices, on_device_four(): got = [lax.ppermute(chunk, 'member', ring) for chunk in own[:STAGGER]]  4.65 us
    ppermute x2, waiting for transfers between devices, on_device_four(): got = [lax.ppermute(chunk, 'member', ring) for chunk in own[:STAGGER]]  4.52 us
    ppermute x1, waiting for transfers between devices, on_device_four(): dn_near = lax.ppermute(dn_theirs, 'fsdp', over_x)  3.39 us
    pallas_call x1, Pallas kernels, backward(): pl.pallas_call(kernel, out_shape=(pltpu.VMEM((rows, cols), f32), pltpu.VM...  3.22 us
  transfers between devices with their start and end apart: 27, of which 17 were waited for; matrix products, arithmetic and copies ran while one was open for 10% of the time, Pallas kernels for 16%

profile of v6, /device:TPU:0, one launch (start us, length us, event | category | flops | bytes accessed | tf_op | source)
XLA Modules:
  0.0 95.7 jit_solution(16700233935907491239)
XLA Ops:
  0.7 1.3 %pack_weights.1 = (bf16[384,256]{1,0:T(8,128)(2,1)S(1)}, bf16[384,256]{1,0:T(8,128)(2,1)S(1)}, bf16[384,256]{1,0:T(8,128)(2,1)S(1)}, bf16[384,256]{1,0:T(8,128)(2,1)S(1)}) custom-call(bf16[1,1024,256]{2,1,0:T(8,128)(2,1)} %gu_ref.1, bf16[1,32,4096]{2,1,0:T(8,128)(2,1)} %down_ref.1), custom_call_target="tpu_custom_call" | custom-call | bytes 1572864 | tf_op jit(solution)/shard_map/pack_weights/pallas_call | solution.py:335
  2.0 3.1 %collective-permute-start = (bf16[384,256]{1,0:T(8,128)(2,1)S(1)}, bf16[384,256]{1,0:T(8,128)(2,1)S(1)}, u32[]{:S(2)}, u32[]{:S(2)}) collective-permute-start(bf16[384,256]{1,0:T(8,128)(2,1)S(1)} %get-tuple-element.63.refs_0_), channel_id=1, source_target_pairs={{0,4},{4,8},{8,12},{12,0},{1,5},{5,9},{9,13},{13,1},{2,6},{6,10},{... | collective-permute-start | bytes 589832 | tf_op jit(solution)/shard_map/ppermute | solution.py:774
  5.1 1.6 %collective-permute-start.1 = (bf16[384,256]{1,0:T(8,128)(2,1)S(1)}, bf16[384,256]{1,0:T(8,128)(2,1)S(1)}, u32[]{:S(2)}, u32[]{:S(2)}) collective-permute-start(bf16[384,256]{1,0:T(8,128)(2,1)S(1)} %get-tuple-element.60.refs_1_.refs_0_), channel_id=1, source_target_pairs={{0,4},{4,8},{8,12},{12,0},{1,5},{5,9},{9,13},{13,1},{2,6},{6,10},{... | collective-permute-start | bytes 589832 | tf_op jit(solution)/shard_map/ppermute | solution.py:774
  6.6 2.1 %dynamic-slice_bitcast_fusion.1 = bf16[192,2048]{1,0:T(8,128)(2,1)} fusion(bf16[1,192,4096]{2,1,0:T(8,128)(2,1)} %tok_r.3, s32[]{:T(128)S(6)} %select_n.76), kind=kLoop, calls=%fused_computation.1 | loop fusion | bytes 1572868 | tf_op jit(solution)/shard_map/dynamic_slice | solution.py:771
  8.7 1.5 %collective-permute-start.11 = (bf16[192,2048]{1,0:T(8,128)(2,1)}, bf16[192,2048]{1,0:T(8,128)(2,1)S(1)}, u32[]{:S(2)}, u32[]{:S(2)}) collective-permute-start(bf16[192,2048]{1,0:T(8,128)(2,1)} %dynamic-slice_bitcast_fusion.1), channel_id=1, source_target_pairs={{0,2},{2,0},{1,3},{3,1},{4,6},{6,4},{5,7},{7,5},{8,10},{10,8},{9,1... | collective-permute-start | bytes 2359304 | tf_op jit(solution)/shard_map/ppermute | solution.py:776
  10.2 0.6 and_reduce_fusion
  10.9 1.9 %collective-permute-done = bf16[384,256]{1,0:T(8,128)(2,1)S(1)} collective-permute-done((bf16[384,256]{1,0:T(8,128)(2,1)S(1)}, bf16[384,256]{1,0:T(8,128)(2,1)S(1)}, u32[]{:S(2)}, u32[]{:S(2)}) %collective-permute-start) | collective-permute-done | bytes 196640 | tf_op jit(solution)/shard_map/ppermute | solution.py:774
  12.8 0.7 broadcast_select_fusion.9.refs_2_.refs_3_
  13.5 0.1 collective-permute-start.2
  13.6 2.6 %collective-permute-done.1 = bf16[384,256]{1,0:T(8,128)(2,1)S(1)} collective-permute-done((bf16[384,256]{1,0:T(8,128)(2,1)S(1)}, bf16[384,256]{1,0:T(8,128)(2,1)S(1)}, u32[]{:S(2)}, u32[]{:S(2)}) %collective-permute-start.1) | collective-permute-done | bytes 196640 | tf_op jit(solution)/shard_map/ppermute | solution.py:774
  16.2 0.7 broadcast_select_fusion.8.refs_3_.refs_4_
  16.9 0.7 collective-permute-start.3
  17.6 2.2 %pack_moments.1 = (bf16[384,256]{1,0:T(8,128)(2,1)S(1)}, bf16[384,256]{1,0:T(8,128)(2,1)S(1)}, bf16[384,256]{1,0:T(8,128)(2,1)S(1)}, bf16[384,256]{1,0:T(8,128)(...) custom-call(f32[1,1024,256]{2,1,0:T(8,128)} %refs_0_.3, ...), custom_call_target="tpu_custom_call" | custom-call | bytes 4718592 | tf_op jit(solution)/shard_map/pack_moments/pallas_call | solution.py:294
  19.8 1.5 %collective-permute-done.2 = bf16[384,256]{1,0:T(8,128)(2,1)S(1)} collective-permute-done((bf16[384,256]{1,0:T(8,128)(2,1)S(1)}, bf16[384,256]{1,0:T(8,128)(2,1)S(1)}, u32[]{:S(2)}, u32[]{:S(2)}) %collective-permute-start.2) | collective-permute-done | bytes 196640 | tf_op jit(solution)/shard_map/ppermute | solution.py:808
  21.4 0.7 broadcast_select_fusion.7.refs_4_.refs_5_
  22.0 0.3 collective-permute-start.4
  22.3 4.3 %collective-permute-done.3 = bf16[384,256]{1,0:T(8,128)(2,1)S(1)} collective-permute-done((bf16[384,256]{1,0:T(8,128)(2,1)S(1)}, bf16[384,256]{1,0:T(8,128)(2,1)S(1)}, u32[]{:S(2)}, u32[]{:S(2)}) %collective-permute-start.3) | collective-permute-done | bytes 196640 | tf_op jit(solution)/shard_map/ppermute | solution.py:808
  26.6 0.7 broadcast_select_fusion.6.refs_5_.refs_6_
  27.2 0.1 collective-permute-start.5
  27.3 2.6 %collective-permute-done.4 = bf16[384,256]{1,0:T(8,128)(2,1)S(1)} collective-permute-done((bf16[384,256]{1,0:T(8,128)(2,1)S(1)}, bf16[384,256]{1,0:T(8,128)(2,1)S(1)}, u32[]{:S(2)}, u32[]{:S(2)}) %collective-permute-start.4) | collective-permute-done | bytes 196640 | tf_op jit(solution)/shard_map/ppermute | solution.py:808
  29.9 0.7 broadcast_select_fusion.5.refs_6_.refs_7_.refs_5_.refs_11_
  30.6 0.1 collective-permute-start.6
  30.7 5.8 %collective-permute-done.5 = bf16[384,256]{1,0:T(8,128)(2,1)S(1)} collective-permute-done((bf16[384,256]{1,0:T(8,128)(2,1)S(1)}, bf16[384,256]{1,0:T(8,128)(2,1)S(1)}, u32[]{:S(2)}, u32[]{:S(2)}) %collective-permute-start.5) | collective-permute-done | bytes 196640 | tf_op jit(solution)/shard_map/ppermute | solution.py:808
  36.5 0.7 broadcast_select_fusion.4.refs_7_.refs_8_.refs_6_.refs_12_
  37.2 0.9 assemble.2
  38.1 0.1 collective-permute-start.7
  38.2 0.1 collective-permute-start.10
  38.3 1.8 %collective-permute-start.8 = (bf16[8,32,256]{2,1,0:T(8,128)(2,1)S(1)}, bf16[8,32,256]{2,1,0:T(8,128)(2,1)S(1)}, u32[]{:S(2)}, u32[]{:S(2)}) collective-permute-start(bf16[8,32,256]{2,1,0:T(8,128)(2,1)S(1)} %get-tuple-element.115), channel_id=1, source_target_pairs={{0,2},{2,0},{1,3},{3,1},{4,6},{6,4},{5,7},{7,5},{8,10},{10,8},{9,1... | collective-permute-start | bytes 393224 | tf_op jit(solution)/shard_map/ppermute | solution.py:816
  40.1 0.1 collective-permute-start.9
  40.2 0.7 broadcast_select_fusion.3.refs_9_.refs_7_.refs_13_
  40.8 0.6 collective-permute-done.9.mate_r
  41.4 1.4 %collective-permute-start.18 = (bf16[192,2048]{1,0:T(8,128)(2,1)S(1)}, bf16[192,2048]{1,0:T(8,128)(2,1)S(1)}, u32[]{:S(2)}, u32[]{:S(2)}) collective-permute-start(bf16[192,2048]{1,0:T(8,128)(2,1)S(1)} %dynamic-slice_bitcast_fusion), channel_id=1, source_target_pairs={{0,2},{2,0},{1,3},{3,1},{4,6},{6,4},{5,7},{7,5},{8,10},{10,8},{9,1... | collective-permute-start | bytes 2359304 | tf_op jit(solution)/shard_map/ppermute | solution.py:778
  42.9 0.9 collective-permute-done.10.far_r
  43.8 3.4 %collective-permute-done.8.near_r = bf16[8,32,256]{2,1,0:T(8,128)(2,1)S(1)} collective-permute-done((bf16[8,32,256]{2,1,0:T(8,128)(2,1)S(1)}, bf16[8,32,256]{2,1,0:T(8,128)(2,1)S(1)}, u32[]{:S(2)}, u32[]{:S(2)}) %collective-permute-start.8) | collective-permute-done | bytes 131104 | tf_op jit(solution)/shard_map/ppermute | solution.py:816
  47.2 0.7 broadcast_select_fusion.2.refs_10_.refs_8_.refs_14_
  47.9 1.3 %assemble.3.gu_r.refs_2_ = bf16[1024,256]{1,0:T(8,128)(2,1)S(1)} custom-call(s32[4]{0:T(128)S(1)} %copy-done, bf16[384,256]{1,0:T(8,128)(2,1)S(1)} %get-tuple-element.60.refs_1_.refs_0_, bf16[384,256]{1,0:T(8,128)(2,1)S(1)} %get-tuple-element.61.refs_1_, bf16[384,256]{1,0:T(8,128)(2,1)S(1)} %get-tuple-element.62.refs_2_, ...), custom_call_target="tpu_custom_call" | custom-call | bytes 1048576 | tf_op jit(solution)/shard_map/assemble/pallas_call | solution.py:248
  49.1 0.1 collective-permute-start.13
  49.2 0.1 collective-permute-start.14
  49.3 3.8 %collective-permute-done.12 = bf16[384,256]{1,0:T(8,128)(2,1)S(1)} collective-permute-done((bf16[384,256]{1,0:T(8,128)(2,1)S(1)}, bf16[384,256]{1,0:T(8,128)(2,1)S(1)}, u32[]{:S(2)}, u32[]{:S(2)}) %collective-permute-start.12) | collective-permute-done | bytes 196640 | tf_op jit(solution)/shard_map/ppermute | solution.py:808
  53.1 0.7 broadcast_select_fusion.1.refs_9_.refs_15_
  53.8 0.1 collective-permute-start.16
  53.8 5.0 %collective-permute-done.14 = bf16[384,256]{1,0:T(8,128)(2,1)S(1)} collective-permute-done((bf16[384,256]{1,0:T(8,128)(2,1)S(1)}, bf16[384,256]{1,0:T(8,128)(2,1)S(1)}, u32[]{:S(2)}, u32[]{:S(2)}) %collective-permute-start.14) | collective-permute-done | bytes 196640 | tf_op jit(solution)/shard_map/ppermute | solution.py:808
  58.8 0.7 broadcast_select_fusion.refs_10_.refs_16_
  59.5 0.1 collective-permute-start.15
  59.6 1.8 %forward_gu.1 = (f32[384,256]{1,0:T(8,128)S(1)}, bf16[384,256]{1,0:T(8,128)(2,1)S(1)}) custom-call(bf16[1,192,4096]{2,1,0:T(8,128)(2,1)} %tok_r.3, bf16[192,2048]{1,0:T(8,128)(2,1)S(1)} %collective-permute-done.11.tokn_r, bf16[1024,256]{1,0:T(8,128)(2,1)S(1)} %assemble.3.gu_r.refs_2_, bf16[1024,256]{1,0:T(8,128)(2,1)S(1)} %collective-permute-done.13.gum_r), custom_call_target="tpu_custom_call" | custom-call | flops 402653184 | bytes 3145728 | tf_op jit(solution)/shard_map/forward_gu/pallas_call | solution.py:378
  61.5 1.3 %collective-permute-start.17 = (bf16[384,256]{1,0:T(8,128)(2,1)S(1)}, bf16[384,256]{1,0:T(8,128)(2,1)S(1)}, u32[]{:S(2)}, u32[]{:S(2)}) collective-permute-start(bf16[384,256]{1,0:T(8,128)(2,1)S(1)} %get-tuple-element.88), channel_id=1, source_target_pairs={{0,2},{2,0},{1,3},{3,1},{4,6},{6,4},{5,7},{7,5},{8,10},{10,8},{9,1... | collective-permute-start | bytes 589832 | tf_op jit(solution)/shard_map/ppermute | solution.py:826
  62.8 0.6 collective-permute-start.20
  63.4 0.3 collective-permute-done.18.upn_r
  63.7 1.8 %forward_dn.1 = (f32[384,128]{1,0:T(8,128)S(1)}, bf16[384,128]{1,0:T(8,128)(2,1)S(1)}) custom-call(bf16[1,192,4096]{2,1,0:T(8,128)(2,1)} %up_r.3, bf16[192,2048]{1,0:T(8,128)(2,1)S(1)} %collective-permute-done.18.upn_r, bf16[8,32,256]{2,1,0:T(8,128)(2,1)S(1)} %get-tuple-element.90.mine_r, bf16[8,32,256]{2,1,0:T(8,128)(2,1)S(1)} %collective-permute-done.8.near_r, ...), custom_call_target="tpu_custom_call" | custom-call | flops 201326592 | bytes 3145728 | tf_op jit(solution)/shard_map/forward_dn/pallas_call | solution.py:423
  65.5 0.4 collective-permute-start.19
  65.9 2.9 %collective-permute-done.15.refs_12_.refs_18_ = bf16[384,256]{1,0:T(8,128)(2,1)S(1)} collective-permute-done((bf16[384,256]{1,0:T(8,128)(2,1)S(1)}, bf16[384,256]{1,0:T(8,128)(2,1)S(1)}, u32[]{:S(2)}, u32[]{:S(2)}) %collective-permute-start.15) | collective-permute-done | bytes 196640 | tf_op jit(solution)/shard_map/ppermute | solution.py:808
  68.8 1.4 %collective-permute-done.19.dhn_r = bf16[384,128]{1,0:T(8,128)(2,1)S(1)} collective-permute-done((bf16[384,128]{1,0:T(8,128)(2,1)S(1)}, bf16[384,128]{1,0:T(8,128)(2,1)S(1)}, u32[]{:S(2)}, u32[]{:S(2)}) %collective-permute-start.19) | collective-permute-done | bytes 98336 | tf_op jit(solution)/shard_map/ppermute | solution.py:831
  70.2 3.2 %backward.1 = (f32[1024,256]{1,0:T(8,128)S(1)}, bf16[1024,256]{1,0:T(8,128)(2,1)S(1)}, f32[2,8,32,256]{3,2,1,0:T(8,128)S(1)}, bf16[2,8,32,256]{3,2,1,0:T(8,128)(2,1)S(1)}) custom-call(f32[384,256]{1,0:T(8,128)S(1)} %get-tuple-element.87.pre_r, bf16[384,256]{1,0:T(8,128)(2,1)S(1)} %collective-permute-done.17.pren_r, f32[384,128]{1,0:T(8,128)S(1)} %get-tuple-element.91.dh_r, ...), custom_call_target="tpu_custom_call" | custom-call | flops 603979776 | bytes 6291456 | tf_op jit(solution)/shard_map/backward/pallas_call | solution.py:497
  73.4 0.1 collective-permute-start.21
  73.5 0.5 collective-permute-start.22
  74.0 2.1 %collective-permute-start.23 = (bf16[384,256]{1,0:T(8,128)(2,1)S(1)}, bf16[384,256]{1,0:T(8,128)(2,1)S(1)}, u32[]{:S(2)}, u32[]{:S(2)}) collective-permute-start(bf16[384,256]{1,0:T(8,128)(2,1)S(1)} %collective-permute-done.15.refs_12_.refs_18_), channel_id=1, source_target_pairs={{0,4},{4,8},{8,12},{12,0},{1,5},{5,9},{9,13},{13,1},{2,6},{6,10},{... | collective-permute-start | bytes 589832 | tf_op jit(solution)/shard_map/ppermute | solution.py:808
  76.2 1.8 %collective-permute-start.25 = (bf16[384,256]{1,0:T(8,128)(2,1)S(1)}, bf16[384,256]{1,0:T(8,128)(2,1)S(1)}, u32[]{:S(2)}, u32[]{:S(2)}) collective-permute-start(bf16[384,256]{1,0:T(8,128)(2,1)S(1)} %collective-permute-done.20.refs_13_.refs_19_), channel_id=1, source_target_pairs={{0,4},{4,8},{8,12},{12,0},{1,5},{5,9},{9,13},{13,1},{2,6},{6,10},{... | collective-permute-start | bytes 589832 | tf_op jit(solution)/shard_map/ppermute | solution.py:808
  77.9 5.9 %collective-permute-done.23.refs_14_.refs_20_ = bf16[384,256]{1,0:T(8,128)(2,1)S(1)} collective-permute-done((bf16[384,256]{1,0:T(8,128)(2,1)S(1)}, bf16[384,256]{1,0:T(8,128)(2,1)S(1)}, u32[]{:S(2)}, u32[]{:S(2)}) %collective-permute-start.23) | collective-permute-done | bytes 196640 | tf_op jit(solution)/shard_map/ppermute | solution.py:808
  83.8 0.1 collective-permute-start.26
  83.9 0.7 collective-permute-start.24
  84.7 3.0 %collective-permute-done.25.refs_21_ = bf16[384,256]{1,0:T(8,128)(2,1)S(1)} collective-permute-done((bf16[384,256]{1,0:T(8,128)(2,1)S(1)}, bf16[384,256]{1,0:T(8,128)(2,1)S(1)}, u32[]{:S(2)}, u32[]{:S(2)}) %collective-permute-start.25) | collective-permute-done | bytes 196640 | tf_op jit(solution)/shard_map/ppermute | solution.py:808
  87.7 3.8 %update.2 = (bf16[1,1024,256]{2,1,0:T(8,128)(2,1)}, f32[1,1024,256]{2,1,0:T(8,128)}, f32[1,1024,256]{2,1,0:T(8,128)}) custom-call(s32[4]{0:T(128)S(1)} %copy-done, f32[4]{0:T(128)S(1)} %copy-done.1, f32[1,1024,256]{2,1,0:T(8,128)} %refs_0_.3, f32[1,1024,256]{2,1,0:T(8,128)} %refs_1_.3, bf16[1024,256]{1,0:T(8,128)(2,1)S(1)} %assemble.3.gu_r.refs_2_, ...), custom_call_target="tpu_custom_call" | custom-call | bytes 4325376 | tf_op jit(solution)/shard_map/update/pallas_call | solution.py:728
  91.5 0.2 collective-permute-done.26.refs_22_
  91.7 4.0 %update.3 = (bf16[1,1024,256]{2,1,0:T(8,128)(2,1)}, f32[1,1024,256]{2,1,0:T(8,128)}, f32[1,1024,256]{2,1,0:T(8,128)}, bf16[1,32,4096]{2,1,0:T(8,128)(2,1)}, f32[...) custom-call(s32[4]{0:T(128)S(1)} %copy-done, ...), custom_call_target="tpu_custom_call", output_to_operand_aliasing={{0}: (25, {}), {1}: (26, {}), {2}: (27, {})} | custom-call | bytes 1441792 | tf_op jit(solution)/shard_map/update/pallas_call | solution.py:728
  (20 shorter events, 0.2 us)
Async XLA Ops:
  0.6 10.2 %copy-start.2 = (bf16[1,192,4096]{2,1,0:T(8,128)(2,1)S(1)}, bf16[1,192,4096]{2,1,0:T(8,128)(2,1)}, u32[]{:S(2)}) copy-start(bf16[1,192,4096]{2,1,0:T(8,128)(2,1)} %up_r.3) | copy-start | bytes 4718596
  0.6 9.6 %copy-start = (s32[4]{0:T(128)S(1)}, s32[4]{0:T(128)}, u32[]{:S(2)}) copy-start(s32[4]{0:T(128)} %winner_ref.7) | copy-start | bytes 52
  2.0 10.8 %collective-permute-start = (bf16[384,256]{1,0:T(8,128)(2,1)S(1)}, bf16[384,256]{1,0:T(8,128)(2,1)S(1)}, u32[]{:S(2)}, u32[]{:S(2)}) collective-permute-start(bf16[384,256]{1,0:T(8,128)(2,1)S(1)} %get-tuple-element.63.refs_0_), channel_id=1, source_target_pairs={{0,4},{4,8},{8,12},{12,0},{1,5},{5,9},{9,13},{13,1},{2,6},{6,10},{... | collective-permute-start | bytes 589832 | tf_op jit(solution)/shard_map/ppermute | solution.py:774
  5.1 11.1 %collective-permute-start.1 = (bf16[384,256]{1,0:T(8,128)(2,1)S(1)}, bf16[384,256]{1,0:T(8,128)(2,1)S(1)}, u32[]{:S(2)}, u32[]{:S(2)}) collective-permute-start(bf16[384,256]{1,0:T(8,128)(2,1)S(1)} %get-tuple-element.60.refs_1_.refs_0_), channel_id=1, source_target_pairs={{0,4},{4,8},{8,12},{12,0},{1,5},{5,9},{9,13},{13,1},{2,6},{6,10},{... | collective-permute-start | bytes 589832 | tf_op jit(solution)/shard_map/ppermute | solution.py:774
  8.7 50.9 %collective-permute-start.11 = (bf16[192,2048]{1,0:T(8,128)(2,1)}, bf16[192,2048]{1,0:T(8,128)(2,1)S(1)}, u32[]{:S(2)}, u32[]{:S(2)}) collective-permute-start(bf16[192,2048]{1,0:T(8,128)(2,1)} %dynamic-slice_bitcast_fusion.1), channel_id=1, source_target_pairs={{0,2},{2,0},{1,3},{3,1},{4,6},{6,4},{5,7},{7,5},{8,10},{10,8},{9,1... | collective-permute-start | bytes 2359304 | tf_op jit(solution)/shard_map/ppermute | solution.py:776
  13.5 7.9 %collective-permute-start.2 = (bf16[384,256]{1,0:T(8,128)(2,1)S(1)}, bf16[384,256]{1,0:T(8,128)(2,1)S(1)}, u32[]{:S(2)}, u32[]{:S(2)}) collective-permute-start(bf16[384,256]{1,0:T(8,128)(2,1)S(1)} %broadcast_select_fusion.9.refs_2_.refs_3_), channel_id=1, source_target_pairs={{0,4},{4,8},{8,12},{12,0},{1,5},{5,9},{9,13},{13,1},{2,6},{6,10},{... | collective-permute-start | bytes 589832 | tf_op jit(solution)/shard_map/ppermute | solution.py:808
  16.9 9.7 %collective-permute-start.3 = (bf16[384,256]{1,0:T(8,128)(2,1)S(1)}, bf16[384,256]{1,0:T(8,128)(2,1)S(1)}, u32[]{:S(2)}, u32[]{:S(2)}) collective-permute-start(bf16[384,256]{1,0:T(8,128)(2,1)S(1)} %broadcast_select_fusion.8.refs_3_.refs_4_), channel_id=1, source_target_pairs={{0,4},{4,8},{8,12},{12,0},{1,5},{5,9},{9,13},{13,1},{2,6},{6,10},{... | collective-permute-start | bytes 589832 | tf_op jit(solution)/shard_map/ppermute | solution.py:808
  22.0 7.9 %collective-permute-start.4 = (bf16[384,256]{1,0:T(8,128)(2,1)S(1)}, bf16[384,256]{1,0:T(8,128)(2,1)S(1)}, u32[]{:S(2)}, u32[]{:S(2)}) collective-permute-start(bf16[384,256]{1,0:T(8,128)(2,1)S(1)} %broadcast_select_fusion.7.refs_4_.refs_5_), channel_id=1, source_target_pairs={{0,4},{4,8},{8,12},{12,0},{1,5},{5,9},{9,13},{13,1},{2,6},{6,10},{... | collective-permute-start | bytes 589832 | tf_op jit(solution)/shard_map/ppermute | solution.py:808
  27.2 9.2 %collective-permute-start.5 = (bf16[384,256]{1,0:T(8,128)(2,1)S(1)}, bf16[384,256]{1,0:T(8,128)(2,1)S(1)}, u32[]{:S(2)}, u32[]{:S(2)}) collective-permute-start(bf16[384,256]{1,0:T(8,128)(2,1)S(1)} %broadcast_select_fusion.6.refs_5_.refs_6_), channel_id=1, source_target_pairs={{0,4},{4,8},{8,12},{12,0},{1,5},{5,9},{9,13},{13,1},{2,6},{6,10},{... | collective-permute-start | bytes 589832 | tf_op jit(solution)/shard_map/ppermute | solution.py:808
  30.6 9.5 %collective-permute-start.6 = (bf16[384,256]{1,0:T(8,128)(2,1)S(1)}, bf16[384,256]{1,0:T(8,128)(2,1)S(1)}, u32[]{:S(2)}, u32[]{:S(2)}) collective-permute-start(bf16[384,256]{1,0:T(8,128)(2,1)S(1)} %broadcast_select_fusion.5.refs_6_.refs_7_.refs_5_.refs_11_), channel_id=1, source_target_pairs={{0,4},{4,8},{8,12},{12,0},{1,5},{5,9},{9,13},{13,1},{2,6},{6,10},{... | collective-permute-start | bytes 589832 | tf_op jit(solution)/shard_map/ppermute | solution.py:808
  38.1 9.1 %collective-permute-start.7 = (bf16[384,256]{1,0:T(8,128)(2,1)S(1)}, bf16[384,256]{1,0:T(8,128)(2,1)S(1)}, u32[]{:S(2)}, u32[]{:S(2)}) collective-permute-start(bf16[384,256]{1,0:T(8,128)(2,1)S(1)} %broadcast_select_fusion.4.refs_7_.refs_8_.refs_6_.refs_12_), channel_id=1, source_target_pairs={{0,4},{4,8},{8,12},{12,0},{1,5},{5,9},{9,13},{13,1},{2,6},{6,10},{... | collective-permute-start | bytes 589832 | tf_op jit(solution)/shard_map/ppermute | solution.py:808
  38.2 5.6 %collective-permute-start.10 = (bf16[8,32,256]{2,1,0:T(8,128)(2,1)S(1)}, bf16[8,32,256]{2,1,0:T(8,128)(2,1)S(1)}, u32[]{:S(2)}, u32[]{:S(2)}) collective-permute-start(bf16[8,32,256]{2,1,0:T(8,128)(2,1)S(1)} %get-tuple-element.115), channel_id=1, source_target_pairs={{0,3},{3,0},{1,2},{2,1},{4,7},{7,4},{5,6},{6,5},{8,11},{11,8},{9,1... | collective-permute-start | bytes 393224 | tf_op jit(solution)/shard_map/ppermute | solution.py:818
  38.3 8.9 %collective-permute-start.8 = (bf16[8,32,256]{2,1,0:T(8,128)(2,1)S(1)}, bf16[8,32,256]{2,1,0:T(8,128)(2,1)S(1)}, u32[]{:S(2)}, u32[]{:S(2)}) collective-permute-start(bf16[8,32,256]{2,1,0:T(8,128)(2,1)S(1)} %get-tuple-element.115), channel_id=1, source_target_pairs={{0,2},{2,0},{1,3},{3,1},{4,6},{6,4},{5,7},{7,5},{8,10},{10,8},{9,1... | collective-permute-start | bytes 393224 | tf_op jit(solution)/shard_map/ppermute | solution.py:816
  40.1 1.3 %collective-permute-start.9 = (bf16[8,32,256]{2,1,0:T(8,128)(2,1)S(1)}, bf16[8,32,256]{2,1,0:T(8,128)(2,1)S(1)}, u32[]{:S(2)}, u32[]{:S(2)}) collective-permute-start(bf16[8,32,256]{2,1,0:T(8,128)(2,1)S(1)} %get-tuple-element.90.mine_r), channel_id=1, source_target_pairs={{0,1},{1,0},{2,3},{3,2},{4,5},{5,4},{6,7},{7,6},{8,9},{9,8},{10,11... | collective-permute-start | bytes 393224 | tf_op jit(solution)/shard_map/ppermute | solution.py:817
  41.4 22.3 %collective-permute-start.18 = (bf16[192,2048]{1,0:T(8,128)(2,1)S(1)}, bf16[192,2048]{1,0:T(8,128)(2,1)S(1)}, u32[]{:S(2)}, u32[]{:S(2)}) collective-permute-start(bf16[192,2048]{1,0:T(8,128)(2,1)S(1)} %dynamic-slice_bitcast_fusion), channel_id=1, source_target_pairs={{0,2},{2,0},{1,3},{3,1},{4,6},{6,4},{5,7},{7,5},{8,10},{10,8},{9,1... | collective-permute-start | bytes 2359304 | tf_op jit(solution)/shard_map/ppermute | solution.py:778
  43.8 9.3 %collective-permute-start.12 = (bf16[384,256]{1,0:T(8,128)(2,1)S(1)}, bf16[384,256]{1,0:T(8,128)(2,1)S(1)}, u32[]{:S(2)}, u32[]{:S(2)}) collective-permute-start(bf16[384,256]{1,0:T(8,128)(2,1)S(1)} %broadcast_select_fusion.3.refs_9_.refs_7_.refs_13_), channel_id=1, source_target_pairs={{0,4},{4,8},{8,12},{12,0},{1,5},{5,9},{9,13},{13,1},{2,6},{6,10},{... | collective-permute-start | bytes 589832 | tf_op jit(solution)/shard_map/ppermute | solution.py:808
  49.1 10.5 %collective-permute-start.13 = (bf16[1024,256]{1,0:T(8,128)(2,1)S(1)}, bf16[1024,256]{1,0:T(8,128)(2,1)S(1)}, u32[]{:S(2)}, u32[]{:S(2)}) collective-permute-start(bf16[1024,256]{1,0:T(8,128)(2,1)S(1)} %assemble.3.gu_r.refs_2_), channel_id=1, source_target_pairs={{0,1},{1,0},{2,3},{3,2},{4,5},{5,4},{6,7},{7,6},{8,9},{9,8},{10,11... | collective-permute-start | bytes 1572872 | tf_op jit(solution)/shard_map/ppermute | solution.py:823
  49.2 9.6 %collective-permute-start.14 = (bf16[384,256]{1,0:T(8,128)(2,1)S(1)}, bf16[384,256]{1,0:T(8,128)(2,1)S(1)}, u32[]{:S(2)}, u32[]{:S(2)}) collective-permute-start(bf16[384,256]{1,0:T(8,128)(2,1)S(1)} %broadcast_select_fusion.2.refs_10_.refs_8_.refs_14_), channel_id=1, source_target_pairs={{0,4},{4,8},{8,12},{12,0},{1,5},{5,9},{9,13},{13,1},{2,6},{6,10},{... | collective-permute-start | bytes 589832 | tf_op jit(solution)/shard_map/ppermute | solution.py:808
  53.8 9.0 %collective-permute-start.16 = (bf16[384,256]{1,0:T(8,128)(2,1)S(1)}, bf16[384,256]{1,0:T(8,128)(2,1)S(1)}, u32[]{:S(2)}, u32[]{:S(2)}) collective-permute-start(bf16[384,256]{1,0:T(8,128)(2,1)S(1)} %broadcast_select_fusion.1.refs_9_.refs_15_), channel_id=1, source_target_pairs={{0,4},{4,8},{8,12},{12,0},{1,5},{5,9},{9,13},{13,1},{2,6},{6,10},{... | collective-permute-start | bytes 589832 | tf_op jit(solution)/shard_map/ppermute | solution.py:808
  59.5 9.3 %collective-permute-start.15 = (bf16[384,256]{1,0:T(8,128)(2,1)S(1)}, bf16[384,256]{1,0:T(8,128)(2,1)S(1)}, u32[]{:S(2)}, u32[]{:S(2)}) collective-permute-start(bf16[384,256]{1,0:T(8,128)(2,1)S(1)} %broadcast_select_fusion.refs_10_.refs_16_), channel_id=1, source_target_pairs={{0,4},{4,8},{8,12},{12,0},{1,5},{5,9},{9,13},{13,1},{2,6},{6,10},{... | collective-permute-start | bytes 589832 | tf_op jit(solution)/shard_map/ppermute | solution.py:808
  61.5 8.7 %collective-permute-start.17 = (bf16[384,256]{1,0:T(8,128)(2,1)S(1)}, bf16[384,256]{1,0:T(8,128)(2,1)S(1)}, u32[]{:S(2)}, u32[]{:S(2)}) collective-permute-start(bf16[384,256]{1,0:T(8,128)(2,1)S(1)} %get-tuple-element.88), channel_id=1, source_target_pairs={{0,2},{2,0},{1,3},{3,1},{4,6},{6,4},{5,7},{7,5},{8,10},{10,8},{9,1... | collective-permute-start | bytes 589832 | tf_op jit(solution)/shard_map/ppermute | solution.py:826
  62.8 10.6 %collective-permute-start.20 = (bf16[384,256]{1,0:T(8,128)(2,1)S(1)}, bf16[384,256]{1,0:T(8,128)(2,1)S(1)}, u32[]{:S(2)}, u32[]{:S(2)}) collective-permute-start(bf16[384,256]{1,0:T(8,128)(2,1)S(1)} %collective-permute-done.16.refs_11_.refs_17_), channel_id=1, source_target_pairs={{0,4},{4,8},{8,12},{12,0},{1,5},{5,9},{9,13},{13,1},{2,6},{6,10},{... | collective-permute-start | bytes 589832 | tf_op jit(solution)/shard_map/ppermute | solution.py:808
  65.5 4.7 %collective-permute-start.19 = (bf16[384,128]{1,0:T(8,128)(2,1)S(1)}, bf16[384,128]{1,0:T(8,128)(2,1)S(1)}, u32[]{:S(2)}, u32[]{:S(2)}) collective-permute-start(bf16[384,128]{1,0:T(8,128)(2,1)S(1)} %get-tuple-element.92), channel_id=1, source_target_pairs={{0,2},{2,0},{1,3},{3,1},{4,6},{6,4},{5,7},{7,5},{8,10},{10,8},{9,1... | collective-permute-start | bytes 294920 | tf_op jit(solution)/shard_map/ppermute | solution.py:831
  70.2 17.5 %copy-start.1 = (f32[4]{0:T(128)S(1)}, f32[4]{0:T(128)}, u32[]{:S(2)}) copy-start(f32[4]{0:T(128)} %rate_ref.3) | copy-start | bytes 52
  73.4 14.2 %collective-permute-start.21 = (bf16[1024,256]{1,0:T(8,128)(2,1)S(1)}, bf16[1024,256]{1,0:T(8,128)(2,1)S(1)}, u32[]{:S(2)}, u32[]{:S(2)}) collective-permute-start(bf16[1024,256]{1,0:T(8,128)(2,1)S(1)} %get-tuple-element.95), channel_id=1, source_target_pairs={{0,1},{1,0},{2,3},{3,2},{4,5},{5,4},{6,7},{7,6},{8,9},{9,8},{10,11... | collective-permute-start | bytes 1572872 | tf_op jit(solution)/shard_map/ppermute | solution.py:800
  73.5 10.4 %collective-permute-start.22 = (bf16[2,8,32,256]{3,2,1,0:T(8,128)(2,1)S(1)}, bf16[2,8,32,256]{3,2,1,0:T(8,128)(2,1)S(1)}, u32[]{:S(2)}, u32[]{:S(2)}) collective-permute-start(bf16[2,8,32,256]{3,2,1,0:T(8,128)(2,1)S(1)} %get-tuple-element.98), channel_id=1, source_target_pairs={{0,1},{1,0},{2,3},{3,2},{4,5},{5,4},{6,7},{7,6},{8,9},{9,8},{10,11... | collective-permute-start | bytes 786440 | tf_op jit(solution)/shard_map/ppermute | solution.py:799
  74.0 9.8 %collective-permute-start.23 = (bf16[384,256]{1,0:T(8,128)(2,1)S(1)}, bf16[384,256]{1,0:T(8,128)(2,1)S(1)}, u32[]{:S(2)}, u32[]{:S(2)}) collective-permute-start(bf16[384,256]{1,0:T(8,128)(2,1)S(1)} %collective-permute-done.15.refs_12_.refs_18_), channel_id=1, source_target_pairs={{0,4},{4,8},{8,12},{12,0},{1,5},{5,9},{9,13},{13,1},{2,6},{6,10},{... | collective-permute-start | bytes 589832 | tf_op jit(solution)/shard_map/ppermute | solution.py:808
  76.2 11.5 %collective-permute-start.25 = (bf16[384,256]{1,0:T(8,128)(2,1)S(1)}, bf16[384,256]{1,0:T(8,128)(2,1)S(1)}, u32[]{:S(2)}, u32[]{:S(2)}) collective-permute-start(bf16[384,256]{1,0:T(8,128)(2,1)S(1)} %collective-permute-done.20.refs_13_.refs_19_), channel_id=1, source_target_pairs={{0,4},{4,8},{8,12},{12,0},{1,5},{5,9},{9,13},{13,1},{2,6},{6,10},{... | collective-permute-start | bytes 589832 | tf_op jit(solution)/shard_map/ppermute | solution.py:808
  83.8 7.9 %collective-permute-start.26 = (bf16[384,256]{1,0:T(8,128)(2,1)S(1)}, bf16[384,256]{1,0:T(8,128)(2,1)S(1)}, u32[]{:S(2)}, u32[]{:S(2)}) collective-permute-start(bf16[384,256]{1,0:T(8,128)(2,1)S(1)} %collective-permute-done.23.refs_14_.refs_20_), channel_id=1, source_target_pairs={{0,4},{4,8},{8,12},{12,0},{1,5},{5,9},{9,13},{13,1},{2,6},{6,10},{... | collective-permute-start | bytes 589832 | tf_op jit(solution)/shard_map/ppermute | solution.py:808
  83.9 7.7 %collective-permute-start.24 = (bf16[8,32,256]{2,1,0:T(8,128)(2,1)S(1)}, bf16[8,32,256]{2,1,0:T(8,128)(2,1)S(1)}, u32[]{:S(2)}, u32[]{:S(2)}) collective-permute-start(bf16[8,32,256]{2,1,0:T(8,128)(2,1)S(1)} %fusion), channel_id=1, source_target_pairs={{0,2},{2,0},{1,3},{3,1},{4,6},{6,4},{5,7},{7,5},{8,10},{10,8},{9,1... | collective-permute-start | bytes 393224 | tf_op jit(solution)/shard_map/ppermute | solution.py:841
